TPU v7x, 32 devices: a whole 2x2x4 slice. The times are simulated.
32 devices in a mesh: rep: 8 (over z, y), fsdp: 4 (over x, core).
Axes of the slice: x: 2, y: 2, z: 4, core: 2. Of those that a mesh axis runs over, the one named last changes fastest.
Arguments:
- context: bfloat16 [8, 512, 2560], P('rep', 'fsdp'), may hold values from -6 to 6
- residual: bfloat16 [8, 5120, 512], P('rep', 'fsdp'), may hold values from -6 to 6
- target: bfloat16 [8, 5120, 512], P('rep', 'fsdp'), may hold values from -6 to 6
- norm_gain: float32 [5120], P('fsdp'), may hold values from 0.5 to 1.5
- params: float32 [8, 5120, 2560], P('rep', 'fsdp'), may hold values from -0.3125 to 0.3125
- momentum: bfloat16 [8, 5120, 2560], P('rep', 'fsdp'), may hold values from -0.3125 to 0.3125
- push_weight: float32 [8], P('rep'), may hold values from 0.5 to 2
- mix_num: int32 [8, 3], replicated, may hold values from 1 to 4
Outputs:
- new_params: float32 [8, 5120, 2560], P('rep', 'fsdp')
- new_momentum: bfloat16 [8, 5120, 2560], P('rep', 'fsdp')
- new_push: float32 [8], P('rep')
All inputs are finite; a program needn't handle non-finite values.
Results may differ from a plain program's by a relative error of at most 0.0061.
Values may be sent and summed in bfloat16 or wider, within the bound.
No kernel may reach another device: no remote copies, remote signals or barrier semaphores. Data moves between devices by JAX's collectives and lax.ppermute only.
A program may use at most 192 MiB of HBM per device.

v0:
```python
import jax
import jax.numpy as jnp
from jax import lax
from jax.sharding import PartitionSpec as P

D = 5120
STEPS = 2


epsilon = 1e-05
learn_rate = 0.5
beta_decay = 0.9


def passed_along(value, axis, steps):
    count = lax.axis_size(axis)
    pairs = [(source, (source + steps) % count) for source in range(count)]
    return lax.ppermute(value, axis, pairs)


def send_state(master, push_one):
    from_lower = (
        passed_along(master.astype(jnp.bfloat16), "rep", 1).astype(master.dtype),
        passed_along(push_one.astype(jnp.bfloat16), "rep", 1).astype(push_one.dtype),
    )
    from_upper = (
        passed_along(master.astype(jnp.bfloat16), "rep", -1).astype(master.dtype),
        passed_along(push_one.astype(jnp.bfloat16), "rep", -1).astype(push_one.dtype),
    )
    return (from_lower, from_upper)


def send_moment(moment):
    from_lower = passed_along(moment, "rep", 1)
    from_upper = passed_along(moment, "rep", -1)
    return (from_lower, from_upper)


def local(context, residual, target, norm_gain, params, momentum, push_weight, mix_num):
    gathered = lax.all_gather(context[0], "fsdp", axis=0, tiled=True)
    token_count = gathered.shape[0]
    stream = residual[0].astype(jnp.float32)
    target_f = target[0].astype(jnp.float32)
    gain_col = norm_gain[:, None]
    master = params[0]
    moment = momentum[0]
    for inner in range(STEPS):
        cast_w = (master / push_weight[0]).astype(jnp.bfloat16)
        product = lax.dot_general(
            cast_w, gathered, (((1,), (1,)), ((), ())), preferred_element_type=jnp.float32
        )
        summed = stream + product
        mean_sq = lax.psum(jnp.sum(summed * summed, axis=0), "fsdp") / D
        inv_rms = lax.rsqrt(mean_sq + epsilon)
        normed = gain_col * summed * inv_rms
        out_grad = (normed - target_f) / token_count
        scaled_grad = gain_col * out_grad
        feat_dot = lax.psum(jnp.sum(scaled_grad * summed, axis=0), "fsdp") / D
        stream_grad = (scaled_grad * inv_rms - summed * inv_rms**3 * feat_dot).astype(jnp.bfloat16)
        weight_grad = jnp.dot(stream_grad, gathered, preferred_element_type=jnp.float32)
        moment = (beta_decay * moment.astype(jnp.float32) + weight_grad).astype(jnp.bfloat16)
        master = master - learn_rate * moment.astype(jnp.float32)
    replica = lax.axis_index("rep")
    replicas = lax.axis_size("rep")
    counts = mix_num.astype(jnp.float32)
    shares = counts / jnp.sum(counts, axis=1, keepdims=True)
    keep_share = shares[replica, 0]
    lower_share = shares[(replica - 1) % replicas, 2]
    upper_share = shares[(replica + 1) % replicas, 1]
    moment_lower, moment_upper = send_moment(moment)
    mixed_moment = (
        keep_share * moment.astype(jnp.float32)
        + lower_share * moment_lower.astype(jnp.float32)
        + upper_share * moment_upper.astype(jnp.float32)
    )
    state_lower, state_upper = send_state(master, push_weight)
    new_master = keep_share * master + lower_share * state_lower[0] + upper_share * state_upper[0]
    new_push = (
        keep_share * push_weight + lower_share * state_lower[1] + upper_share * state_upper[1]
    )
    return (new_master[None], mixed_moment.astype(jnp.bfloat16)[None], new_push)


def solution(mesh):
    return jax.shard_map(
        local,
        mesh=mesh,
        in_specs=(
            P("rep", "fsdp", None),
            P("rep", "fsdp", None),
            P("rep", "fsdp", None),
            P("fsdp"),
            P("rep", "fsdp", None),
            P("rep", "fsdp", None),
            P("rep"),
            P(),
        ),
        out_specs=(P("rep", "fsdp", None), P("rep", "fsdp", None), P("rep")),
        check_vma=False,
    )
```

profile of v0, /device:TPU:0, one launch (start us, length us, event | category | flops | bytes accessed | tf_op | source)
XLA Modules:
  0.0 731.0 jit_solution(331730946100659326)
XLA Ops:
  7.2 0.0 all-gather.3.cloned.1.call-start
  7.2 0.7 all-gather.3.cloned.1.call-update
  8.5 0.7 broadcast_multiply_fusion
  9.2 28.6 %all-gather.3.cloned.1.call-done = bf16[1,512,2560]{2,1,0:T(8,128)(2,1)} async-done(((bf16[1,128,2560]{2,1,0:T(8,128)(2,1)}), bf16[1,512,2560]{2,1,0:T(8,128)(2,1)}) %all-gather.3.cloned.1.call-update) | async-done | bytes 2621456 | tf_op jit(solution)/shard_map/all_gather | solution.py:40
  37.8 11.1 %multiply_reduce_fusion.3 = (f32[512]{0:T(512)S(1)}, f32[1280,512]{1,0:T(8,128)}) fusion(bf16[1,512,2560]{2,1,0:T(8,128)(2,1)} %all-gather.3.cloned.1.call-done, f32[1,1280,2560]{2,1,0:T(8,128)} %param.12, f32[]{:T(128)} %bitcast.65, bf16[1,1280,512]{2,1,0:T(8,128)(2,1)} %param.9), kind=kOutput, calls=%fused_computation.36 | convolution fusion | flops 3364617728 | bytes 19662852 | tf_op jit(solution)/shard_map/dot_general | solution.py:49
  49.0 5.9 psum.28
  54.9 0.0 slice-start
  54.9 2.5 multiply_reduce_fusion.2
  57.3 5.7 psum.29
  63.0 11.4 %fusion.6 = bf16[1280,2560]{1,0:T(8,128)(2,1)} fusion(bf16[1,1280,2560]{2,1,0:T(8,128)(2,1)} %param.13, bf16[1,512,2560]{2,1,0:T(8,128)(2,1)} %all-gather.3.cloned.1.call-done, f32[1280,512]{1,0:T(8,128)} %get-tuple-element.13, bf16[1,1280,512]{2,1,0:T(8,128)(2,1)S(1)} %copy-done, f32[512]{0:T(512)S(1)} %broadcast_multiply_fusion.2, ...), kind=kOutput, calls=%fused_computation.15 | convolution fusion | flops 3375104000 | bytes 19677184 | tf_op jit(solution)/shard_map/dot_general | solution.py:60
  74.5 8.4 %multiply_reduce_fusion.1 = (f32[512]{0:T(512)S(1)}, f32[1280,512]{1,0:T(8,128)}) fusion(bf16[1,512,2560]{2,1,0:T(8,128)(2,1)S(1)} %copy-done.3, f32[]{:T(128)} %bitcast.66, bf16[1280,2560]{1,0:T(8,128)(2,1)} %fusion.6, f32[1,1280,2560]{2,1,0:T(8,128)S(1)} %bitcast.68, bf16[1,1280,512]{2,1,0:T(8,128)(2,1)} %param.9), kind=kOutput, calls=%fused_computation.33 | convolution fusion | flops 3374448128 | bytes 26216452 | tf_op jit(solution)/shard_map/dot_general | solution.py:49
  82.9 6.9 psum.30
  89.8 2.4 multiply_reduce_fusion
  92.3 5.8 psum.31
  98.1 11.7 %fusion.7 = bf16[1280,2560]{1,0:T(8,128)(2,1)} fusion(bf16[1280,2560]{1,0:T(8,128)(2,1)} %fusion.6, bf16[1,512,2560]{2,1,0:T(8,128)(2,1)} %all-gather.3.cloned.1.call-done, f32[1280,512]{1,0:T(8,128)} %get-tuple-element.15, bf16[1,1280,512]{2,1,0:T(8,128)(2,1)} %param.10, f32[512]{0:T(512)S(1)} %broadcast_multiply_fusion.1, f32[512]{0:T(512)S(1)} %get-tuple-element.8, ...), kind=kOutput, calls=%fused_computation.16 | convolution fusion | flops 3375104000 | bytes 19677184 | tf_op jit(solution)/shard_map/dot_general | solution.py:60
  109.7 4.4 collective-permute-start.3
  114.2 0.7 constant_dynamic-slice_fusion.2
  114.8 278.5 %collective-permute-done.3 = bf16[1280,2560]{1,0:T(8,128)(2,1)} collective-permute-done((bf16[1280,2560]{1,0:T(8,128)(2,1)}, bf16[1280,2560]{1,0:T(8,128)(2,1)}, u32[]{:S(2)}, u32[]{:S(2)}) %collective-permute-start.3) | collective-permute-done | bytes 6553632 | tf_op jit(solution)/shard_map/ppermute | solution.py:18
  393.3 24.0 %fusion.9 = (bf16[1,1280,2560]{2,1,0:T(8,128)(2,1)}, bf16[1280,2560]{1,0:T(8,128)(2,1)}) fusion(bf16[1280,2560]{1,0:T(8,128)(2,1)} %collective-permute-done.3, bf16[1280,2560]{1,0:T(8,128)(2,1)} %collective-permute-done.2, bf16[1280,2560]{1,0:T(8,128)(2,1)} %fusion.7, f32[]{:T(128)} %bitcast.10, f32[]{:T(128)} %bitcast.9, f32[]{:T(128)} %bitcast, ...), kind=kLoop, calls=%fused_computation.18 | loop fusion | flops 49152000 | bytes 52428812 | tf_op jit(solution)/shard_map/broadcast_in_dim | solution.py:81
  417.3 4.5 collective-permute-start.1
  421.8 139.3 %collective-permute-start.5 = (bf16[1]{0:T(256)(128)(2,1)}, bf16[1]{0:T(256)(128)(2,1)}, u32[]{:S(2)}, u32[]{:S(2)}) collective-permute-start(bf16[1]{0:T(256)(128)(2,1)} %convert_element_type.94), channel_id=1, source_target_pairs={{0,28},{4,0},{8,4},{12,8},{16,12},{20,16},{24,20},{28,24},{1,29},{... | collective-permute-start | bytes 14 | tf_op jit(solution)/shard_map/ppermute | solution.py:18
  561.0 141.5 %collective-permute-start.4 = (bf16[1]{0:T(256)(128)(2,1)}, bf16[1]{0:T(256)(128)(2,1)}, u32[]{:S(2)}, u32[]{:S(2)}) collective-permute-start(bf16[1]{0:T(256)(128)(2,1)} %convert_element_type.94), channel_id=1, source_target_pairs={{0,4},{4,8},{8,12},{12,16},{16,20},{20,24},{24,28},{28,0},{1,5},{5... | collective-permute-start | bytes 14 | tf_op jit(solution)/shard_map/ppermute | solution.py:18
  703.2 0.5 collective-permute-done.4
  706.4 16.5 %add_bitcast_fusion = f32[1,1280,2560]{2,1,0:T(8,128)} fusion(bf16[1280,2560]{1,0:T(8,128)(2,1)} %collective-permute-done.1, bf16[1280,2560]{1,0:T(8,128)(2,1)} %collective-permute-done, bf16[1280,2560]{1,0:T(8,128)(2,1)} %fusion.7, f32[]{:T(128)} %bitcast.10, f32[]{:T(128)} %bitcast.9, f32[]{:T(128)} %bitcast, bf16[1280,2560]{1,0:T(8,128)(2,1)S(1)} %bitcast.72, ...), kind=kLoop, calls=%fused_computation.13 | loop fusion | flops 42598400 | bytes 52428812 | tf_op jit(solution)/shard_map/broadcast_in_dim | solution.py:81
  (42 shorter events, 0.1 us)
Async XLA Ops:
  7.2 30.7 %all-gather.3.cloned.1.call-start = ((), (), s32[]{:S(2)}) async-start(), calls=%async_computation | async-start | bytes 3276800 | tf_op jit(solution)/shard_map/all_gather | solution.py:40
  37.8 17.0 %copy-start = (bf16[1,1280,512]{2,1,0:T(8,128)(2,1)S(1)}, bf16[1,1280,512]{2,1,0:T(8,128)(2,1)}, u32[]{:S(2)}) copy-start(bf16[1,1280,512]{2,1,0:T(8,128)(2,1)} %param.10) | copy-start | bytes 3932164
  37.8 17.0 %copy-start.1 = (f32[1280]{0:T(1024)S(1)}, f32[1280]{0:T(1024)}, u32[]{:S(2)}) copy-start(f32[1280]{0:T(1024)} %param.11) | copy-start | bytes 15364
  54.9 19.6 %slice-start = ((s8[13107200]{0:T(1024)(128)(4,1)}), s8[524288]{0:T(1024)(128)(4,1)S(1)}, s32[]{:S(2)}) async-start(s8[13107200]{0:T(1024)(128)(4,1)} %bitcast.67), calls=%async_computation.1 | async-start | bytes 1048576
  63.0 11.4 %slice-start.1 = ((s8[13107200]{0:T(1024)(128)(4,1)}), s8[4194304]{0:T(1024)(128)(4,1)S(1)}, s32[]{:S(2)}) async-start(s8[13107200]{0:T(1024)(128)(4,1)} %bitcast.67), calls=%async_computation.2 | async-start | bytes 8388608
  63.0 11.4 %slice-start.2 = ((s8[13107200]{0:T(1024)(128)(4,1)}), s8[4194304]{0:T(1024)(128)(4,1)S(1)}, s32[]{:S(2)}) async-start(s8[13107200]{0:T(1024)(128)(4,1)} %bitcast.67), calls=%async_computation.3 | async-start | bytes 8388608
  63.0 11.4 %slice-start.3 = ((s8[13107200]{0:T(1024)(128)(4,1)}), s8[4194304]{0:T(1024)(128)(4,1)S(1)}, s32[]{:S(2)}) async-start(s8[13107200]{0:T(1024)(128)(4,1)} %bitcast.67), calls=%async_computation.4 | async-start | bytes 8388608
  63.0 11.4 %copy-start.3 = (bf16[1,512,2560]{2,1,0:T(8,128)(2,1)S(1)}, bf16[1,512,2560]{2,1,0:T(8,128)(2,1)}, u32[]{:S(2)}) copy-start(bf16[1,512,2560]{2,1,0:T(8,128)(2,1)} %all-gather.3.cloned.1.call-done) | copy-start | bytes 7864324
  98.0 16.1 %copy-start.2 = (s32[8,3]{0,1:T(4,128)S(1)}, s32[8,3]{0,1:T(4,128)}, u32[]{:S(2)}) copy-start(s32[8,3]{0,1:T(4,128)} %param.15) | copy-start | bytes 292
  98.1 608.3 %slice-start.8 = ((s8[6553600]{0:T(1024)(128)(4,1)}), s8[2359296]{0:T(1024)(128)(4,1)S(1)}, s32[]{:S(2)}) async-start(s8[6553600]{0:T(1024)(128)(4,1)} %bitcast.71), calls=%async_computation.9 | async-start | bytes 4718592
  109.7 283.5 %collective-permute-start.3 = (bf16[1280,2560]{1,0:T(8,128)(2,1)}, bf16[1280,2560]{1,0:T(8,128)(2,1)}, u32[]{:S(2)}, u32[]{:S(2)}) collective-permute-start(bf16[1280,2560]{1,0:T(8,128)(2,1)} %fusion.7), channel_id=1, source_target_pairs={{0,28},{4,0},{8,4},{12,8},{16,12},{20,16},{24,20},{28,24},{1,29},{... | collective-permute-start | bytes 19660808 | tf_op jit(solution)/shard_map/ppermute | solution.py:18
  114.1 279.2 %collective-permute-start.2 = (bf16[1280,2560]{1,0:T(8,128)(2,1)}, bf16[1280,2560]{1,0:T(8,128)(2,1)}, u32[]{:S(2)}, u32[]{:S(2)}) collective-permute-start(bf16[1280,2560]{1,0:T(8,128)(2,1)} %fusion.7), channel_id=1, source_target_pairs={{0,4},{4,8},{8,12},{12,16},{16,20},{20,24},{24,28},{28,0},{1,5},{5... | collective-permute-start | bytes 19660808 | tf_op jit(solution)/shard_map/ppermute | solution.py:18
  393.3 313.1 %slice-start.4 = ((s8[13107200]{0:T(1024)(128)(4,1)}), s8[4194304]{0:T(1024)(128)(4,1)S(1)}, s32[]{:S(2)}) async-start(s8[13107200]{0:T(1024)(128)(4,1)} %bitcast.69), calls=%async_computation.5 | async-start | bytes 8388608
  393.3 313.1 %slice-start.5 = ((s8[13107200]{0:T(1024)(128)(4,1)}), s8[4194304]{0:T(1024)(128)(4,1)S(1)}, s32[]{:S(2)}) async-start(s8[13107200]{0:T(1024)(128)(4,1)} %bitcast.69), calls=%async_computation.6 | async-start | bytes 8388608
  393.3 313.1 %slice-start.6 = ((s8[13107200]{0:T(1024)(128)(4,1)}), s8[4194304]{0:T(1024)(128)(4,1)S(1)}, s32[]{:S(2)}) async-start(s8[13107200]{0:T(1024)(128)(4,1)} %bitcast.69), calls=%async_computation.7 | async-start | bytes 8388608
  393.3 313.1 %slice-start.7 = ((s8[13107200]{0:T(1024)(128)(4,1)}), s8[524288]{0:T(1024)(128)(4,1)S(1)}, s32[]{:S(2)}) async-start(s8[13107200]{0:T(1024)(128)(4,1)} %bitcast.69), calls=%async_computation.8 | async-start | bytes 1048576
  393.3 313.1 %slice-start.9 = ((s8[6553600]{0:T(1024)(128)(4,1)}), s8[4194304]{0:T(1024)(128)(4,1)S(1)}, s32[]{:S(2)}) async-start(s8[6553600]{0:T(1024)(128)(4,1)} %bitcast.71), calls=%async_computation.10 | async-start | bytes 8388608
  417.3 289.1 %collective-permute-start.1 = (bf16[1280,2560]{1,0:T(8,128)(2,1)}, bf16[1280,2560]{1,0:T(8,128)(2,1)}, u32[]{:S(2)}, u32[]{:S(2)}) collective-permute-start(bf16[1280,2560]{1,0:T(8,128)(2,1)} %get-tuple-element.4), channel_id=1, source_target_pairs={{0,28},{4,0},{8,4},{12,8},{16,12},{20,16},{24,20},{28,24},{1,29},{... | collective-permute-start | bytes 19660808 | tf_op jit(solution)/shard_map/ppermute | solution.py:18
  421.8 284.6 %collective-permute-start = (bf16[1280,2560]{1,0:T(8,128)(2,1)}, bf16[1280,2560]{1,0:T(8,128)(2,1)}, u32[]{:S(2)}, u32[]{:S(2)}) collective-permute-start(bf16[1280,2560]{1,0:T(8,128)(2,1)} %get-tuple-element.4), channel_id=1, source_target_pairs={{0,4},{4,8},{8,12},{12,16},{16,20},{20,24},{24,28},{28,0},{1,5},{5... | collective-permute-start | bytes 19660808 | tf_op jit(solution)/shard_map/ppermute | solution.py:18
  421.8 283.2 %collective-permute-start.5 = (bf16[1]{0:T(256)(128)(2,1)}, bf16[1]{0:T(256)(128)(2,1)}, u32[]{:S(2)}, u32[]{:S(2)}) collective-permute-start(bf16[1]{0:T(256)(128)(2,1)} %convert_element_type.94), channel_id=1, source_target_pairs={{0,28},{4,0},{8,4},{12,8},{16,12},{20,16},{24,20},{28,24},{1,29},{... | collective-permute-start | bytes 14 | tf_op jit(solution)/shard_map/ppermute | solution.py:18
  561.0 142.7 %collective-permute-start.4 = (bf16[1]{0:T(256)(128)(2,1)}, bf16[1]{0:T(256)(128)(2,1)}, u32[]{:S(2)}, u32[]{:S(2)}) collective-permute-start(bf16[1]{0:T(256)(128)(2,1)} %convert_element_type.94), channel_id=1, source_target_pairs={{0,4},{4,8},{8,12},{12,16},{16,20},{20,24},{24,28},{28,0},{1,5},{5... | collective-permute-start | bytes 14 | tf_op jit(solution)/shard_map/ppermute | solution.py:18
Sparse Core Ops, SparseCore 0:
  9.6 28.2 all-gather.2
where the time goes:
time: 731 us
  waiting for transfers between devices  308 us (42%)
  starting transfers between devices  290 us (40%)
  other arithmetic  46.2 us (6%)
  matrix products  42.7 us (6%)
  blocking collectives  24.2 us (3%)
  between operations  19.2 us (3%)
    ppermute x6, starting transfers between devices, passed_along(): return lax.ppermute(value, axis, pairs)  290 us
    ppermute x6, waiting for transfers between devices, passed_along(): return lax.ppermute(value, axis, pairs)  279 us
    broadcast_in_dim x2, other arithmetic, local(): return (new_master[None], mixed_moment.astype(jnp.bfloat16)[None], new_push)  40.5 us
    all_gather x1, waiting for transfers between devices, local(): gathered = lax.all_gather(context[0], 'fsdp', axis=0, tiled=True)  28.6 us
    dot_general x2, matrix products, local(): jnp.dot(stream_grad, gathered, preferred_element_type=jnp.float32)  23.1 us
    dot_general x2, matrix products, local(): lax.dot_general(cast_w, gathered, (((1,), (1,)), ((), ())), preferred_ele...  19.6 us
  transfers between devices with their start and end apart: 7, of which 3 were waited for; matrix products, arithmetic and copies ran while one was open for 0% of the time, Pallas kernels for 0%

commit v1 on v0

v1 whole, which is shorter than its diff:
```python
import functools

import jax
import jax.numpy as jnp
from jax import lax
from jax.experimental import pallas as pl
from jax.experimental.pallas import tpu as pltpu
from jax.sharding import PartitionSpec as P

epsilon = 1e-05
learn_rate = 0.5
beta_decay = 0.9

UNIT = 32
VMEM_LIMIT = 56 * 1024 * 1024
F32 = jnp.float32
BF16 = jnp.bfloat16
NT = (((1,), (1,)), ((), ()))

SMEM_SPEC = pl.BlockSpec(memory_space=pltpu.SMEM)


def whole_spec(shape):
    return pl.BlockSpec(shape, lambda i: (0,) * len(shape))


def params_of(limit=VMEM_LIMIT):
    return pltpu.CompilerParams(
        dimension_semantics=("arbitrary",), vmem_limit_bytes=limit
    )


def cost(flops, nbytes):
    return pl.CostEstimate(flops=flops, bytes_accessed=nbytes, transcendentals=0)


def local_tokens(ref, index, count):
    width = ref.shape[1] // count
    blocks = [
        ref[:, pl.ds(pl.multiple_of(lax.bitwise_xor(index, j) * width, width), width)]
        for j in range(count)
    ]
    return jnp.concatenate(blocks, axis=1)


def add_sums(sums_ref, step, total, scaled, target):
    parts = jnp.concatenate(
        [
            jnp.sum(total * total, axis=0, keepdims=True),
            jnp.sum(scaled * scaled, axis=0, keepdims=True),
            jnp.sum(scaled * target, axis=0, keepdims=True),
            jnp.zeros((5, total.shape[1]), F32),
        ],
        axis=0,
    )

    @pl.when(step == 0)
    def _():
        sums_ref[...] = parts

    @pl.when(step > 0)
    def _():
        sums_ref[...] += parts


def token_stats(sum_refs, features):
    count = len(sum_refs)
    tokens = sum_refs[0].shape[1]
    width = tokens // count
    full = sum_refs[0][...]
    for m in range(1, count):
        other = sum_refs[m]
        full = full + jnp.concatenate(
            [other[:, (j ^ m) * width : ((j ^ m) + 1) * width] for j in range(count)],
            axis=1,
        )
    inv = lax.rsqrt(full[0:1] / features + epsilon)
    dot = (inv * full[1:2] - full[2:3]) / (tokens * features)
    return inv, dot


def stream_grad(total, target, gain, inv, dot, tokens):
    scaled = gain * ((gain * total * inv - target) / tokens)
    return (scaled * inv - total * (inv * inv * inv * dot)).astype(BF16)


def forward_kernel(
    count, idx_ref, coef_ref, p_ref, m_ref, c_ref, r_ref, t_ref, g_ref, s_ref, y_ref, q_ref
):
    index = idx_ref[0]
    weights = (p_ref[...] * coef_ref[0]).astype(BF16)
    context = c_ref[...]
    product = lax.dot_general(weights, context, NT, preferred_element_type=F32)
    y_ref[...] = lax.dot_general(m_ref[...], context, NT, preferred_element_type=F32)
    total = local_tokens(r_ref, index, count).astype(F32) + product
    s_ref[...] = total
    target = local_tokens(t_ref, index, count).astype(F32)
    add_sums(q_ref, pl.program_id(0), total, g_ref[...] * total, target)


def forward(index, coef, params, moment, context, residual, target, gain, count):
    rows, width = params.shape
    tokens = context.shape[0]
    block = min(128, rows)
    row = lambda n: pl.BlockSpec((block, n), lambda i: (i, 0))
    return pl.pallas_call(
        functools.partial(forward_kernel, count),
        grid=(rows // block,),
        in_specs=[
            SMEM_SPEC,
            SMEM_SPEC,
            row(width),
            row(width),
            whole_spec((tokens, width)),
            row(tokens),
            row(tokens),
            row(1),
        ],
        out_specs=[row(tokens), row(tokens), whole_spec((8, tokens))],
        out_shape=[
            jax.ShapeDtypeStruct((rows, tokens), F32),
            jax.ShapeDtypeStruct((rows, tokens), F32),
            jax.ShapeDtypeStruct((8, tokens), F32),
        ],
        compiler_params=params_of(),
        cost_estimate=cost(4 * rows * width * tokens, rows * width * 6),
    )(index, coef, params, moment, context, residual, target, gain)


def second_kernel(count, features, idx_ref, coef_ref, s_ref, t_ref, g_ref, y_ref, gram_ref, *rest):
    sum_refs, (grad_ref, s2_ref, q_ref, high_ref, low_ref) = rest[:count], rest[count:]
    index = idx_ref[0]
    step = pl.program_id(0)

    @pl.when(step == 0)
    def _():
        gram = gram_ref[...]
        high = gram.astype(BF16)
        high_ref[...] = high
        low_ref[...] = (gram - high.astype(F32)).astype(BF16)

    inv, dot = token_stats(sum_refs, features)
    total = s_ref[...]
    target = local_tokens(t_ref, index, count).astype(F32)
    gain = g_ref[...]
    grad = stream_grad(total, target, gain, inv, dot, total.shape[1])
    grad_ref[...] = grad
    moved = jnp.dot(grad, high_ref[...], preferred_element_type=F32)
    moved += jnp.dot(grad, low_ref[...], preferred_element_type=F32)
    total = total - coef_ref[1] * (beta_decay * y_ref[...] + moved)
    s2_ref[...] = total
    add_sums(q_ref, step, total, gain * total, target)


def second(index, coef, total, target, gain, moment_product, gram, sums, features):
    rows, tokens = total.shape
    count = len(sums)
    block = min(256, rows) if rows % 256 == 0 else min(64, rows)
    row = lambda n: pl.BlockSpec((block, n), lambda i: (i, 0))
    return pl.pallas_call(
        functools.partial(second_kernel, count, features),
        grid=(rows // block,),
        in_specs=[
            SMEM_SPEC,
            SMEM_SPEC,
            row(tokens),
            row(tokens),
            row(1),
            row(tokens),
            pl.BlockSpec((tokens, tokens), lambda i: (0, 0), pipeline_mode=pl.Buffered(1)),
        ]
        + [whole_spec((8, tokens))] * count,
        out_specs=[row(tokens), row(tokens), whole_spec((8, tokens))],
        out_shape=[
            jax.ShapeDtypeStruct((rows, tokens), BF16),
            jax.ShapeDtypeStruct((rows, tokens), F32),
            jax.ShapeDtypeStruct((8, tokens), F32),
        ],
        scratch_shapes=[pltpu.VMEM((tokens, tokens), BF16)] * 2,
        compiler_params=params_of(),
        cost_estimate=cost(4 * rows * tokens * tokens, rows * tokens * 16),
    )(index, coef, total, target, gain, moment_product, gram, *sums)


def update_kernel(count, features, idx_ref, p_ref, m_ref, grad_ref, s_ref, t_ref, g_ref, c_ref, *rest):
    sum_refs, (out_ref, master_ref) = rest[:count], rest[count:]
    inv, dot = token_stats(sum_refs, features)
    target = local_tokens(t_ref, idx_ref[0], count).astype(F32)
    grad2 = stream_grad(s_ref[...], target, g_ref[...], inv, dot, s_ref.shape[1])
    rows = grad2.shape[0]
    both = jnp.dot(
        jnp.concatenate([grad_ref[...], grad2], axis=0), c_ref[...], preferred_element_type=F32
    )
    moment = (beta_decay * m_ref[...].astype(F32) + both[:rows]).astype(BF16).astype(F32)
    master = p_ref[...] - learn_rate * moment
    moment = (beta_decay * moment + both[rows:]).astype(BF16)
    master = master - learn_rate * moment.astype(F32)
    out_ref[0] = master.astype(BF16)
    out_ref[1] = moment
    master_ref[...] = master


def update(start, units, index, params, moment, grad, total, target, gain, context, sums, features):
    width = params.shape[1]
    tokens = total.shape[1]
    count = len(sums)
    rows = units * UNIT
    row = lambda n: pl.BlockSpec((UNIT, n), lambda i: (start + i, 0))
    return pl.pallas_call(
        functools.partial(update_kernel, count, features),
        grid=(units,),
        in_specs=[
            SMEM_SPEC,
            row(width),
            row(width),
            row(tokens),
            row(tokens),
            row(tokens),
            row(1),
            whole_spec((tokens, width)),
        ]
        + [whole_spec((8, tokens))] * count,
        out_specs=[
            pl.BlockSpec((2, UNIT, width), lambda i: (0, i, 0)),
            pl.BlockSpec((UNIT, width), lambda i: (i, 0)),
        ],
        out_shape=[
            jax.ShapeDtypeStruct((2, rows, width), BF16),
            jax.ShapeDtypeStruct((rows, width), F32),
        ],
        compiler_params=params_of(),
        cost_estimate=cost(4 * rows * width * tokens, rows * width * 14),
    )(index, params, moment, grad, total, target, gain, context, *sums)


def pair_kernel(coef_ref, master_ref, state_ref, other_ref, out_ref):
    mine, theirs = coef_ref[2], coef_ref[3]
    out_ref[0] = (mine * master_ref[...] + theirs * other_ref[0].astype(F32)).astype(BF16)
    out_ref[1] = (mine * state_ref[0].astype(F32) + theirs * other_ref[1].astype(F32)).astype(BF16)


def pair_sum(coef, master, state, other):
    _, rows, width = state.shape
    block = UNIT
    return pl.pallas_call(
        pair_kernel,
        grid=(rows // block,),
        in_specs=[
            SMEM_SPEC,
            pl.BlockSpec((block, width), lambda i: (i, 0)),
            pl.BlockSpec((1, block, width), lambda i: (1, i, 0)),
            pl.BlockSpec((2, block, width), lambda i: (0, i, 0)),
        ],
        out_specs=pl.BlockSpec((2, block, width), lambda i: (0, i, 0)),
        out_shape=jax.ShapeDtypeStruct((2, rows, width), BF16),
        compiler_params=params_of(),
        cost_estimate=cost(6 * rows * width, rows * width * 14),
    )(coef, master, state, other)


def final_kernel(coef_ref, master_ref, state_ref, sum_ref, *rest):
    p_ref, m_ref = rest[-2:]
    keep = coef_ref[4]
    p_ref[...] = keep * master_ref[...] + sum_ref[0].astype(F32)
    m_ref[...] = (keep * state_ref[0].astype(F32) + sum_ref[1].astype(F32)).astype(BF16)


def final(start, total_rows, coef, master, state, arrived, held):
    _, rows, width = state.shape
    block = UNIT
    out = pl.BlockSpec((block, width), lambda i: (start + i, 0))
    held = held or ()
    return pl.pallas_call(
        final_kernel,
        grid=(rows // block,),
        in_specs=[
            SMEM_SPEC,
            pl.BlockSpec((block, width), lambda i: (i, 0)),
            pl.BlockSpec((1, block, width), lambda i: (1, i, 0)),
            pl.BlockSpec((2, block, width), lambda i: (0, i, 0)),
        ]
        + [pl.BlockSpec(memory_space=pl.ANY)] * len(held),
        out_specs=[out, out],
        out_shape=[
            jax.ShapeDtypeStruct((total_rows, width), F32),
            jax.ShapeDtypeStruct((total_rows, width), BF16),
        ],
        input_output_aliases={4: 0, 5: 1} if held else {},
        compiler_params=params_of(),
        cost_estimate=cost(4 * rows * width, rows * width * 16),
    )(coef, master, state, arrived, *held)


def with_partner(value, distance, count):
    return lax.ppermute(value, "fsdp", [(i, i ^ distance) for i in range(count)])


def gather_tokens(block, count):
    pieces = {0: block}
    distance = count // 2
    while distance:
        for j in list(pieces):
            pieces[j | distance] = with_partner(pieces[j], distance, count)
        distance //= 2
    return jnp.concatenate([pieces[j] for j in range(count)], axis=0)


def all_sums(sums, count):
    return [sums] + [with_partner(sums, m, count) for m in range(1, count)]


def local(context, residual, target, norm_gain, params, momentum, push_weight, mix_num):
    count = lax.axis_size("fsdp")
    replicas = lax.axis_size("rep")
    replica = lax.axis_index("rep")
    index = lax.axis_index("fsdp").astype(jnp.int32)[None]
    residual, target, params, momentum = residual[0], target[0], params[0], momentum[0]
    rows, width = params.shape
    features = rows * count

    shares = mix_num.astype(F32)
    shares = shares / jnp.sum(shares, axis=1, keepdims=True)
    even = replica % 2 == 0
    away = jnp.where(even, (replica + 2) % replicas, (replica - 2) % replicas)
    mine = jnp.where(even, shares[replica, 2], shares[replica, 1])
    theirs = jnp.where(even, shares[away, 1], shares[away, 2])
    keep = shares[replica, 0]
    push = push_weight[0]
    zero = jnp.zeros((), F32)
    coef = jnp.stack([1.0 / push, learn_rate / push, mine, theirs, keep, zero, zero, zero])

    along_z = [(r, (r - 2) % replicas if r % 2 == 0 else (r + 2) % replicas) for r in range(replicas)]
    along_y = [(r, r ^ 1) for r in range(replicas)]

    tokens_all = gather_tokens(context[0], count)
    gain = norm_gain[:, None]
    total, moment_product, sums = forward(
        index, coef, params, momentum, tokens_all, residual, target, gain, count
    )
    sums = all_sums(sums, count)
    gram = lax.dot_general(tokens_all, tokens_all, NT, preferred_element_type=F32)
    grad, total, sums = second(
        index, coef, total, target, gain, moment_product, gram, sums, features
    )
    sums = all_sums(sums, count)

    units = 1
    starts = list(range(0, rows // UNIT, units))
    held = None
    chunks = []
    for start in starts:
        state, master = update(
            start, units, index, params, momentum, grad, total, target, gain, tokens_all, sums, features
        )
        chunks.append((state, master, lax.ppermute(state, "rep", along_z)))
    for at, (state, master, other) in enumerate(chunks):
        both = pair_sum(coef, master, state, other)
        chunks[at] = (state, master, lax.ppermute(both, "rep", along_y))
    for start, (state, master, arrived) in zip(starts, chunks):
        held = final(start, rows, coef, master, state, arrived, held)

    push_row = jnp.broadcast_to(push, (8, 128))
    push_other = lax.ppermute(push_row, "rep", along_z)
    push_sum = lax.ppermute(mine * push_row + theirs * push_other, "rep", along_y)
    new_push = keep * push + push_sum[0, 0]
    return (held[0][None], held[1][None], new_push[None])


def solution(mesh):
    return jax.shard_map(
        local,
        mesh=mesh,
        in_specs=(
            P("rep", "fsdp", None),
            P("rep", "fsdp", None),
            P("rep", "fsdp", None),
            P("fsdp"),
            P("rep", "fsdp", None),
            P("rep", "fsdp", None),
            P("rep"),
            P(),
        ),
        out_specs=(P("rep", "fsdp", None), P("rep", "fsdp", None), P("rep")),
        check_vma=False,
    )
```

time: 731 us -> 684 us (0.936); the launches traced: 731 us -> 676 us
  Pallas kernels: 0 us -> 336 us
  starting transfers between devices: 290 us -> 89.7 us
  waiting for transfers between devices: 308 us -> 229 us
  other arithmetic: 46.2 us -> 3.94 us
  matrix products: 42.7 us -> 2.52 us
  blocking collectives: 24.2 us -> 0 us
  between operations: 19.2 us -> 7.2 us
    pallas_call x0 -> x122, Pallas kernels: none -> 336 us  [the longest x40 142 us: update(): pl.pallas_call(functools.partial(update_kernel, count, features), grid=(u...]
    ppermute x6 -> x91, starting transfers between devices: 290 us -> 89.7 us  [the longest x40 68.9 us: local(): chunks.append((state, master, lax.ppermute(state, 'rep', along_z)))]
    ppermute x6 -> x91, waiting for transfers between devices: 279 us -> 229 us  [the longest x40 150 us: local(): chunks[at] = (state, master, lax.ppermute(both, 'rep', along_y))]
    broadcast_in_dim x2 -> x0, other arithmetic: 40.5 us -> none  [local(): return (new_master[None], mixed_moment.astype(jnp.bfloat16)[None], new_push)]
    dot_general x4 -> x1, matrix products: 42.7 us -> 2.52 us  [local(): lax.dot_general(tokens_all, tokens_all, NT, preferred_element_type=F32)]
    all_gather x1 -> x0, waiting for transfers between devices: 28.6 us -> none  [local(): gathered = lax.all_gather(context[0], 'fsdp', axis=0, tiled=True)]
    psum x4 -> x0, blocking collectives: 24.2 us -> none  [the longest x2 12.8 us: local(): mean_sq = lax.psum(jnp.sum(summed * summed, axis=0), 'fsdp') / D]
  transfers between devices with their start and end apart: 7 -> 91, of which waited for: 3 -> 55; matrix products, arithmetic and copies ran while one was open for 0% -> 2% of each run, Pallas kernels for 0% -> 49%
where the time goes in v1:
time: 684 us; the launch traced here: 676 us
  Pallas kernels  336 us (49%)
  waiting for transfers between devices  229 us (33%)
  starting transfers between devices  89.7 us (13%)
  local copies, waits for them, and re-layouts  7.8 us (1%)
  between operations  7.2 us (1%)
    ppermute x40, waiting for transfers between devices, local(): chunks[at] = (state, master, lax.ppermute(both, 'rep', along_y))  150 us
    pallas_call x40, Pallas kernels, update(): pl.pallas_call(functools.partial(update_kernel, count, features), grid=(u...  142 us
    pallas_call x40, Pallas kernels, pair_sum(): pl.pallas_call(pair_kernel, grid=(rows // block,), in_specs=[SMEM_SPEC, p...  83.6 us
    pallas_call x40, Pallas kernels, final(): pl.pallas_call(final_kernel, grid=(rows // block,), in_specs=[SMEM_SPEC,...  79.1 us
    ppermute x40, starting transfers between devices, local(): chunks.append((state, master, lax.ppermute(state, 'rep', along_z)))  68.9 us
    ppermute x40, waiting for transfers between devices, local(): chunks.append((state, master, lax.ppermute(state, 'rep', along_z)))  60.3 us
    pallas_call x1, Pallas kernels, forward(): pl.pallas_call(functools.partial(forward_kernel, count), grid=(rows // bl...  22.5 us
    ppermute x9, waiting for transfers between devices, with_partner(): lax.ppermute(value, 'fsdp', [(i, i ^ distance) for i in range(count)])  18.5 us
  transfers between devices with their start and end apart: 91, of which 55 were waited for; matrix products, arithmetic and copies ran while one was open for 2% of the time, Pallas kernels for 49%

profile of v1, /device:TPU:0, one launch (start us, length us, event | category | flops | bytes accessed | tf_op | source)
XLA Modules:
  0.0 675.5 jit_solution(12138308874186479255)
XLA Ops:
  3.6 14.9 %collective-permute-done.1 = bf16[128,2560]{1,0:T(8,128)(2,1)S(1)} collective-permute-done((bf16[128,2560]{1,0:T(8,128)(2,1)}, bf16[128,2560]{1,0:T(8,128)(2,1)S(1)}, u32[]{:S(2)}, u32[]{:S(2)}) %collective-permute-start.1) | collective-permute-done | bytes 655392 | tf_op jit(solution)/shard_map/ppermute | solution.py:295
  33.4 22.5 %shard_map.103 = (f32[1280,512]{1,0:T(8,128)}, f32[1280,512]{1,0:T(8,128)}, f32[8,512]{1,0:T(8,128)}) custom-call(s32[1]{0:T(128)} %bitcast.10.idx_ref, f32[8]{0:T(128)} %stack.19.coef_ref, f32[1280,2560]{1,0:T(8,128)} %bitcast.28, bf16[1280,2560]{1,0:T(8,128)(2,1)} %bitcast.70, bf16[512,2560]{1,0:T(8,128)(2,1)} %pad_maximum_fusion.c_ref, ...), custom_call_target="tpu_custom_call" | custom-call | flops 6710886400 | bytes 19660800 | tf_op jit(solution)/shard_map/pallas_call | solution.py:106
  61.7 8.3 %shard_map.104 = (bf16[1280,512]{1,0:T(8,128)(2,1)}, f32[1280,512]{1,0:T(8,128)}, f32[8,512]{1,0:T(8,128)}) custom-call(s32[1]{0:T(128)} %bitcast.10.idx_ref, f32[8]{0:T(128)} %stack.19.coef_ref, f32[1280,512]{1,0:T(8,128)} %get-tuple-element.169.s_ref, bf16[1280,512]{1,0:T(8,128)(2,1)} %bitcast.113, f32[1280,1]{1,0:T(8,128)} %broadcast_in_dim.25.g_ref, ...), custom_call_target="tpu_custom_call" | custom-call | flops 1342177280 | bytes 10485760 | tf_op jit(solution)/shard_map/pallas_call | solution.py:160
  328.5 11.7 %collective-permute-start.9 = (bf16[2,32,2560]{2,1,0:T(8,128)(2,1)}, bf16[2,32,2560]{2,1,0:T(8,128)(2,1)S(1)}, u32[]{:S(2)}, u32[]{:S(2)}) collective-permute-start(bf16[2,32,2560]{2,1,0:T(8,128)(2,1)} %get-tuple-element.176.state_ref), channel_id=1, source_target_pairs={{0,24},{4,12},{8,0},{12,20},{16,8},{20,28},{24,16},{28,4},{1,25},{... | collective-permute-start | bytes 983048 | tf_op jit(solution)/shard_map/ppermute | solution.py:355
  383.3 4.9 collective-permute-done.78.sum_ref
  404.4 4.9 collective-permute-done.72.sum_ref
  418.4 4.9 collective-permute-done.68.sum_ref
  432.5 4.9 collective-permute-done.64.sum_ref
  446.5 4.9 collective-permute-done.60.sum_ref
  460.5 4.9 collective-permute-done.56.sum_ref
  474.6 4.9 collective-permute-done.52.sum_ref
  481.6 4.9 collective-permute-done.50.sum_ref
  495.7 4.9 collective-permute-done.46.sum_ref
  502.7 4.9 collective-permute-done.44.sum_ref
  516.7 4.9 collective-permute-done.40.sum_ref
  523.8 4.9 collective-permute-done.38.sum_ref
  530.8 4.9 collective-permute-done.36.sum_ref
  537.8 4.9 collective-permute-done.34.sum_ref
  544.8 4.9 collective-permute-done.32.sum_ref
  551.8 4.9 collective-permute-done.30.sum_ref
  565.9 4.9 collective-permute-done.26.sum_ref
  572.9 4.9 collective-permute-done.24.sum_ref
  579.9 4.9 collective-permute-done.22.sum_ref
  586.9 4.9 collective-permute-done.20.sum_ref
  (499 shorter events, 512.8 us)
Async XLA Ops:
  19.2 52.7 %collective-permute-start.89 = (f32[8,128]{1,0:T(8,128)S(1)}, f32[8,128]{1,0:T(8,128)S(1)}, u32[]{:S(2)}, u32[]{:S(2)}) collective-permute-start(f32[8,128]{1,0:T(8,128)S(1)} %broadcast_in_dim.23), channel_id=1, source_target_pairs={{0,24},{4,12},{8,0},{12,20},{16,8},{20,28},{24,16},{28,4},{1,25},{... | collective-permute-start | bytes 12296 | tf_op jit(solution)/shard_map/ppermute | solution.py:363
  145.9 35.1 %collective-permute-start.61 = (bf16[2,32,2560]{2,1,0:T(8,128)(2,1)}, bf16[2,32,2560]{2,1,0:T(8,128)(2,1)S(1)}, u32[]{:S(2)}, u32[]{:S(2)}) collective-permute-start(bf16[2,32,2560]{2,1,0:T(8,128)(2,1)} %get-tuple-element.228.state_ref), channel_id=1, source_target_pairs={{0,24},{4,12},{8,0},{12,20},{16,8},{20,28},{24,16},{28,4},{1,25},{... | collective-permute-start | bytes 983048 | tf_op jit(solution)/shard_map/ppermute | solution.py:355
  153.0 35.1 %collective-permute-start.59 = (bf16[2,32,2560]{2,1,0:T(8,128)(2,1)}, bf16[2,32,2560]{2,1,0:T(8,128)(2,1)S(1)}, u32[]{:S(2)}, u32[]{:S(2)}) collective-permute-start(bf16[2,32,2560]{2,1,0:T(8,128)(2,1)} %get-tuple-element.226.state_ref), channel_id=1, source_target_pairs={{0,24},{4,12},{8,0},{12,20},{16,8},{20,28},{24,16},{28,4},{1,25},{... | collective-permute-start | bytes 983048 | tf_op jit(solution)/shard_map/ppermute | solution.py:355
  169.4 35.2 %collective-permute-start.57 = (bf16[2,32,2560]{2,1,0:T(8,128)(2,1)S(1)}, bf16[2,32,2560]{2,1,0:T(8,128)(2,1)S(1)}, u32[]{:S(2)}, u32[]{:S(2)}) collective-permute-start(bf16[2,32,2560]{2,1,0:T(8,128)(2,1)S(1)} %copy-done.16), channel_id=1, source_target_pairs={{0,24},{4,12},{8,0},{12,20},{16,8},{20,28},{24,16},{28,4},{1,25},{... | collective-permute-start | bytes 983048 | tf_op jit(solution)/shard_map/ppermute | solution.py:355
  169.6 35.2 %collective-permute-start.55 = (bf16[2,32,2560]{2,1,0:T(8,128)(2,1)S(1)}, bf16[2,32,2560]{2,1,0:T(8,128)(2,1)S(1)}, u32[]{:S(2)}, u32[]{:S(2)}) collective-permute-start(bf16[2,32,2560]{2,1,0:T(8,128)(2,1)S(1)} %copy-done.11), channel_id=1, source_target_pairs={{0,24},{4,12},{8,0},{12,20},{16,8},{20,28},{24,16},{28,4},{1,25},{... | collective-permute-start | bytes 983048 | tf_op jit(solution)/shard_map/ppermute | solution.py:355
  181.1 35.1 %collective-permute-start.51 = (bf16[2,32,2560]{2,1,0:T(8,128)(2,1)}, bf16[2,32,2560]{2,1,0:T(8,128)(2,1)S(1)}, u32[]{:S(2)}, u32[]{:S(2)}) collective-permute-start(bf16[2,32,2560]{2,1,0:T(8,128)(2,1)} %get-tuple-element.218.state_ref), channel_id=1, source_target_pairs={{0,24},{4,12},{8,0},{12,20},{16,8},{20,28},{24,16},{28,4},{1,25},{... | collective-permute-start | bytes 983048 | tf_op jit(solution)/shard_map/ppermute | solution.py:355
  204.6 35.2 %collective-permute-start.47 = (bf16[2,32,2560]{2,1,0:T(8,128)(2,1)S(1)}, bf16[2,32,2560]{2,1,0:T(8,128)(2,1)S(1)}, u32[]{:S(2)}, u32[]{:S(2)}) collective-permute-start(bf16[2,32,2560]{2,1,0:T(8,128)(2,1)S(1)} %copy-done.19), channel_id=1, source_target_pairs={{0,24},{4,12},{8,0},{12,20},{16,8},{20,28},{24,16},{28,4},{1,25},{... | collective-permute-start | bytes 983048 | tf_op jit(solution)/shard_map/ppermute | solution.py:355
  204.7 35.2 %collective-permute-start.45 = (bf16[2,32,2560]{2,1,0:T(8,128)(2,1)S(1)}, bf16[2,32,2560]{2,1,0:T(8,128)(2,1)S(1)}, u32[]{:S(2)}, u32[]{:S(2)}) collective-permute-start(bf16[2,32,2560]{2,1,0:T(8,128)(2,1)S(1)} %copy-done.15), channel_id=1, source_target_pairs={{0,24},{4,12},{8,0},{12,20},{16,8},{20,28},{24,16},{28,4},{1,25},{... | collective-permute-start | bytes 983048 | tf_op jit(solution)/shard_map/ppermute | solution.py:355
  223.2 35.1 %collective-permute-start.39 = (bf16[2,32,2560]{2,1,0:T(8,128)(2,1)}, bf16[2,32,2560]{2,1,0:T(8,128)(2,1)S(1)}, u32[]{:S(2)}, u32[]{:S(2)}) collective-permute-start(bf16[2,32,2560]{2,1,0:T(8,128)(2,1)} %get-tuple-element.206.state_ref), channel_id=1, source_target_pairs={{0,24},{4,12},{8,0},{12,20},{16,8},{20,28},{24,16},{28,4},{1,25},{... | collective-permute-start | bytes 983048 | tf_op jit(solution)/shard_map/ppermute | solution.py:355
  251.3 35.1 %collective-permute-start.31 = (bf16[2,32,2560]{2,1,0:T(8,128)(2,1)}, bf16[2,32,2560]{2,1,0:T(8,128)(2,1)S(1)}, u32[]{:S(2)}, u32[]{:S(2)}) collective-permute-start(bf16[2,32,2560]{2,1,0:T(8,128)(2,1)} %get-tuple-element.198.state_ref), channel_id=1, source_target_pairs={{0,24},{4,12},{8,0},{12,20},{16,8},{20,28},{24,16},{28,4},{1,25},{... | collective-permute-start | bytes 983048 | tf_op jit(solution)/shard_map/ppermute | solution.py:355
  258.3 35.1 %collective-permute-start.29 = (bf16[2,32,2560]{2,1,0:T(8,128)(2,1)}, bf16[2,32,2560]{2,1,0:T(8,128)(2,1)S(1)}, u32[]{:S(2)}, u32[]{:S(2)}) collective-permute-start(bf16[2,32,2560]{2,1,0:T(8,128)(2,1)} %get-tuple-element.196.state_ref), channel_id=1, source_target_pairs={{0,24},{4,12},{8,0},{12,20},{16,8},{20,28},{24,16},{28,4},{1,25},{... | collective-permute-start | bytes 983048 | tf_op jit(solution)/shard_map/ppermute | solution.py:355
  293.4 35.1 %collective-permute-start.19 = (bf16[2,32,2560]{2,1,0:T(8,128)(2,1)}, bf16[2,32,2560]{2,1,0:T(8,128)(2,1)S(1)}, u32[]{:S(2)}, u32[]{:S(2)}) collective-permute-start(bf16[2,32,2560]{2,1,0:T(8,128)(2,1)} %get-tuple-element.186.state_ref), channel_id=1, source_target_pairs={{0,24},{4,12},{8,0},{12,20},{16,8},{20,28},{24,16},{28,4},{1,25},{... | collective-permute-start | bytes 983048 | tf_op jit(solution)/shard_map/ppermute | solution.py:355
  321.5 35.1 %collective-permute-start.11 = (bf16[2,32,2560]{2,1,0:T(8,128)(2,1)}, bf16[2,32,2560]{2,1,0:T(8,128)(2,1)S(1)}, u32[]{:S(2)}, u32[]{:S(2)}) collective-permute-start(bf16[2,32,2560]{2,1,0:T(8,128)(2,1)} %get-tuple-element.178.state_ref), channel_id=1, source_target_pairs={{0,24},{4,12},{8,0},{12,20},{16,8},{20,28},{24,16},{28,4},{1,25},{... | collective-permute-start | bytes 983048 | tf_op jit(solution)/shard_map/ppermute | solution.py:355
  381.2 35.1 %collective-permute-start.70 = (bf16[2,32,2560]{2,1,0:T(8,128)(2,1)}, bf16[2,32,2560]{2,1,0:T(8,128)(2,1)S(1)}, u32[]{:S(2)}, u32[]{:S(2)}) collective-permute-start(bf16[2,32,2560]{2,1,0:T(8,128)(2,1)} %shard_map.166), channel_id=1, source_target_pairs={{0,4},{4,0},{8,12},{12,8},{16,20},{20,16},{24,28},{28,24},{1,5},{5... | collective-permute-start | bytes 983048 | tf_op jit(solution)/shard_map/ppermute | solution.py:358
  416.3 35.1 %collective-permute-start.60 = (bf16[2,32,2560]{2,1,0:T(8,128)(2,1)}, bf16[2,32,2560]{2,1,0:T(8,128)(2,1)S(1)}, u32[]{:S(2)}, u32[]{:S(2)}) collective-permute-start(bf16[2,32,2560]{2,1,0:T(8,128)(2,1)} %shard_map.156), channel_id=1, source_target_pairs={{0,4},{4,0},{8,12},{12,8},{16,20},{20,16},{24,28},{28,24},{1,5},{5... | collective-permute-start | bytes 983048 | tf_op jit(solution)/shard_map/ppermute | solution.py:358
  423.3 35.1 %collective-permute-start.58 = (bf16[2,32,2560]{2,1,0:T(8,128)(2,1)}, bf16[2,32,2560]{2,1,0:T(8,128)(2,1)S(1)}, u32[]{:S(2)}, u32[]{:S(2)}) collective-permute-start(bf16[2,32,2560]{2,1,0:T(8,128)(2,1)} %shard_map.154), channel_id=1, source_target_pairs={{0,4},{4,0},{8,12},{12,8},{16,20},{20,16},{24,28},{28,24},{1,5},{5... | collective-permute-start | bytes 983048 | tf_op jit(solution)/shard_map/ppermute | solution.py:358
  430.4 35.1 %collective-permute-start.56 = (bf16[2,32,2560]{2,1,0:T(8,128)(2,1)}, bf16[2,32,2560]{2,1,0:T(8,128)(2,1)S(1)}, u32[]{:S(2)}, u32[]{:S(2)}) collective-permute-start(bf16[2,32,2560]{2,1,0:T(8,128)(2,1)} %shard_map.152), channel_id=1, source_target_pairs={{0,4},{4,0},{8,12},{12,8},{16,20},{20,16},{24,28},{28,24},{1,5},{5... | collective-permute-start | bytes 983048 | tf_op jit(solution)/shard_map/ppermute | solution.py:358
  437.4 35.1 %collective-permute-start.54 = (bf16[2,32,2560]{2,1,0:T(8,128)(2,1)}, bf16[2,32,2560]{2,1,0:T(8,128)(2,1)S(1)}, u32[]{:S(2)}, u32[]{:S(2)}) collective-permute-start(bf16[2,32,2560]{2,1,0:T(8,128)(2,1)} %shard_map.150), channel_id=1, source_target_pairs={{0,4},{4,0},{8,12},{12,8},{16,20},{20,16},{24,28},{28,24},{1,5},{5... | collective-permute-start | bytes 983048 | tf_op jit(solution)/shard_map/ppermute | solution.py:358
  444.4 35.1 %collective-permute-start.52 = (bf16[2,32,2560]{2,1,0:T(8,128)(2,1)}, bf16[2,32,2560]{2,1,0:T(8,128)(2,1)S(1)}, u32[]{:S(2)}, u32[]{:S(2)}) collective-permute-start(bf16[2,32,2560]{2,1,0:T(8,128)(2,1)} %shard_map.148), channel_id=1, source_target_pairs={{0,4},{4,0},{8,12},{12,8},{16,20},{20,16},{24,28},{28,24},{1,5},{5... | collective-permute-start | bytes 983048 | tf_op jit(solution)/shard_map/ppermute | solution.py:358
  563.8 100.5 %collective-permute-start.18 = (bf16[2,32,2560]{2,1,0:T(8,128)(2,1)}, bf16[2,32,2560]{2,1,0:T(8,128)(2,1)}, u32[]{:S(2)}, u32[]{:S(2)}) collective-permute-start(bf16[2,32,2560]{2,1,0:T(8,128)(2,1)} %shard_map.114), channel_id=1, source_target_pairs={{0,4},{4,0},{8,12},{12,8},{16,20},{20,16},{24,28},{28,24},{1,5},{5... | collective-permute-start | bytes 983048 | tf_op jit(solution)/shard_map/ppermute | solution.py:358
  570.8 95.5 %collective-permute-start.16 = (bf16[2,32,2560]{2,1,0:T(8,128)(2,1)}, bf16[2,32,2560]{2,1,0:T(8,128)(2,1)}, u32[]{:S(2)}, u32[]{:S(2)}) collective-permute-start(bf16[2,32,2560]{2,1,0:T(8,128)(2,1)} %shard_map.112), channel_id=1, source_target_pairs={{0,4},{4,0},{8,12},{12,8},{16,20},{20,16},{24,28},{28,24},{1,5},{5... | collective-permute-start | bytes 983048 | tf_op jit(solution)/shard_map/ppermute | solution.py:358
  577.8 90.4 %collective-permute-start.14 = (bf16[2,32,2560]{2,1,0:T(8,128)(2,1)}, bf16[2,32,2560]{2,1,0:T(8,128)(2,1)}, u32[]{:S(2)}, u32[]{:S(2)}) collective-permute-start(bf16[2,32,2560]{2,1,0:T(8,128)(2,1)} %shard_map.110), channel_id=1, source_target_pairs={{0,4},{4,0},{8,12},{12,8},{16,20},{20,16},{24,28},{28,24},{1,5},{5... | collective-permute-start | bytes 983048 | tf_op jit(solution)/shard_map/ppermute | solution.py:358
  584.8 85.4 %collective-permute-start.12 = (bf16[2,32,2560]{2,1,0:T(8,128)(2,1)}, bf16[2,32,2560]{2,1,0:T(8,128)(2,1)}, u32[]{:S(2)}, u32[]{:S(2)}) collective-permute-start(bf16[2,32,2560]{2,1,0:T(8,128)(2,1)} %shard_map.108), channel_id=1, source_target_pairs={{0,4},{4,0},{8,12},{12,8},{16,20},{20,16},{24,28},{28,24},{1,5},{5... | collective-permute-start | bytes 983048 | tf_op jit(solution)/shard_map/ppermute | solution.py:358
  591.9 80.4 %collective-permute-start.10 = (bf16[2,32,2560]{2,1,0:T(8,128)(2,1)}, bf16[2,32,2560]{2,1,0:T(8,128)(2,1)}, u32[]{:S(2)}, u32[]{:S(2)}) collective-permute-start(bf16[2,32,2560]{2,1,0:T(8,128)(2,1)} %shard_map.106), channel_id=1, source_target_pairs={{0,4},{4,0},{8,12},{12,8},{16,20},{20,16},{24,28},{28,24},{1,5},{5... | collective-permute-start | bytes 983048 | tf_op jit(solution)/shard_map/ppermute | solution.py:358
  (171 other events, 4646.2 us)

commit v2 on v1

v2 whole, which is shorter than its diff:
```python
import functools

import jax
import jax.numpy as jnp
from jax import lax
from jax.experimental import pallas as pl
from jax.experimental.pallas import tpu as pltpu
from jax.sharding import PartitionSpec as P

epsilon = 1e-05
learn_rate = 0.5
beta_decay = 0.9

UNIT = 32
CHUNK = 64
Z_AHEAD = 3
Y_AHEAD = 2
MIB = 1024 * 1024
FORWARD_ROWS = 256
FORWARD_MIB = SECOND_MIB = STEP_MIB = PAIR_MIB = 24
F32 = jnp.float32
BF16 = jnp.bfloat16
NT = (((1,), (1,)), ((), ()))

SMEM_SPEC = pl.BlockSpec(memory_space=pltpu.SMEM)


def whole_spec(shape):
    return pl.BlockSpec(shape, lambda i: (0,) * len(shape))


def params_of(limit):
    return pltpu.CompilerParams(
        dimension_semantics=("arbitrary",), vmem_limit_bytes=limit
    )


def cost(flops, nbytes):
    return pl.CostEstimate(flops=flops, bytes_accessed=nbytes, transcendentals=0)


def shares_of(mix_ref):
    replicas = mix_ref.shape[0] // 3
    replica = lax.axis_index("rep")
    odd = lax.rem(replica, 2)
    away = lax.rem(replica + jnp.where(odd == 1, replicas - 2, 2), replicas)

    def share(at, column):
        row = [mix_ref[3 * at + k].astype(F32) for k in range(3)]
        return mix_ref[3 * at + column].astype(F32) / (row[0] + row[1] + row[2])

    return share(replica, 0), share(replica, 2 - odd), share(away, 1 + odd)


def neighbour_shares(mix_ref):
    replicas = mix_ref.shape[0] // 3
    replica = lax.axis_index("rep")

    def share(at, column):
        row = [mix_ref[3 * at + k].astype(F32) for k in range(3)]
        return row[column] / (row[0] + row[1] + row[2])

    lower = lax.rem(replica + replicas - 1, replicas)
    upper = lax.rem(replica + 1, replicas)
    return share(replica, 0), share(lower, 2), share(upper, 1)


def local_tokens(ref, index, count):
    width = ref.shape[1] // count
    blocks = [
        ref[:, pl.ds(pl.multiple_of(lax.bitwise_xor(index, j) * width, width), width)]
        for j in range(count)
    ]
    return jnp.concatenate(blocks, axis=1)


def add_sums(sums_ref, step, total, scaled, target):
    parts = jnp.concatenate(
        [
            jnp.sum(total * total, axis=0, keepdims=True),
            jnp.sum(scaled * scaled, axis=0, keepdims=True),
            jnp.sum(scaled * target, axis=0, keepdims=True),
            jnp.zeros((5, total.shape[1]), F32),
        ],
        axis=0,
    )

    @pl.when(step == 0)
    def _():
        sums_ref[...] = parts

    @pl.when(step > 0)
    def _():
        sums_ref[...] += parts


def token_stats(sum_refs, features):
    count = len(sum_refs)
    tokens = sum_refs[0].shape[1]
    width = tokens // count
    full = sum_refs[0][...]
    for m in range(1, count):
        other = sum_refs[m]
        full = full + jnp.concatenate(
            [other[:, (j ^ m) * width : ((j ^ m) + 1) * width] for j in range(count)],
            axis=1,
        )
    inv = lax.rsqrt(full[0:1] / features + epsilon)
    dot = (inv * full[1:2] - full[2:3]) / (tokens * features)
    return inv, dot


def stream_grad(total, target, gain, inv, dot, tokens):
    scaled = gain * ((gain * total * inv - target) / tokens)
    return (scaled * inv - total * (inv * inv * inv * dot)).astype(BF16)


def transpose_pieces(piece_refs, out_ref):
    width = piece_refs[0].shape[0]
    for j, piece in enumerate(piece_refs):
        out_ref[:, j * width : (j + 1) * width] = piece[...].T


def forward_kernel(count, mix_ref, push_ref, low_ref, high_ref, p_ref, m_ref, r_ref, t_ref, g_ref, *rest):
    pieces, (s_ref, y_ref, q_ref, c_ref, push_out, ct_ref) = rest[:count], rest[count:]
    index = lax.axis_index("fsdp")
    step = pl.program_id(0)

    @pl.when(step == 0)
    def _():
        transpose_pieces(pieces, ct_ref)
        width = pieces[0].shape[0]
        for j, piece in enumerate(pieces):
            c_ref[j * width : (j + 1) * width, :] = piece[...]
        keep, lower, upper = neighbour_shares(mix_ref)
        push_out[...] = keep * push_ref[0] + lower * low_ref[...] + upper * high_ref[...]

    rows = p_ref.shape[0]
    weights = (p_ref[...] * (1.0 / push_ref[0])).astype(BF16)
    both = jnp.concatenate([weights, m_ref[...]], axis=0)
    product = jnp.dot(both, ct_ref[...], preferred_element_type=F32)
    y_ref[...] = product[rows:]
    total = local_tokens(r_ref, index, count).astype(F32) + product[:rows]
    s_ref[...] = total
    target = local_tokens(t_ref, index, count).astype(F32)
    add_sums(q_ref, step, total, g_ref[...] * total, target)


def forward(mix, push, lower, upper, params, moment, residual, target, gain, pieces):
    rows, width = params.shape
    piece = pieces[0].shape[0]
    count = len(pieces)
    tokens = piece * count
    block = FORWARD_ROWS if rows % FORWARD_ROWS == 0 else 64
    row = lambda n: pl.BlockSpec((block, n), lambda i: (i, 0))
    return pl.pallas_call(
        functools.partial(forward_kernel, count),
        grid=(rows // block,),
        in_specs=[
            SMEM_SPEC,
            SMEM_SPEC,
            whole_spec((8, 128)),
            whole_spec((8, 128)),
            row(width),
            row(width),
            row(tokens),
            row(tokens),
            row(1),
        ]
        + [whole_spec((piece, width))] * count,
        out_specs=[
            row(tokens),
            row(tokens),
            whole_spec((8, tokens)),
            whole_spec((tokens, width)),
            whole_spec((8, 128)),
        ],
        out_shape=[
            jax.ShapeDtypeStruct((rows, tokens), F32),
            jax.ShapeDtypeStruct((rows, tokens), F32),
            jax.ShapeDtypeStruct((8, tokens), F32),
            jax.ShapeDtypeStruct((tokens, width), BF16),
            jax.ShapeDtypeStruct((8, 128), F32),
        ],
        scratch_shapes=[pltpu.VMEM((width, tokens), BF16)],
        compiler_params=params_of(FORWARD_MIB * MIB if tokens <= 512 else 58 * MIB),
        cost_estimate=cost(4 * rows * width * tokens, rows * width * 6),
    )(mix, push, lower, upper, params, moment, residual, target, gain, *pieces)


def second_kernel(count, features, push_ref, s_ref, t_ref, g_ref, y_ref, gram_ref, *rest):
    sum_refs, (grad_ref, s2_ref, q_ref, high_ref, low_ref) = rest[:count], rest[count:]
    index = lax.axis_index("fsdp")
    step = pl.program_id(0)

    @pl.when(step == 0)
    def _():
        gram = gram_ref[...]
        high = gram.astype(BF16)
        high_ref[...] = high
        low_ref[...] = (gram - high.astype(F32)).astype(BF16)

    inv, dot = token_stats(sum_refs, features)
    total = s_ref[...]
    target = local_tokens(t_ref, index, count).astype(F32)
    gain = g_ref[...]
    grad = stream_grad(total, target, gain, inv, dot, total.shape[1])
    grad_ref[...] = grad
    moved = jnp.dot(grad, high_ref[...], preferred_element_type=F32)
    moved += jnp.dot(grad, low_ref[...], preferred_element_type=F32)
    total = total - (learn_rate / push_ref[0]) * (beta_decay * y_ref[...] + moved)
    s2_ref[...] = total
    add_sums(q_ref, step, total, gain * total, target)


def second(push, total, target, gain, moment_product, gram, sums, features):
    rows, tokens = total.shape
    count = len(sums)
    block = min(256, rows) if rows % 256 == 0 else min(64, rows)
    row = lambda n: pl.BlockSpec((block, n), lambda i: (i, 0))
    return pl.pallas_call(
        functools.partial(second_kernel, count, features),
        grid=(rows // block,),
        in_specs=[
            SMEM_SPEC,
            row(tokens),
            row(tokens),
            row(1),
            row(tokens),
            pl.BlockSpec((tokens, tokens), lambda i: (0, 0), pipeline_mode=pl.Buffered(1)),
        ]
        + [whole_spec((8, tokens))] * count,
        out_specs=[row(tokens), row(tokens), whole_spec((8, tokens))],
        out_shape=[
            jax.ShapeDtypeStruct((rows, tokens), BF16),
            jax.ShapeDtypeStruct((rows, tokens), F32),
            jax.ShapeDtypeStruct((8, tokens), F32),
        ],
        scratch_shapes=[pltpu.VMEM((tokens, tokens), BF16)] * 2,
        compiler_params=params_of(SECOND_MIB * MIB if tokens <= 512 else 56 * MIB),
        cost_estimate=cost(4 * rows * tokens * tokens, rows * tokens * 16),
    )(push, total, target, gain, moment_product, gram, *sums)


def step_kernel(count, features, has_update, has_final, waits, *refs):
    refs = list(refs)
    take = lambda n: [refs.pop(0) for _ in range(n)]
    (mix_ref,) = take(1)
    if has_update:
        p_in, m_in, grad_ref, s_ref, t_ref, g_ref, c_ref = take(7)
        sum_refs = take(count)
    if has_final:
        master_in, state_in, arrived_ref = take(3)
    take(waits)
    if has_update:
        state_ref, master_ref = take(2)
        inv, dot = token_stats(sum_refs, features)
        target = local_tokens(t_ref, lax.axis_index("fsdp"), count).astype(F32)
        grad2 = stream_grad(s_ref[...], target, g_ref[...], inv, dot, s_ref.shape[1])
        rows = grad2.shape[0]
        both = jnp.dot(
            jnp.concatenate([grad_ref[...], grad2], axis=0),
            c_ref[...],
            preferred_element_type=F32,
        )
        moment = (beta_decay * m_in[...].astype(F32) + both[:rows]).astype(BF16).astype(F32)
        master = p_in[...] - learn_rate * moment
        moment = (beta_decay * moment + both[rows:]).astype(BF16)
        master = master - learn_rate * moment.astype(F32)
        state_ref[0] = master.astype(BF16)
        state_ref[1] = moment
        master_ref[...] = master
    if has_final:
        p_out, m_out = take(2)
        keep, _, _ = shares_of(mix_ref)
        p_out[...] = keep * master_in[...] + arrived_ref[0].astype(F32)
        m_out[...] = (keep * state_in[0].astype(F32) + arrived_ref[1].astype(F32)).astype(BF16)


def step_call(mix, rows, update, done, held, after, features):
    units = rows // UNIT
    operands, specs, out_specs, out_shape = [mix], [SMEM_SPEC], [], []
    count = 0
    flops = nbytes = 0
    if update:
        start, arrays, sums = update
        params, moment, grad, total, target, gain, context = arrays
        width, tokens, count = params.shape[1], total.shape[1], len(sums)
        first = start // UNIT
        row = lambda n: pl.BlockSpec((UNIT, n), lambda i: (first + i, 0))
        operands += [*arrays, *sums]
        specs += [row(width), row(width), row(tokens), row(tokens), row(tokens), row(1)]
        specs += [whole_spec((tokens, width))] + [whole_spec((8, tokens))] * count
        flops += 4 * rows * width * tokens
        nbytes += rows * width * 14
    if done:
        begin, all_rows, master, state, arrived = done
        width = master.shape[1]
        operands += [master, state, arrived]
        specs += [
            pl.BlockSpec((UNIT, width), lambda i: (i, 0)),
            pl.BlockSpec((1, UNIT, width), lambda i: (1, i, 0)),
            pl.BlockSpec((2, UNIT, width), lambda i: (0, i, 0)),
        ]
        nbytes += rows * width * 16
    waits = [*(held if done and held else ()), *after]
    alias = {}
    if done and held:
        alias = {len(operands): 2 if update else 0, len(operands) + 1: 3 if update else 1}
    operands += waits
    specs += [pl.BlockSpec(memory_space=pl.ANY)] * len(waits)
    if update:
        out_specs += [
            pl.BlockSpec((2, UNIT, width), lambda i: (0, i, 0)),
            pl.BlockSpec((UNIT, width), lambda i: (i, 0)),
        ]
        out_shape += [
            jax.ShapeDtypeStruct((2, rows, width), BF16),
            jax.ShapeDtypeStruct((rows, width), F32),
        ]
    if done:
        at = begin // UNIT
        out_specs += [pl.BlockSpec((UNIT, width), lambda i: (at + i, 0))] * 2
        out_shape += [
            jax.ShapeDtypeStruct((all_rows, width), F32),
            jax.ShapeDtypeStruct((all_rows, width), BF16),
        ]
    out = pl.pallas_call(
        functools.partial(
            step_kernel, count, features, bool(update), bool(done), len(waits)
        ),
        grid=(units,),
        in_specs=specs,
        out_specs=out_specs,
        out_shape=out_shape,
        input_output_aliases=alias,
        compiler_params=params_of(STEP_MIB * MIB),
        cost_estimate=cost(flops, nbytes),
    )(*operands)
    made = tuple(out[:2]) if update else None
    return made, tuple(out[-2:]) if done else held


def pair_kernel(mix_ref, master_ref, state_ref, other_ref, *rest):
    out_ref = rest[-1]
    _, mine, theirs = shares_of(mix_ref)
    out_ref[0] = (mine * master_ref[...] + theirs * other_ref[0].astype(F32)).astype(BF16)
    out_ref[1] = (mine * state_ref[0].astype(F32) + theirs * other_ref[1].astype(F32)).astype(BF16)


def pair_sum(mix, master, state, other, after):
    _, rows, width = state.shape
    return pl.pallas_call(
        pair_kernel,
        grid=(rows // UNIT,),
        in_specs=[
            SMEM_SPEC,
            pl.BlockSpec((UNIT, width), lambda i: (i, 0)),
            pl.BlockSpec((1, UNIT, width), lambda i: (1, i, 0)),
            pl.BlockSpec((2, UNIT, width), lambda i: (0, i, 0)),
        ]
        + [pl.BlockSpec(memory_space=pl.ANY)] * len(after),
        out_specs=pl.BlockSpec((2, UNIT, width), lambda i: (0, i, 0)),
        out_shape=jax.ShapeDtypeStruct((2, rows, width), BF16),
        compiler_params=params_of(PAIR_MIB * MIB),
        cost_estimate=cost(6 * rows * width, rows * width * 14),
    )(mix, master, state, other, *after)


def with_partner(value, distance, count):
    return lax.ppermute(value, "fsdp", [(i, i ^ distance) for i in range(count)])


def gather_low(block, count):
    pieces = {0: block}
    distance = count // 4
    while distance:
        for j in list(pieces):
            pieces[j | distance] = with_partner(pieces[j], distance, count)
        distance //= 2
    return [pieces[j] for j in sorted(pieces)]


def all_sums(sums, count):
    return [sums] + [with_partner(sums, m, count) for m in range(1, count)]


def local(context, residual, target, norm_gain, params, momentum, push_weight, mix_num):
    count = lax.axis_size("fsdp")
    replicas = lax.axis_size("rep")
    residual, target, params, momentum = residual[0], target[0], params[0], momentum[0]
    rows, width = params.shape
    features = rows * count

    along_z = [(r, (r - 2) % replicas if r % 2 == 0 else (r + 2) % replicas) for r in range(replicas)]
    along_y = [(r, r ^ 1) for r in range(replicas)]
    over_z = lambda value: lax.ppermute(value, "rep", along_z)
    over_y = lambda value: lax.ppermute(value, "rep", along_y)

    far = with_partner(context[0], count // 2, count)
    near_pieces = gather_low(context[0], count)
    push_row = jnp.broadcast_to(push_weight, (8, 128))
    push_lower = lax.ppermute(push_row, "rep", [(r, (r + 1) % replicas) for r in range(replicas)])
    push_upper = lax.ppermute(push_row, "rep", [(r, (r - 1) % replicas) for r in range(replicas)])
    gain = norm_gain[:, None]
    mix = mix_num.reshape(-1)
    far, gain, push_lower, push_upper, mix, *near_pieces = lax.optimization_barrier(
        (far, gain, push_lower, push_upper, mix, *near_pieces)
    )
    pieces = near_pieces + gather_low(far, count)
    total, moment_product, sums, tokens_all, new_push = forward(
        mix,
        push_weight,
        push_lower,
        push_upper,
        params,
        momentum,
        residual,
        target,
        gain,
        pieces,
    )
    sums = all_sums(sums, count)
    gram = lax.dot_general(tokens_all, tokens_all, NT, preferred_element_type=F32)
    grad, total, sums = second(
        push_weight, total, target, gain, moment_product, gram, sums, features
    )
    sums = all_sums(sums, count)

    arrays = (params, momentum, grad, total, target, gain, tokens_all)
    chunk = CHUNK if rows % CHUNK == 0 else UNIT
    chunks = rows // chunk
    made, crossing, arriving = {}, {}, {}
    held = None
    last = ()
    for c in range(-Z_AHEAD, chunks + Y_AHEAD):
        if 0 <= c < chunks:
            state, master = made[c]
            both = pair_sum(mix, master, state, crossing.pop(c), last)
            arriving[c] = over_y(both)
            last = (both,)
        ahead, behind = c + Z_AHEAD, c - Y_AHEAD
        update = (ahead * chunk, arrays, sums) if ahead < chunks else None
        done = None
        if behind >= 0:
            state, master = made.pop(behind)
            done = (behind * chunk, rows, master, state, arriving.pop(behind))
        if update or done:
            out, held = step_call(mix, chunk, update, done, held, last, features)
            if out:
                made[ahead] = out
                crossing[ahead] = over_z(out[0])
                last = (out[0],)
    return (held[0][None], held[1][None], new_push[0, 0:1])


def solution(mesh):
    return jax.shard_map(
        local,
        mesh=mesh,
        in_specs=(
            P("rep", "fsdp", None),
            P("rep", "fsdp", None),
            P("rep", "fsdp", None),
            P("fsdp"),
            P("rep", "fsdp", None),
            P("rep", "fsdp", None),
            P("rep"),
            P(),
        ),
        out_specs=(P("rep", "fsdp", None), P("rep", "fsdp", None), P("rep")),
        check_vma=False,
    )
```

time: 684 us -> 384 us (0.56); the launches traced: 676 us -> 383 us
  Pallas kernels: 336 us -> 103 us
  waiting for transfers between devices: 229 us -> 151 us
  local copies, waits for them, and re-layouts: 7.8 us -> 25 us
  starting transfers between devices: 89.7 us -> 100 us
    pallas_call x120 -> x45, Pallas kernels: 305 us -> 88.4 us  [the longest x25 66.5 us: step_call(): pl.pallas_call(functools.partial(step_kernel, count, features, bool(updat...]
    ppermute x82 -> x42, waiting for transfers between devices: 210 us -> 137 us  [the longest x20 111 us: local(): over_z = lambda value: lax.ppermute(value, 'rep', along_z)]
    unnamed x208 -> x25, local copies, waits for them, and re-layouts: 2.95 us -> 23.5 us
    pallas_call x1, Pallas kernels: 22.5 us -> 11.1 us  [forward(): pl.pallas_call(functools.partial(forward_kernel, count), grid=(rows // bl...]
    ppermute x82 -> x42, starting transfers between devices: 82.9 us -> 93.1 us  [the longest x20 45 us: local(): over_z = lambda value: lax.ppermute(value, 'rep', along_z)]
  transfers between devices with their start and end apart: 91 -> 51, of which waited for: 55 -> 29; matrix products, arithmetic and copies ran while one was open for 2% -> 1% of each run, Pallas kernels for 49% -> 22%
where the time goes in v2:
time: 384 us; the launch traced here: 383 us
  waiting for transfers between devices  151 us (39%)
  Pallas kernels  103 us (27%)
  starting transfers between devices  100 us (26%)
  local copies, waits for them, and re-layouts  25 us (7%)
    ppermute x20, waiting for transfers between devices, local(): over_z = lambda value: lax.ppermute(value, 'rep', along_z)  111 us
    pallas_call x25, Pallas kernels, step_call(): pl.pallas_call(functools.partial(step_kernel, count, features, bool(updat...  66.5 us
    ppermute x20, starting transfers between devices, local(): over_z = lambda value: lax.ppermute(value, 'rep', along_z)  45 us
    ppermute x20, starting transfers between devices, local(): over_y = lambda value: lax.ppermute(value, 'rep', along_y)  43.4 us
    ppermute x20, waiting for transfers between devices, local(): over_y = lambda value: lax.ppermute(value, 'rep', along_y)  26.6 us
    unnamed x25, local copies, waits for them, and re-layouts  23.5 us
    pallas_call x20, Pallas kernels, pair_sum(): pl.pallas_call(pair_kernel, grid=(rows // UNIT,), in_specs=[SMEM_SPEC, pl...  21.9 us
    ppermute x9, waiting for transfers between devices, with_partner(): lax.ppermute(value, 'fsdp', [(i, i ^ distance) for i in range(count)])  13.7 us
  transfers between devices with their start and end apart: 51, of which 29 were waited for; matrix products, arithmetic and copies ran while one was open for 1% of the time, Pallas kernels for 22%

profile of v2, /device:TPU:0, one launch (start us, length us, event | category | flops | bytes accessed | tf_op | source)
XLA Modules:
  0.0 382.9 jit_solution(9037327081430197230)
XLA Ops:
  10.7 7.9 %collective-permute-done.rest_2_ = bf16[128,2560]{1,0:T(8,128)(2,1)S(1)} collective-permute-done((bf16[128,2560]{1,0:T(8,128)(2,1)}, bf16[128,2560]{1,0:T(8,128)(2,1)S(1)}, u32[]{:S(2)}, u32[]{:S(2)}) %collective-permute-start) | collective-permute-done | bytes 655392 | tf_op jit(solution)/shard_map/ppermute | solution.py:371
  29.2 11.1 %shard_map.106 = (f32[1280,512]{1,0:T(8,128)S(1)}, f32[1280,512]{1,0:T(8,128)S(1)}, f32[8,512]{1,0:T(8,128)S(1)}, bf16[512,2560]{1,0:T(8,128)(2,1)S(1)}, f32[8,128]{1,0:T(8,128)S(1)}) custom-call(s32[24]{0:T(128)S(1)} %reshape.10.mix_ref.refs_0_, f32[1]{0:T(128)} %copy.111.push_ref, f32[8,128]{1,0:T(8,128)S(1)} %collective-permute-done.1.low_ref, ...), custom_call_target="tpu_custom_call" | custom-call | flops 6710886400 | bytes 19660800 | tf_op jit(solution)/shard_map/pallas_call | solution.py:156
  53.8 4.7 %copy-done = f32[1,1280,2560]{2,1,0:T(8,128)S(1)} copy-done((f32[1,1280,2560]{2,1,0:T(8,128)S(1)}, f32[1,1280,2560]{2,1,0:T(8,128)}, u32[]{:S(2)}) %copy-start) | copy-done | bytes 13107224
  69.0 10.4 %collective-permute-done.12.other_ref = bf16[2,64,2560]{2,1,0:T(8,128)(2,1)S(1)} collective-permute-done((bf16[2,64,2560]{2,1,0:T(8,128)(2,1)S(1)}, bf16[2,64,2560]{2,1,0:T(8,128)(2,1)S(1)}, u32[]{:S(2)}, u32[]{:S(2)}) %collective-permute-start.12) | collective-permute-done | bytes 655392 | tf_op jit(solution)/shard_map/ppermute | solution.py:397
  82.8 4.7 %copy-done.1 = f32[1,1280,2560]{2,1,0:T(8,128)S(1)} copy-done((f32[1,1280,2560]{2,1,0:T(8,128)S(1)}, f32[1,1280,2560]{2,1,0:T(8,128)}, u32[]{:S(2)}) %copy-start.1) | copy-done | bytes 13107224
  116.2 5.3 %collective-permute-done.17.other_ref = bf16[2,64,2560]{2,1,0:T(8,128)(2,1)S(1)} collective-permute-done((bf16[2,64,2560]{2,1,0:T(8,128)(2,1)S(1)}, bf16[2,64,2560]{2,1,0:T(8,128)(2,1)S(1)}, u32[]{:S(2)}, u32[]{:S(2)}) %collective-permute-start.17) | collective-permute-done | bytes 655392 | tf_op jit(solution)/shard_map/ppermute | solution.py:397
  130.3 5.3 %collective-permute-done.13.other_ref = bf16[2,64,2560]{2,1,0:T(8,128)(2,1)S(1)} collective-permute-done((bf16[2,64,2560]{2,1,0:T(8,128)(2,1)S(1)}, bf16[2,64,2560]{2,1,0:T(8,128)(2,1)S(1)}, u32[]{:S(2)}, u32[]{:S(2)}) %collective-permute-start.13) | collective-permute-done | bytes 655392 | tf_op jit(solution)/shard_map/ppermute | solution.py:397
  144.3 5.3 %collective-permute-done.21.other_ref = bf16[2,64,2560]{2,1,0:T(8,128)(2,1)S(1)} collective-permute-done((bf16[2,64,2560]{2,1,0:T(8,128)(2,1)S(1)}, bf16[2,64,2560]{2,1,0:T(8,128)(2,1)S(1)}, u32[]{:S(2)}, u32[]{:S(2)}) %collective-permute-start.21) | collective-permute-done | bytes 655392 | tf_op jit(solution)/shard_map/ppermute | solution.py:397
  158.4 5.3 %collective-permute-done.22.other_ref = bf16[2,64,2560]{2,1,0:T(8,128)(2,1)S(1)} collective-permute-done((bf16[2,64,2560]{2,1,0:T(8,128)(2,1)S(1)}, bf16[2,64,2560]{2,1,0:T(8,128)(2,1)S(1)}, u32[]{:S(2)}, u32[]{:S(2)}) %collective-permute-start.22) | collective-permute-done | bytes 655392 | tf_op jit(solution)/shard_map/ppermute | solution.py:397
  172.4 5.3 %collective-permute-done.26.other_ref = bf16[2,64,2560]{2,1,0:T(8,128)(2,1)S(1)} collective-permute-done((bf16[2,64,2560]{2,1,0:T(8,128)(2,1)S(1)}, bf16[2,64,2560]{2,1,0:T(8,128)(2,1)S(1)}, u32[]{:S(2)}, u32[]{:S(2)}) %collective-permute-start.26) | collective-permute-done | bytes 655392 | tf_op jit(solution)/shard_map/ppermute | solution.py:397
  186.5 5.3 %collective-permute-done.27.other_ref = bf16[2,64,2560]{2,1,0:T(8,128)(2,1)S(1)} collective-permute-done((bf16[2,64,2560]{2,1,0:T(8,128)(2,1)S(1)}, bf16[2,64,2560]{2,1,0:T(8,128)(2,1)S(1)}, u32[]{:S(2)}, u32[]{:S(2)}) %collective-permute-start.27) | collective-permute-done | bytes 655392 | tf_op jit(solution)/shard_map/ppermute | solution.py:397
  200.5 5.3 %collective-permute-done.23.other_ref = bf16[2,64,2560]{2,1,0:T(8,128)(2,1)S(1)} collective-permute-done((bf16[2,64,2560]{2,1,0:T(8,128)(2,1)S(1)}, bf16[2,64,2560]{2,1,0:T(8,128)(2,1)S(1)}, u32[]{:S(2)}, u32[]{:S(2)}) %collective-permute-start.23) | collective-permute-done | bytes 655392 | tf_op jit(solution)/shard_map/ppermute | solution.py:397
  214.5 5.3 %collective-permute-done.31.other_ref = bf16[2,64,2560]{2,1,0:T(8,128)(2,1)S(1)} collective-permute-done((bf16[2,64,2560]{2,1,0:T(8,128)(2,1)S(1)}, bf16[2,64,2560]{2,1,0:T(8,128)(2,1)S(1)}, u32[]{:S(2)}, u32[]{:S(2)}) %collective-permute-start.31) | collective-permute-done | bytes 655392 | tf_op jit(solution)/shard_map/ppermute | solution.py:397
  228.6 5.3 %collective-permute-done.32.other_ref = bf16[2,64,2560]{2,1,0:T(8,128)(2,1)S(1)} collective-permute-done((bf16[2,64,2560]{2,1,0:T(8,128)(2,1)S(1)}, bf16[2,64,2560]{2,1,0:T(8,128)(2,1)S(1)}, u32[]{:S(2)}, u32[]{:S(2)}) %collective-permute-start.32) | collective-permute-done | bytes 655392 | tf_op jit(solution)/shard_map/ppermute | solution.py:397
  242.6 5.3 %collective-permute-done.36.other_ref = bf16[2,64,2560]{2,1,0:T(8,128)(2,1)S(1)} collective-permute-done((bf16[2,64,2560]{2,1,0:T(8,128)(2,1)S(1)}, bf16[2,64,2560]{2,1,0:T(8,128)(2,1)S(1)}, u32[]{:S(2)}, u32[]{:S(2)}) %collective-permute-start.36) | collective-permute-done | bytes 655392 | tf_op jit(solution)/shard_map/ppermute | solution.py:397
  256.7 5.3 %collective-permute-done.37.other_ref = bf16[2,64,2560]{2,1,0:T(8,128)(2,1)S(1)} collective-permute-done((bf16[2,64,2560]{2,1,0:T(8,128)(2,1)S(1)}, bf16[2,64,2560]{2,1,0:T(8,128)(2,1)S(1)}, u32[]{:S(2)}, u32[]{:S(2)}) %collective-permute-start.37) | collective-permute-done | bytes 655392 | tf_op jit(solution)/shard_map/ppermute | solution.py:397
  270.7 5.3 %collective-permute-done.33.other_ref = bf16[2,64,2560]{2,1,0:T(8,128)(2,1)S(1)} collective-permute-done((bf16[2,64,2560]{2,1,0:T(8,128)(2,1)S(1)}, bf16[2,64,2560]{2,1,0:T(8,128)(2,1)S(1)}, u32[]{:S(2)}, u32[]{:S(2)}) %collective-permute-start.33) | collective-permute-done | bytes 655392 | tf_op jit(solution)/shard_map/ppermute | solution.py:397
  284.8 5.3 %collective-permute-done.41.other_ref = bf16[2,64,2560]{2,1,0:T(8,128)(2,1)S(1)} collective-permute-done((bf16[2,64,2560]{2,1,0:T(8,128)(2,1)S(1)}, bf16[2,64,2560]{2,1,0:T(8,128)(2,1)S(1)}, u32[]{:S(2)}, u32[]{:S(2)}) %collective-permute-start.41) | collective-permute-done | bytes 655392 | tf_op jit(solution)/shard_map/ppermute | solution.py:397
  298.7 5.4 %collective-permute-done.42.other_ref = bf16[2,64,2560]{2,1,0:T(8,128)(2,1)S(1)} collective-permute-done((bf16[2,64,2560]{2,1,0:T(8,128)(2,1)S(1)}, bf16[2,64,2560]{2,1,0:T(8,128)(2,1)S(1)}, u32[]{:S(2)}, u32[]{:S(2)}) %collective-permute-start.42) | collective-permute-done | bytes 655392 | tf_op jit(solution)/shard_map/ppermute | solution.py:397
  321.5 10.6 %collective-permute-done.44.other_ref = bf16[2,64,2560]{2,1,0:T(8,128)(2,1)S(1)} collective-permute-done((bf16[2,64,2560]{2,1,0:T(8,128)(2,1)S(1)}, bf16[2,64,2560]{2,1,0:T(8,128)(2,1)S(1)}, u32[]{:S(2)}, u32[]{:S(2)}) %collective-permute-start.44) | collective-permute-done | bytes 655392 | tf_op jit(solution)/shard_map/ppermute | solution.py:397
  335.6 8.6 %collective-permute-done.43.other_ref = bf16[2,64,2560]{2,1,0:T(8,128)(2,1)S(1)} collective-permute-done((bf16[2,64,2560]{2,1,0:T(8,128)(2,1)S(1)}, bf16[2,64,2560]{2,1,0:T(8,128)(2,1)S(1)}, u32[]{:S(2)}, u32[]{:S(2)}) %collective-permute-start.43) | collective-permute-done | bytes 655392 | tf_op jit(solution)/shard_map/ppermute | solution.py:397
  351.4 7.2 %collective-permute-done.48.refs_3_ = bf16[2,64,2560]{2,1,0:T(8,128)(2,1)S(1)} collective-permute-done((bf16[2,64,2560]{2,1,0:T(8,128)(2,1)S(1)}, bf16[2,64,2560]{2,1,0:T(8,128)(2,1)S(1)}, u32[]{:S(2)}, u32[]{:S(2)}) %collective-permute-start.48) | collective-permute-done | bytes 655392 | tf_op jit(solution)/shard_map/ppermute | solution.py:398
  360.2 12.4 %collective-permute-done.47.refs_3_ = bf16[2,64,2560]{2,1,0:T(8,128)(2,1)S(1)} collective-permute-done((bf16[2,64,2560]{2,1,0:T(8,128)(2,1)S(1)}, bf16[2,64,2560]{2,1,0:T(8,128)(2,1)S(1)}, u32[]{:S(2)}, u32[]{:S(2)}) %collective-permute-start.47) | collective-permute-done | bytes 655392 | tf_op jit(solution)/shard_map/ppermute | solution.py:398
  374.2 7.0 %collective-permute-done.46.refs_3_ = bf16[2,64,2560]{2,1,0:T(8,128)(2,1)S(1)} collective-permute-done((bf16[2,64,2560]{2,1,0:T(8,128)(2,1)S(1)}, bf16[2,64,2560]{2,1,0:T(8,128)(2,1)S(1)}, u32[]{:S(2)}, u32[]{:S(2)}) %collective-permute-start.46) | collective-permute-done | bytes 655392 | tf_op jit(solution)/shard_map/ppermute | solution.py:398
  (157 shorter events, 222.7 us)
Async XLA Ops:
  68.5 39.0 %collective-permute-start.16 = (bf16[2,64,2560]{2,1,0:T(8,128)(2,1)S(1)}, bf16[2,64,2560]{2,1,0:T(8,128)(2,1)S(1)}, u32[]{:S(2)}, u32[]{:S(2)}) collective-permute-start(bf16[2,64,2560]{2,1,0:T(8,128)(2,1)S(1)} %get-tuple-element.116.rest_0_.state_ref.refs_13_), channel_id=1, source_target_pairs={{0,24},{4,12},{8,0},{12,20},{16,8},{20,28},{24,16},{28,4},{1,25},{... | collective-permute-start | bytes 1966088 | tf_op jit(solution)/shard_map/ppermute | solution.py:397
  80.5 30.4 %collective-permute-start.15 = (bf16[2,64,2560]{2,1,0:T(8,128)(2,1)S(1)}, bf16[2,64,2560]{2,1,0:T(8,128)(2,1)S(1)}, u32[]{:S(2)}, u32[]{:S(2)}) collective-permute-start(bf16[2,64,2560]{2,1,0:T(8,128)(2,1)S(1)} %shard_map.111.refs_12_), channel_id=1, source_target_pairs={{0,4},{4,0},{8,12},{12,8},{16,20},{20,16},{24,28},{28,24},{1,5},{5... | collective-permute-start | bytes 1966088 | tf_op jit(solution)/shard_map/ppermute | solution.py:398
  89.4 32.1 %collective-permute-start.17 = (bf16[2,64,2560]{2,1,0:T(8,128)(2,1)S(1)}, bf16[2,64,2560]{2,1,0:T(8,128)(2,1)S(1)}, u32[]{:S(2)}, u32[]{:S(2)}) collective-permute-start(bf16[2,64,2560]{2,1,0:T(8,128)(2,1)S(1)} %get-tuple-element.117.rest_0_.state_ref.refs_13_), channel_id=1, source_target_pairs={{0,24},{4,12},{8,0},{12,20},{16,8},{20,28},{24,16},{28,4},{1,25},{... | collective-permute-start | bytes 1966088 | tf_op jit(solution)/shard_map/ppermute | solution.py:397
  103.4 32.1 %collective-permute-start.13 = (bf16[2,64,2560]{2,1,0:T(8,128)(2,1)S(1)}, bf16[2,64,2560]{2,1,0:T(8,128)(2,1)S(1)}, u32[]{:S(2)}, u32[]{:S(2)}) collective-permute-start(bf16[2,64,2560]{2,1,0:T(8,128)(2,1)S(1)} %get-tuple-element.119.rest_0_.state_ref.refs_13_), channel_id=1, source_target_pairs={{0,24},{4,12},{8,0},{12,20},{16,8},{20,28},{24,16},{28,4},{1,25},{... | collective-permute-start | bytes 1966088 | tf_op jit(solution)/shard_map/ppermute | solution.py:397
  114.1 35.5 %collective-permute-start.21 = (bf16[2,64,2560]{2,1,0:T(8,128)(2,1)S(1)}, bf16[2,64,2560]{2,1,0:T(8,128)(2,1)S(1)}, u32[]{:S(2)}, u32[]{:S(2)}) collective-permute-start(bf16[2,64,2560]{2,1,0:T(8,128)(2,1)S(1)} %get-tuple-element.124.rest_0_.state_ref.refs_13_), channel_id=1, source_target_pairs={{0,24},{4,12},{8,0},{12,20},{16,8},{20,28},{24,16},{28,4},{1,25},{... | collective-permute-start | bytes 1966088 | tf_op jit(solution)/shard_map/ppermute | solution.py:397
  128.2 35.5 %collective-permute-start.22 = (bf16[2,64,2560]{2,1,0:T(8,128)(2,1)S(1)}, bf16[2,64,2560]{2,1,0:T(8,128)(2,1)S(1)}, u32[]{:S(2)}, u32[]{:S(2)}) collective-permute-start(bf16[2,64,2560]{2,1,0:T(8,128)(2,1)S(1)} %get-tuple-element.125.rest_0_.state_ref.refs_13_), channel_id=1, source_target_pairs={{0,24},{4,12},{8,0},{12,20},{16,8},{20,28},{24,16},{28,4},{1,25},{... | collective-permute-start | bytes 1966088 | tf_op jit(solution)/shard_map/ppermute | solution.py:397
  142.2 35.5 %collective-permute-start.26 = (bf16[2,64,2560]{2,1,0:T(8,128)(2,1)S(1)}, bf16[2,64,2560]{2,1,0:T(8,128)(2,1)S(1)}, u32[]{:S(2)}, u32[]{:S(2)}) collective-permute-start(bf16[2,64,2560]{2,1,0:T(8,128)(2,1)S(1)} %get-tuple-element.131.rest_0_.state_ref.refs_13_), channel_id=1, source_target_pairs={{0,24},{4,12},{8,0},{12,20},{16,8},{20,28},{24,16},{28,4},{1,25},{... | collective-permute-start | bytes 1966088 | tf_op jit(solution)/shard_map/ppermute | solution.py:397
  156.3 35.5 %collective-permute-start.27 = (bf16[2,64,2560]{2,1,0:T(8,128)(2,1)S(1)}, bf16[2,64,2560]{2,1,0:T(8,128)(2,1)S(1)}, u32[]{:S(2)}, u32[]{:S(2)}) collective-permute-start(bf16[2,64,2560]{2,1,0:T(8,128)(2,1)S(1)} %get-tuple-element.135.rest_0_.state_ref.refs_13_), channel_id=1, source_target_pairs={{0,24},{4,12},{8,0},{12,20},{16,8},{20,28},{24,16},{28,4},{1,25},{... | collective-permute-start | bytes 1966088 | tf_op jit(solution)/shard_map/ppermute | solution.py:397
  170.3 35.5 %collective-permute-start.23 = (bf16[2,64,2560]{2,1,0:T(8,128)(2,1)S(1)}, bf16[2,64,2560]{2,1,0:T(8,128)(2,1)S(1)}, u32[]{:S(2)}, u32[]{:S(2)}) collective-permute-start(bf16[2,64,2560]{2,1,0:T(8,128)(2,1)S(1)} %get-tuple-element.137.rest_0_.state_ref.refs_13_), channel_id=1, source_target_pairs={{0,24},{4,12},{8,0},{12,20},{16,8},{20,28},{24,16},{28,4},{1,25},{... | collective-permute-start | bytes 1966088 | tf_op jit(solution)/shard_map/ppermute | solution.py:397
  184.3 35.5 %collective-permute-start.31 = (bf16[2,64,2560]{2,1,0:T(8,128)(2,1)S(1)}, bf16[2,64,2560]{2,1,0:T(8,128)(2,1)S(1)}, u32[]{:S(2)}, u32[]{:S(2)}) collective-permute-start(bf16[2,64,2560]{2,1,0:T(8,128)(2,1)S(1)} %get-tuple-element.144.rest_0_.state_ref.refs_13_), channel_id=1, source_target_pairs={{0,24},{4,12},{8,0},{12,20},{16,8},{20,28},{24,16},{28,4},{1,25},{... | collective-permute-start | bytes 1966088 | tf_op jit(solution)/shard_map/ppermute | solution.py:397
  198.4 35.5 %collective-permute-start.32 = (bf16[2,64,2560]{2,1,0:T(8,128)(2,1)S(1)}, bf16[2,64,2560]{2,1,0:T(8,128)(2,1)S(1)}, u32[]{:S(2)}, u32[]{:S(2)}) collective-permute-start(bf16[2,64,2560]{2,1,0:T(8,128)(2,1)S(1)} %get-tuple-element.145.rest_0_.state_ref.refs_13_), channel_id=1, source_target_pairs={{0,24},{4,12},{8,0},{12,20},{16,8},{20,28},{24,16},{28,4},{1,25},{... | collective-permute-start | bytes 1966088 | tf_op jit(solution)/shard_map/ppermute | solution.py:397
  212.4 35.5 %collective-permute-start.36 = (bf16[2,64,2560]{2,1,0:T(8,128)(2,1)S(1)}, bf16[2,64,2560]{2,1,0:T(8,128)(2,1)S(1)}, u32[]{:S(2)}, u32[]{:S(2)}) collective-permute-start(bf16[2,64,2560]{2,1,0:T(8,128)(2,1)S(1)} %get-tuple-element.151.rest_0_.state_ref.refs_13_), channel_id=1, source_target_pairs={{0,24},{4,12},{8,0},{12,20},{16,8},{20,28},{24,16},{28,4},{1,25},{... | collective-permute-start | bytes 1966088 | tf_op jit(solution)/shard_map/ppermute | solution.py:397
  226.5 35.5 %collective-permute-start.37 = (bf16[2,64,2560]{2,1,0:T(8,128)(2,1)S(1)}, bf16[2,64,2560]{2,1,0:T(8,128)(2,1)S(1)}, u32[]{:S(2)}, u32[]{:S(2)}) collective-permute-start(bf16[2,64,2560]{2,1,0:T(8,128)(2,1)S(1)} %get-tuple-element.155.rest_0_.state_ref.refs_13_), channel_id=1, source_target_pairs={{0,24},{4,12},{8,0},{12,20},{16,8},{20,28},{24,16},{28,4},{1,25},{... | collective-permute-start | bytes 1966088 | tf_op jit(solution)/shard_map/ppermute | solution.py:397
  240.5 35.5 %collective-permute-start.33 = (bf16[2,64,2560]{2,1,0:T(8,128)(2,1)S(1)}, bf16[2,64,2560]{2,1,0:T(8,128)(2,1)S(1)}, u32[]{:S(2)}, u32[]{:S(2)}) collective-permute-start(bf16[2,64,2560]{2,1,0:T(8,128)(2,1)S(1)} %get-tuple-element.157.rest_0_.state_ref.refs_13_), channel_id=1, source_target_pairs={{0,24},{4,12},{8,0},{12,20},{16,8},{20,28},{24,16},{28,4},{1,25},{... | collective-permute-start | bytes 1966088 | tf_op jit(solution)/shard_map/ppermute | solution.py:397
  254.6 35.5 %collective-permute-start.41 = (bf16[2,64,2560]{2,1,0:T(8,128)(2,1)S(1)}, bf16[2,64,2560]{2,1,0:T(8,128)(2,1)S(1)}, u32[]{:S(2)}, u32[]{:S(2)}) collective-permute-start(bf16[2,64,2560]{2,1,0:T(8,128)(2,1)S(1)} %get-tuple-element.164.rest_0_.state_ref.refs_2_), channel_id=1, source_target_pairs={{0,24},{4,12},{8,0},{12,20},{16,8},{20,28},{24,16},{28,4},{1,25},{... | collective-permute-start | bytes 1966088 | tf_op jit(solution)/shard_map/ppermute | solution.py:397
  268.6 35.5 %collective-permute-start.42 = (bf16[2,64,2560]{2,1,0:T(8,128)(2,1)S(1)}, bf16[2,64,2560]{2,1,0:T(8,128)(2,1)S(1)}, u32[]{:S(2)}, u32[]{:S(2)}) collective-permute-start(bf16[2,64,2560]{2,1,0:T(8,128)(2,1)S(1)} %get-tuple-element.165.rest_0_.state_ref.refs_2_), channel_id=1, source_target_pairs={{0,24},{4,12},{8,0},{12,20},{16,8},{20,28},{24,16},{28,4},{1,25},{... | collective-permute-start | bytes 1966088 | tf_op jit(solution)/shard_map/ppermute | solution.py:397
  282.7 35.5 %collective-permute-start.45 = (bf16[2,64,2560]{2,1,0:T(8,128)(2,1)S(1)}, bf16[2,64,2560]{2,1,0:T(8,128)(2,1)S(1)}, u32[]{:S(2)}, u32[]{:S(2)}) collective-permute-start(bf16[2,64,2560]{2,1,0:T(8,128)(2,1)S(1)} %get-tuple-element.171.rest_0_.state_ref.refs_2_), channel_id=1, source_target_pairs={{0,24},{4,12},{8,0},{12,20},{16,8},{20,28},{24,16},{28,4},{1,25},{... | collective-permute-start | bytes 1966088 | tf_op jit(solution)/shard_map/ppermute | solution.py:397
  294.4 37.7 %collective-permute-start.44 = (bf16[2,64,2560]{2,1,0:T(8,128)(2,1)S(1)}, bf16[2,64,2560]{2,1,0:T(8,128)(2,1)S(1)}, u32[]{:S(2)}, u32[]{:S(2)}) collective-permute-start(bf16[2,64,2560]{2,1,0:T(8,128)(2,1)S(1)} %get-tuple-element.175.rest_0_.state_ref.refs_2_), channel_id=1, source_target_pairs={{0,24},{4,12},{8,0},{12,20},{16,8},{20,28},{24,16},{28,4},{1,25},{... | collective-permute-start | bytes 1966088 | tf_op jit(solution)/shard_map/ppermute | solution.py:397
  308.5 35.6 %collective-permute-start.43 = (bf16[2,64,2560]{2,1,0:T(8,128)(2,1)S(1)}, bf16[2,64,2560]{2,1,0:T(8,128)(2,1)S(1)}, u32[]{:S(2)}, u32[]{:S(2)}) collective-permute-start(bf16[2,64,2560]{2,1,0:T(8,128)(2,1)S(1)} %get-tuple-element.177.rest_0_.state_ref.refs_2_), channel_id=1, source_target_pairs={{0,24},{4,12},{8,0},{12,20},{16,8},{20,28},{24,16},{28,4},{1,25},{... | collective-permute-start | bytes 1966088 | tf_op jit(solution)/shard_map/ppermute | solution.py:397
  312.8 35.3 %collective-permute-start.50 = (bf16[2,64,2560]{2,1,0:T(8,128)(2,1)S(1)}, bf16[2,64,2560]{2,1,0:T(8,128)(2,1)S(1)}, u32[]{:S(2)}, u32[]{:S(2)}) collective-permute-start(bf16[2,64,2560]{2,1,0:T(8,128)(2,1)S(1)} %shard_map.141.refs_17_), channel_id=1, source_target_pairs={{0,4},{4,0},{8,12},{12,8},{16,20},{20,16},{24,28},{28,24},{1,5},{5... | collective-permute-start | bytes 1966088 | tf_op jit(solution)/shard_map/ppermute | solution.py:398
  312.8 36.9 %collective-permute-start.49 = (bf16[2,64,2560]{2,1,0:T(8,128)(2,1)S(1)}, bf16[2,64,2560]{2,1,0:T(8,128)(2,1)S(1)}, u32[]{:S(2)}, u32[]{:S(2)}) collective-permute-start(bf16[2,64,2560]{2,1,0:T(8,128)(2,1)S(1)} %shard_map.143.refs_17_), channel_id=1, source_target_pairs={{0,4},{4,0},{8,12},{12,8},{16,20},{20,16},{24,28},{28,24},{1,5},{5... | collective-permute-start | bytes 1966088 | tf_op jit(solution)/shard_map/ppermute | solution.py:398
  319.2 39.3 %collective-permute-start.48 = (bf16[2,64,2560]{2,1,0:T(8,128)(2,1)S(1)}, bf16[2,64,2560]{2,1,0:T(8,128)(2,1)S(1)}, u32[]{:S(2)}, u32[]{:S(2)}) collective-permute-start(bf16[2,64,2560]{2,1,0:T(8,128)(2,1)S(1)} %shard_map.145.rest_0_.refs_6_), channel_id=1, source_target_pairs={{0,4},{4,0},{8,12},{12,8},{16,20},{20,16},{24,28},{28,24},{1,5},{5... | collective-permute-start | bytes 1966088 | tf_op jit(solution)/shard_map/ppermute | solution.py:398
  333.3 39.3 %collective-permute-start.47 = (bf16[2,64,2560]{2,1,0:T(8,128)(2,1)S(1)}, bf16[2,64,2560]{2,1,0:T(8,128)(2,1)S(1)}, u32[]{:S(2)}, u32[]{:S(2)}) collective-permute-start(bf16[2,64,2560]{2,1,0:T(8,128)(2,1)S(1)} %shard_map.146.rest_0_.refs_6_), channel_id=1, source_target_pairs={{0,4},{4,0},{8,12},{12,8},{16,20},{20,16},{24,28},{28,24},{1,5},{5... | collective-permute-start | bytes 1966088 | tf_op jit(solution)/shard_map/ppermute | solution.py:398
  345.2 36.0 %collective-permute-start.46 = (bf16[2,64,2560]{2,1,0:T(8,128)(2,1)S(1)}, bf16[2,64,2560]{2,1,0:T(8,128)(2,1)S(1)}, u32[]{:S(2)}, u32[]{:S(2)}) collective-permute-start(bf16[2,64,2560]{2,1,0:T(8,128)(2,1)S(1)} %shard_map.147.refs_6_), channel_id=1, source_target_pairs={{0,4},{4,0},{8,12},{12,8},{16,20},{20,16},{24,28},{28,24},{1,5},{5... | collective-permute-start | bytes 1966088 | tf_op jit(solution)/shard_map/ppermute | solution.py:398
  (39 other events, 584.5 us)

commit v3 on v2

--- a/solution.py
+++ b/solution.py
@@ -12,9 +12,9 @@
 beta_decay = 0.9
 
 UNIT = 32
-CHUNK = 64
-Z_AHEAD = 3
-Y_AHEAD = 2
+CHUNKS = ((64, 1),)
+Z_AHEAD = 2
+Y_AHEAD = 1
 MIB = 1024 * 1024
 FORWARD_ROWS = 256
 FORWARD_MIB = SECOND_MIB = STEP_MIB = PAIR_MIB = 24
@@ -121,14 +121,38 @@
         out_ref[:, j * width : (j + 1) * width] = piece[...].T
 
 
-def forward_kernel(count, mix_ref, push_ref, low_ref, high_ref, p_ref, m_ref, r_ref, t_ref, g_ref, *rest):
+def near_kernel(count, *refs):
+    transpose_pieces(refs[:count], refs[-1])
+
+
+def near_turned(pieces, mix, beside):
+    piece, width = pieces[0].shape
+    tokens = piece * len(pieces)
+    return pl.pallas_call(
+        functools.partial(near_kernel, len(pieces)),
+        grid=(1,),
+        in_specs=[whole_spec((piece, width))] * len(pieces)
+        + [SMEM_SPEC]
+        + [pl.BlockSpec(memory_space=pl.ANY)] * len(beside),
+        out_specs=whole_spec((width, tokens)),
+        out_shape=jax.ShapeDtypeStruct((width, tokens), BF16),
+        compiler_params=params_of(FORWARD_MIB * MIB),
+        cost_estimate=cost(2 * tokens * width, 4 * tokens * width),
+    )(*pieces, mix, *beside)
+
+
+def forward_kernel(
+    count, mix_ref, push_ref, low_ref, high_ref, p_ref, m_ref, r_ref, t_ref, g_ref, near_ref, *rest
+):
     pieces, (s_ref, y_ref, q_ref, c_ref, push_out, ct_ref) = rest[:count], rest[count:]
     index = lax.axis_index("fsdp")
     step = pl.program_id(0)
 
     @pl.when(step == 0)
     def _():
-        transpose_pieces(pieces, ct_ref)
+        half = near_ref.shape[1]
+        ct_ref[:, :half] = near_ref[...]
+        transpose_pieces(pieces[count // 2 :], ct_ref.at[:, half:])
         width = pieces[0].shape[0]
         for j, piece in enumerate(pieces):
             c_ref[j * width : (j + 1) * width, :] = piece[...]
@@ -146,7 +170,7 @@
     add_sums(q_ref, step, total, g_ref[...] * total, target)
 
 
-def forward(mix, push, lower, upper, params, moment, residual, target, gain, pieces):
+def forward(mix, push, lower, upper, params, moment, residual, target, gain, near, pieces):
     rows, width = params.shape
     piece = pieces[0].shape[0]
     count = len(pieces)
@@ -166,6 +190,7 @@
             row(tokens),
             row(tokens),
             row(1),
+            whole_spec((width, tokens // 2)),
         ]
         + [whole_spec((piece, width))] * count,
         out_specs=[
@@ -185,7 +210,7 @@
         scratch_shapes=[pltpu.VMEM((width, tokens), BF16)],
         compiler_params=params_of(FORWARD_MIB * MIB if tokens <= 512 else 58 * MIB),
         cost_estimate=cost(4 * rows * width * tokens, rows * width * 6),
-    )(mix, push, lower, upper, params, moment, residual, target, gain, *pieces)
+    )(mix, push, lower, upper, params, moment, residual, target, gain, near, *pieces)
 
 
 def second_kernel(count, features, push_ref, s_ref, t_ref, g_ref, y_ref, gram_ref, *rest):
@@ -385,6 +410,16 @@
     return [sums] + [with_partner(sums, m, count) for m in range(1, count)]
 
 
+def chunk_sizes(rows):
+    sizes = []
+    for size, part in CHUNKS:
+        while sum(sizes) + size <= min(part * rows, rows):
+            sizes.append(size)
+    while sum(sizes) < rows:
+        sizes.append(UNIT)
+    return sizes
+
+
 def local(context, residual, target, norm_gain, params, momentum, push_weight, mix_num):
     count = lax.axis_size("fsdp")
     replicas = lax.axis_size("rep")
@@ -404,9 +439,8 @@
     push_upper = lax.ppermute(push_row, "rep", [(r, (r - 1) % replicas) for r in range(replicas)])
     gain = norm_gain[:, None]
     mix = mix_num.reshape(-1)
-    far, gain, push_lower, push_upper, mix, *near_pieces = lax.optimization_barrier(
-        (far, gain, push_lower, push_upper, mix, *near_pieces)
-    )
+    near = near_turned(near_pieces, mix, (gain, push_lower, push_upper, momentum, residual, target))
+    far, near = lax.optimization_barrier((far, near))
     pieces = near_pieces + gather_low(far, count)
     total, moment_product, sums, tokens_all, new_push = forward(
         mix,
@@ -418,6 +452,7 @@
         residual,
         target,
         gain,
+        near,
         pieces,
     )
     sums = all_sums(sums, count)
@@ -428,8 +463,9 @@
     sums = all_sums(sums, count)
 
     arrays = (params, momentum, grad, total, target, gain, tokens_all)
-    chunk = CHUNK if rows % CHUNK == 0 else UNIT
-    chunks = rows // chunk
+    sizes = chunk_sizes(rows)
+    chunks = len(sizes)
+    starts = [sum(sizes[:c]) for c in range(chunks)]
     made, crossing, arriving = {}, {}, {}
     held = None
     last = ()
@@ -440,13 +476,18 @@
             arriving[c] = over_y(both)
             last = (both,)
         ahead, behind = c + Z_AHEAD, c - Y_AHEAD
-        update = (ahead * chunk, arrays, sums) if ahead < chunks else None
+        update = (starts[ahead], arrays, sums) if ahead < chunks else None
         done = None
         if behind >= 0:
             state, master = made.pop(behind)
-            done = (behind * chunk, rows, master, state, arriving.pop(behind))
-        if update or done:
-            out, held = step_call(mix, chunk, update, done, held, last, features)
+            done = (starts[behind], rows, master, state, arriving.pop(behind))
+        if update and done and sizes[ahead] == sizes[behind]:
+            calls = [(sizes[ahead], update, done)]
+        else:
+            calls = [(sizes[ahead], update, None)] if update else []
+            calls += [(sizes[behind], None, done)] if done else []
+        for size, update, done in calls:
+            out, held = step_call(mix, size, update, done, held, last, features)
             if out:
                 made[ahead] = out
                 crossing[ahead] = over_z(out[0])

time: 384 us -> 362 us (0.943)
  local copies, waits for them, and re-layouts: 25 us -> 13.6 us
  waiting for transfers between devices: 151 us -> 140 us
    unnamed x25 -> x17, local copies, waits for them, and re-layouts: 23.5 us -> 12.1 us
    ppermute x20, waiting for transfers between devices: 26.6 us -> 15.9 us  [local(): over_y = lambda value: lax.ppermute(value, 'rep', along_y)]
    ppermute x20, waiting for transfers between devices: 111 us -> 118 us  [local(): over_z = lambda value: lax.ppermute(value, 'rep', along_z)]
    ppermute x9, waiting for transfers between devices: 13.7 us -> 6.78 us  [with_partner(): lax.ppermute(value, 'fsdp', [(i, i ^ distance) for i in range(count)])]
    pallas_call x25 -> x23, Pallas kernels: 66.5 us -> 66 us  [step_call(): pl.pallas_call(functools.partial(step_kernel, count, features, bool(updat...]
  transfers between devices with their start and end apart: 51 -> 51, of which waited for: 29 -> 28; matrix products, arithmetic and copies ran while one was open for 1% -> 1% of each run, Pallas kernels for 22% -> 24%
where the time goes in v3:
time: 362 us; the launch traced here: 361 us
  waiting for transfers between devices  140 us (39%)
  Pallas kernels  104 us (29%)
  starting transfers between devices  100 us (28%)
  local copies, waits for them, and re-layouts  13.6 us (4%)
    ppermute x20, waiting for transfers between devices, local(): over_z = lambda value: lax.ppermute(value, 'rep', along_z)  118 us
    pallas_call x23, Pallas kernels, step_call(): pl.pallas_call(functools.partial(step_kernel, count, features, bool(updat...  66 us
    ppermute x20, starting transfers between devices, local(): over_z = lambda value: lax.ppermute(value, 'rep', along_z)  44.8 us
    ppermute x20, starting transfers between devices, local(): over_y = lambda value: lax.ppermute(value, 'rep', along_y)  43.3 us
    pallas_call x20, Pallas kernels, pair_sum(): pl.pallas_call(pair_kernel, grid=(rows // UNIT,), in_specs=[SMEM_SPEC, pl...  21.9 us
    ppermute x20, waiting for transfers between devices, local(): over_y = lambda value: lax.ppermute(value, 'rep', along_y)  15.9 us
    unnamed x17, local copies, waits for them, and re-layouts  12.1 us
    pallas_call x1, Pallas kernels, forward(): pl.pallas_call(functools.partial(forward_kernel, count), grid=(rows // bl...  10.8 us
  transfers between devices with their start and end apart: 51, of which 28 were waited for; matrix products, arithmetic and copies ran while one was open for 1% of the time, Pallas kernels for 24%

profile of v3, /device:TPU:0, one launch (start us, length us, event | category | flops | bytes accessed | tf_op | source)
XLA Modules:
  0.0 360.8 jit_solution(1917184309645213397)
XLA Ops:
  21.3 10.8 %shard_map.107 = (f32[1280,512]{1,0:T(8,128)S(1)}, f32[1280,512]{1,0:T(8,128)S(1)}, f32[8,512]{1,0:T(8,128)S(1)}, bf16[512,2560]{1,0:T(8,128)(2,1)S(1)}, f32[8,128]{1,0:T(8,128)S(1)}) custom-call(s32[24]{0:T(128)S(1)} %reshape.10.refs_2_.mix_ref.refs_0_, f32[1]{0:T(128)} %copy.112.push_ref, f32[8,128]{1,0:T(8,128)S(1)} %collective-permute-done.refs_4_.low_ref, ...), custom_call_target="tpu_custom_call" | custom-call | flops 6710886400 | bytes 19660800 | tf_op jit(solution)/shard_map/pallas_call | solution.py:180
  45.7 4.7 %copy-done = f32[1,1280,2560]{2,1,0:T(8,128)S(1)} copy-done((f32[1,1280,2560]{2,1,0:T(8,128)S(1)}, f32[1,1280,2560]{2,1,0:T(8,128)}, u32[]{:S(2)}) %copy-start) | copy-done | bytes 13107224
  58.5 12.8 %collective-permute-done.12.other_ref = bf16[2,64,2560]{2,1,0:T(8,128)(2,1)S(1)} collective-permute-done((bf16[2,64,2560]{2,1,0:T(8,128)(2,1)S(1)}, bf16[2,64,2560]{2,1,0:T(8,128)(2,1)S(1)}, u32[]{:S(2)}, u32[]{:S(2)}) %collective-permute-start.12) | collective-permute-done | bytes 655392 | tf_op jit(solution)/shard_map/ppermute | solution.py:432
  78.7 6.6 %collective-permute-done.11.other_ref = bf16[2,64,2560]{2,1,0:T(8,128)(2,1)S(1)} collective-permute-done((bf16[2,64,2560]{2,1,0:T(8,128)(2,1)S(1)}, bf16[2,64,2560]{2,1,0:T(8,128)(2,1)S(1)}, u32[]{:S(2)}, u32[]{:S(2)}) %collective-permute-start.11) | collective-permute-done | bytes 655392 | tf_op jit(solution)/shard_map/ppermute | solution.py:432
  94.1 5.3 %collective-permute-done.15.other_ref = bf16[2,64,2560]{2,1,0:T(8,128)(2,1)S(1)} collective-permute-done((bf16[2,64,2560]{2,1,0:T(8,128)(2,1)S(1)}, bf16[2,64,2560]{2,1,0:T(8,128)(2,1)S(1)}, u32[]{:S(2)}, u32[]{:S(2)}) %collective-permute-start.15) | collective-permute-done | bytes 655392 | tf_op jit(solution)/shard_map/ppermute | solution.py:432
  108.1 5.3 %collective-permute-done.18.other_ref = bf16[2,64,2560]{2,1,0:T(8,128)(2,1)S(1)} collective-permute-done((bf16[2,64,2560]{2,1,0:T(8,128)(2,1)S(1)}, bf16[2,64,2560]{2,1,0:T(8,128)(2,1)S(1)}, u32[]{:S(2)}, u32[]{:S(2)}) %collective-permute-start.18) | collective-permute-done | bytes 655392 | tf_op jit(solution)/shard_map/ppermute | solution.py:432
  122.2 5.3 %collective-permute-done.16.other_ref = bf16[2,64,2560]{2,1,0:T(8,128)(2,1)S(1)} collective-permute-done((bf16[2,64,2560]{2,1,0:T(8,128)(2,1)S(1)}, bf16[2,64,2560]{2,1,0:T(8,128)(2,1)S(1)}, u32[]{:S(2)}, u32[]{:S(2)}) %collective-permute-start.16) | collective-permute-done | bytes 655392 | tf_op jit(solution)/shard_map/ppermute | solution.py:432
  136.2 5.3 %collective-permute-done.21.other_ref = bf16[2,64,2560]{2,1,0:T(8,128)(2,1)S(1)} collective-permute-done((bf16[2,64,2560]{2,1,0:T(8,128)(2,1)S(1)}, bf16[2,64,2560]{2,1,0:T(8,128)(2,1)S(1)}, u32[]{:S(2)}, u32[]{:S(2)}) %collective-permute-start.21) | collective-permute-done | bytes 655392 | tf_op jit(solution)/shard_map/ppermute | solution.py:432
  150.3 5.3 %collective-permute-done.24.other_ref = bf16[2,64,2560]{2,1,0:T(8,128)(2,1)S(1)} collective-permute-done((bf16[2,64,2560]{2,1,0:T(8,128)(2,1)S(1)}, bf16[2,64,2560]{2,1,0:T(8,128)(2,1)S(1)}, u32[]{:S(2)}, u32[]{:S(2)}) %collective-permute-start.24) | collective-permute-done | bytes 655392 | tf_op jit(solution)/shard_map/ppermute | solution.py:432
  164.3 5.3 %collective-permute-done.22.other_ref = bf16[2,64,2560]{2,1,0:T(8,128)(2,1)S(1)} collective-permute-done((bf16[2,64,2560]{2,1,0:T(8,128)(2,1)S(1)}, bf16[2,64,2560]{2,1,0:T(8,128)(2,1)S(1)}, u32[]{:S(2)}, u32[]{:S(2)}) %collective-permute-start.22) | collective-permute-done | bytes 655392 | tf_op jit(solution)/shard_map/ppermute | solution.py:432
  178.4 5.3 %collective-permute-done.27.other_ref = bf16[2,64,2560]{2,1,0:T(8,128)(2,1)S(1)} collective-permute-done((bf16[2,64,2560]{2,1,0:T(8,128)(2,1)S(1)}, bf16[2,64,2560]{2,1,0:T(8,128)(2,1)S(1)}, u32[]{:S(2)}, u32[]{:S(2)}) %collective-permute-start.27) | collective-permute-done | bytes 655392 | tf_op jit(solution)/shard_map/ppermute | solution.py:432
  192.4 5.3 %collective-permute-done.30.other_ref = bf16[2,64,2560]{2,1,0:T(8,128)(2,1)S(1)} collective-permute-done((bf16[2,64,2560]{2,1,0:T(8,128)(2,1)S(1)}, bf16[2,64,2560]{2,1,0:T(8,128)(2,1)S(1)}, u32[]{:S(2)}, u32[]{:S(2)}) %collective-permute-start.30) | collective-permute-done | bytes 655392 | tf_op jit(solution)/shard_map/ppermute | solution.py:432
  206.5 5.3 %collective-permute-done.28.other_ref = bf16[2,64,2560]{2,1,0:T(8,128)(2,1)S(1)} collective-permute-done((bf16[2,64,2560]{2,1,0:T(8,128)(2,1)S(1)}, bf16[2,64,2560]{2,1,0:T(8,128)(2,1)S(1)}, u32[]{:S(2)}, u32[]{:S(2)}) %collective-permute-start.28) | collective-permute-done | bytes 655392 | tf_op jit(solution)/shard_map/ppermute | solution.py:432
  220.5 5.3 %collective-permute-done.33.other_ref = bf16[2,64,2560]{2,1,0:T(8,128)(2,1)S(1)} collective-permute-done((bf16[2,64,2560]{2,1,0:T(8,128)(2,1)S(1)}, bf16[2,64,2560]{2,1,0:T(8,128)(2,1)S(1)}, u32[]{:S(2)}, u32[]{:S(2)}) %collective-permute-start.33) | collective-permute-done | bytes 655392 | tf_op jit(solution)/shard_map/ppermute | solution.py:432
  234.5 5.3 %collective-permute-done.36.other_ref = bf16[2,64,2560]{2,1,0:T(8,128)(2,1)S(1)} collective-permute-done((bf16[2,64,2560]{2,1,0:T(8,128)(2,1)S(1)}, bf16[2,64,2560]{2,1,0:T(8,128)(2,1)S(1)}, u32[]{:S(2)}, u32[]{:S(2)}) %collective-permute-start.36) | collective-permute-done | bytes 655392 | tf_op jit(solution)/shard_map/ppermute | solution.py:432
  248.6 5.3 %collective-permute-done.34.other_ref = bf16[2,64,2560]{2,1,0:T(8,128)(2,1)S(1)} collective-permute-done((bf16[2,64,2560]{2,1,0:T(8,128)(2,1)S(1)}, bf16[2,64,2560]{2,1,0:T(8,128)(2,1)S(1)}, u32[]{:S(2)}, u32[]{:S(2)}) %collective-permute-start.34) | collective-permute-done | bytes 655392 | tf_op jit(solution)/shard_map/ppermute | solution.py:432
  262.6 5.3 %collective-permute-done.39.other_ref = bf16[2,64,2560]{2,1,0:T(8,128)(2,1)S(1)} collective-permute-done((bf16[2,64,2560]{2,1,0:T(8,128)(2,1)S(1)}, bf16[2,64,2560]{2,1,0:T(8,128)(2,1)S(1)}, u32[]{:S(2)}, u32[]{:S(2)}) %collective-permute-start.39) | collective-permute-done | bytes 655392 | tf_op jit(solution)/shard_map/ppermute | solution.py:432
  276.7 5.3 %collective-permute-done.42.other_ref = bf16[2,64,2560]{2,1,0:T(8,128)(2,1)S(1)} collective-permute-done((bf16[2,64,2560]{2,1,0:T(8,128)(2,1)S(1)}, bf16[2,64,2560]{2,1,0:T(8,128)(2,1)S(1)}, u32[]{:S(2)}, u32[]{:S(2)}) %collective-permute-start.42) | collective-permute-done | bytes 655392 | tf_op jit(solution)/shard_map/ppermute | solution.py:432
  290.7 5.3 %collective-permute-done.40.other_ref = bf16[2,64,2560]{2,1,0:T(8,128)(2,1)S(1)} collective-permute-done((bf16[2,64,2560]{2,1,0:T(8,128)(2,1)S(1)}, bf16[2,64,2560]{2,1,0:T(8,128)(2,1)S(1)}, u32[]{:S(2)}, u32[]{:S(2)}) %collective-permute-start.40) | collective-permute-done | bytes 655392 | tf_op jit(solution)/shard_map/ppermute | solution.py:432
  304.8 5.3 %collective-permute-done.45.other_ref = bf16[2,64,2560]{2,1,0:T(8,128)(2,1)S(1)} collective-permute-done((bf16[2,64,2560]{2,1,0:T(8,128)(2,1)S(1)}, bf16[2,64,2560]{2,1,0:T(8,128)(2,1)S(1)}, u32[]{:S(2)}, u32[]{:S(2)}) %collective-permute-start.45) | collective-permute-done | bytes 655392 | tf_op jit(solution)/shard_map/ppermute | solution.py:432
  318.7 5.3 %collective-permute-done.47.other_ref = bf16[2,64,2560]{2,1,0:T(8,128)(2,1)S(1)} collective-permute-done((bf16[2,64,2560]{2,1,0:T(8,128)(2,1)S(1)}, bf16[2,64,2560]{2,1,0:T(8,128)(2,1)S(1)}, u32[]{:S(2)}, u32[]{:S(2)}) %collective-permute-start.47) | collective-permute-done | bytes 655392 | tf_op jit(solution)/shard_map/ppermute | solution.py:432
  327.5 8.6 %collective-permute-done.46.other_ref = bf16[2,64,2560]{2,1,0:T(8,128)(2,1)S(1)} collective-permute-done((bf16[2,64,2560]{2,1,0:T(8,128)(2,1)S(1)}, bf16[2,64,2560]{2,1,0:T(8,128)(2,1)S(1)}, u32[]{:S(2)}, u32[]{:S(2)}) %collective-permute-start.46) | collective-permute-done | bytes 655392 | tf_op jit(solution)/shard_map/ppermute | solution.py:432
  341.6 8.8 %collective-permute-done.49.refs_3_ = bf16[2,64,2560]{2,1,0:T(8,128)(2,1)S(1)} collective-permute-done((bf16[2,64,2560]{2,1,0:T(8,128)(2,1)S(1)}, bf16[2,64,2560]{2,1,0:T(8,128)(2,1)S(1)}, u32[]{:S(2)}, u32[]{:S(2)}) %collective-permute-start.49) | collective-permute-done | bytes 655392 | tf_op jit(solution)/shard_map/ppermute | solution.py:433
  352.1 7.0 %collective-permute-done.48.refs_3_ = bf16[2,64,2560]{2,1,0:T(8,128)(2,1)S(1)} collective-permute-done((bf16[2,64,2560]{2,1,0:T(8,128)(2,1)S(1)}, bf16[2,64,2560]{2,1,0:T(8,128)(2,1)S(1)}, u32[]{:S(2)}, u32[]{:S(2)}) %collective-permute-start.48) | collective-permute-done | bytes 655392 | tf_op jit(solution)/shard_map/ppermute | solution.py:433
  (147 shorter events, 210.0 us)
Async XLA Ops:
  1.1 18.1 %collective-permute-start.2 = (bf16[128,2560]{1,0:T(8,128)(2,1)}, bf16[128,2560]{1,0:T(8,128)(2,1)S(1)}, u32[]{:S(2)}, u32[]{:S(2)}) collective-permute-start(bf16[128,2560]{1,0:T(8,128)(2,1)} %bitcast.83), channel_id=1, source_target_pairs={{0,2},{1,3},{2,0},{3,1},{4,6},{5,7},{6,4},{7,5},{8,10},{9,11},{10,... | collective-permute-start | bytes 1966088 | tf_op jit(solution)/shard_map/ppermute | solution.py:396
  52.3 19.0 %collective-permute-start.12 = (bf16[2,64,2560]{2,1,0:T(8,128)(2,1)S(1)}, bf16[2,64,2560]{2,1,0:T(8,128)(2,1)S(1)}, u32[]{:S(2)}, u32[]{:S(2)}) collective-permute-start(bf16[2,64,2560]{2,1,0:T(8,128)(2,1)S(1)} %get-tuple-element.102.refs_12_.state_ref.refs_13_), channel_id=1, source_target_pairs={{0,24},{4,12},{8,0},{12,20},{16,8},{20,28},{24,16},{28,4},{1,25},{... | collective-permute-start | bytes 1966088 | tf_op jit(solution)/shard_map/ppermute | solution.py:432
  58.0 27.4 %collective-permute-start.11 = (bf16[2,64,2560]{2,1,0:T(8,128)(2,1)S(1)}, bf16[2,64,2560]{2,1,0:T(8,128)(2,1)S(1)}, u32[]{:S(2)}, u32[]{:S(2)}) collective-permute-start(bf16[2,64,2560]{2,1,0:T(8,128)(2,1)S(1)} %get-tuple-element.104.rest_0_.state_ref.refs_13_), channel_id=1, source_target_pairs={{0,24},{4,12},{8,0},{12,20},{16,8},{20,28},{24,16},{28,4},{1,25},{... | collective-permute-start | bytes 1966088 | tf_op jit(solution)/shard_map/ppermute | solution.py:432
  76.5 22.8 %collective-permute-start.15 = (bf16[2,64,2560]{2,1,0:T(8,128)(2,1)S(1)}, bf16[2,64,2560]{2,1,0:T(8,128)(2,1)S(1)}, u32[]{:S(2)}, u32[]{:S(2)}) collective-permute-start(bf16[2,64,2560]{2,1,0:T(8,128)(2,1)S(1)} %get-tuple-element.106.rest_0_.state_ref.refs_13_), channel_id=1, source_target_pairs={{0,24},{4,12},{8,0},{12,20},{16,8},{20,28},{24,16},{28,4},{1,25},{... | collective-permute-start | bytes 1966088 | tf_op jit(solution)/shard_map/ppermute | solution.py:432
  92.0 21.4 %collective-permute-start.18 = (bf16[2,64,2560]{2,1,0:T(8,128)(2,1)S(1)}, bf16[2,64,2560]{2,1,0:T(8,128)(2,1)S(1)}, u32[]{:S(2)}, u32[]{:S(2)}) collective-permute-start(bf16[2,64,2560]{2,1,0:T(8,128)(2,1)S(1)} %get-tuple-element.110.rest_0_.state_ref.refs_13_), channel_id=1, source_target_pairs={{0,24},{4,12},{8,0},{12,20},{16,8},{20,28},{24,16},{28,4},{1,25},{... | collective-permute-start | bytes 1966088 | tf_op jit(solution)/shard_map/ppermute | solution.py:432
  106.0 21.4 %collective-permute-start.16 = (bf16[2,64,2560]{2,1,0:T(8,128)(2,1)S(1)}, bf16[2,64,2560]{2,1,0:T(8,128)(2,1)S(1)}, u32[]{:S(2)}, u32[]{:S(2)}) collective-permute-start(bf16[2,64,2560]{2,1,0:T(8,128)(2,1)S(1)} %get-tuple-element.112.rest_0_.state_ref.refs_13_), channel_id=1, source_target_pairs={{0,24},{4,12},{8,0},{12,20},{16,8},{20,28},{24,16},{28,4},{1,25},{... | collective-permute-start | bytes 1966088 | tf_op jit(solution)/shard_map/ppermute | solution.py:432
  120.1 21.4 %collective-permute-start.21 = (bf16[2,64,2560]{2,1,0:T(8,128)(2,1)S(1)}, bf16[2,64,2560]{2,1,0:T(8,128)(2,1)S(1)}, u32[]{:S(2)}, u32[]{:S(2)}) collective-permute-start(bf16[2,64,2560]{2,1,0:T(8,128)(2,1)S(1)} %get-tuple-element.116.rest_0_.state_ref.refs_13_), channel_id=1, source_target_pairs={{0,24},{4,12},{8,0},{12,20},{16,8},{20,28},{24,16},{28,4},{1,25},{... | collective-permute-start | bytes 1966088 | tf_op jit(solution)/shard_map/ppermute | solution.py:432
  134.1 21.4 %collective-permute-start.24 = (bf16[2,64,2560]{2,1,0:T(8,128)(2,1)S(1)}, bf16[2,64,2560]{2,1,0:T(8,128)(2,1)S(1)}, u32[]{:S(2)}, u32[]{:S(2)}) collective-permute-start(bf16[2,64,2560]{2,1,0:T(8,128)(2,1)S(1)} %get-tuple-element.122.rest_0_.state_ref.refs_13_), channel_id=1, source_target_pairs={{0,24},{4,12},{8,0},{12,20},{16,8},{20,28},{24,16},{28,4},{1,25},{... | collective-permute-start | bytes 1966088 | tf_op jit(solution)/shard_map/ppermute | solution.py:432
  148.1 21.4 %collective-permute-start.22 = (bf16[2,64,2560]{2,1,0:T(8,128)(2,1)S(1)}, bf16[2,64,2560]{2,1,0:T(8,128)(2,1)S(1)}, u32[]{:S(2)}, u32[]{:S(2)}) collective-permute-start(bf16[2,64,2560]{2,1,0:T(8,128)(2,1)S(1)} %get-tuple-element.124.rest_0_.state_ref.refs_13_), channel_id=1, source_target_pairs={{0,24},{4,12},{8,0},{12,20},{16,8},{20,28},{24,16},{28,4},{1,25},{... | collective-permute-start | bytes 1966088 | tf_op jit(solution)/shard_map/ppermute | solution.py:432
  162.2 21.4 %collective-permute-start.27 = (bf16[2,64,2560]{2,1,0:T(8,128)(2,1)S(1)}, bf16[2,64,2560]{2,1,0:T(8,128)(2,1)S(1)}, u32[]{:S(2)}, u32[]{:S(2)}) collective-permute-start(bf16[2,64,2560]{2,1,0:T(8,128)(2,1)S(1)} %get-tuple-element.128.rest_0_.state_ref.refs_13_), channel_id=1, source_target_pairs={{0,24},{4,12},{8,0},{12,20},{16,8},{20,28},{24,16},{28,4},{1,25},{... | collective-permute-start | bytes 1966088 | tf_op jit(solution)/shard_map/ppermute | solution.py:432
  176.2 21.4 %collective-permute-start.30 = (bf16[2,64,2560]{2,1,0:T(8,128)(2,1)S(1)}, bf16[2,64,2560]{2,1,0:T(8,128)(2,1)S(1)}, u32[]{:S(2)}, u32[]{:S(2)}) collective-permute-start(bf16[2,64,2560]{2,1,0:T(8,128)(2,1)S(1)} %get-tuple-element.134.rest_0_.state_ref.refs_13_), channel_id=1, source_target_pairs={{0,24},{4,12},{8,0},{12,20},{16,8},{20,28},{24,16},{28,4},{1,25},{... | collective-permute-start | bytes 1966088 | tf_op jit(solution)/shard_map/ppermute | solution.py:432
  190.3 21.4 %collective-permute-start.28 = (bf16[2,64,2560]{2,1,0:T(8,128)(2,1)S(1)}, bf16[2,64,2560]{2,1,0:T(8,128)(2,1)S(1)}, u32[]{:S(2)}, u32[]{:S(2)}) collective-permute-start(bf16[2,64,2560]{2,1,0:T(8,128)(2,1)S(1)} %get-tuple-element.136.rest_0_.state_ref.refs_13_), channel_id=1, source_target_pairs={{0,24},{4,12},{8,0},{12,20},{16,8},{20,28},{24,16},{28,4},{1,25},{... | collective-permute-start | bytes 1966088 | tf_op jit(solution)/shard_map/ppermute | solution.py:432
  204.3 21.4 %collective-permute-start.33 = (bf16[2,64,2560]{2,1,0:T(8,128)(2,1)S(1)}, bf16[2,64,2560]{2,1,0:T(8,128)(2,1)S(1)}, u32[]{:S(2)}, u32[]{:S(2)}) collective-permute-start(bf16[2,64,2560]{2,1,0:T(8,128)(2,1)S(1)} %get-tuple-element.140.rest_0_.state_ref.refs_13_), channel_id=1, source_target_pairs={{0,24},{4,12},{8,0},{12,20},{16,8},{20,28},{24,16},{28,4},{1,25},{... | collective-permute-start | bytes 1966088 | tf_op jit(solution)/shard_map/ppermute | solution.py:432
  218.4 21.4 %collective-permute-start.36 = (bf16[2,64,2560]{2,1,0:T(8,128)(2,1)S(1)}, bf16[2,64,2560]{2,1,0:T(8,128)(2,1)S(1)}, u32[]{:S(2)}, u32[]{:S(2)}) collective-permute-start(bf16[2,64,2560]{2,1,0:T(8,128)(2,1)S(1)} %get-tuple-element.146.rest_0_.state_ref.refs_13_), channel_id=1, source_target_pairs={{0,24},{4,12},{8,0},{12,20},{16,8},{20,28},{24,16},{28,4},{1,25},{... | collective-permute-start | bytes 1966088 | tf_op jit(solution)/shard_map/ppermute | solution.py:432
  232.4 21.4 %collective-permute-start.34 = (bf16[2,64,2560]{2,1,0:T(8,128)(2,1)S(1)}, bf16[2,64,2560]{2,1,0:T(8,128)(2,1)S(1)}, u32[]{:S(2)}, u32[]{:S(2)}) collective-permute-start(bf16[2,64,2560]{2,1,0:T(8,128)(2,1)S(1)} %get-tuple-element.148.rest_0_.state_ref.refs_13_), channel_id=1, source_target_pairs={{0,24},{4,12},{8,0},{12,20},{16,8},{20,28},{24,16},{28,4},{1,25},{... | collective-permute-start | bytes 1966088 | tf_op jit(solution)/shard_map/ppermute | solution.py:432
  246.5 21.4 %collective-permute-start.39 = (bf16[2,64,2560]{2,1,0:T(8,128)(2,1)S(1)}, bf16[2,64,2560]{2,1,0:T(8,128)(2,1)S(1)}, u32[]{:S(2)}, u32[]{:S(2)}) collective-permute-start(bf16[2,64,2560]{2,1,0:T(8,128)(2,1)S(1)} %get-tuple-element.152.rest_0_.state_ref.refs_13_), channel_id=1, source_target_pairs={{0,24},{4,12},{8,0},{12,20},{16,8},{20,28},{24,16},{28,4},{1,25},{... | collective-permute-start | bytes 1966088 | tf_op jit(solution)/shard_map/ppermute | solution.py:432
  260.5 21.4 %collective-permute-start.42 = (bf16[2,64,2560]{2,1,0:T(8,128)(2,1)S(1)}, bf16[2,64,2560]{2,1,0:T(8,128)(2,1)S(1)}, u32[]{:S(2)}, u32[]{:S(2)}) collective-permute-start(bf16[2,64,2560]{2,1,0:T(8,128)(2,1)S(1)} %get-tuple-element.158.rest_0_.state_ref.refs_13_), channel_id=1, source_target_pairs={{0,24},{4,12},{8,0},{12,20},{16,8},{20,28},{24,16},{28,4},{1,25},{... | collective-permute-start | bytes 1966088 | tf_op jit(solution)/shard_map/ppermute | solution.py:432
  274.5 21.4 %collective-permute-start.40 = (bf16[2,64,2560]{2,1,0:T(8,128)(2,1)S(1)}, bf16[2,64,2560]{2,1,0:T(8,128)(2,1)S(1)}, u32[]{:S(2)}, u32[]{:S(2)}) collective-permute-start(bf16[2,64,2560]{2,1,0:T(8,128)(2,1)S(1)} %get-tuple-element.160.rest_0_.state_ref.refs_13_), channel_id=1, source_target_pairs={{0,24},{4,12},{8,0},{12,20},{16,8},{20,28},{24,16},{28,4},{1,25},{... | collective-permute-start | bytes 1966088 | tf_op jit(solution)/shard_map/ppermute | solution.py:432
  288.6 21.4 %collective-permute-start.45 = (bf16[2,64,2560]{2,1,0:T(8,128)(2,1)S(1)}, bf16[2,64,2560]{2,1,0:T(8,128)(2,1)S(1)}, u32[]{:S(2)}, u32[]{:S(2)}) collective-permute-start(bf16[2,64,2560]{2,1,0:T(8,128)(2,1)S(1)} %get-tuple-element.164.rest_0_.state_ref.refs_2_), channel_id=1, source_target_pairs={{0,24},{4,12},{8,0},{12,20},{16,8},{20,28},{24,16},{28,4},{1,25},{... | collective-permute-start | bytes 1966088 | tf_op jit(solution)/shard_map/ppermute | solution.py:432
  302.6 21.4 %collective-permute-start.47 = (bf16[2,64,2560]{2,1,0:T(8,128)(2,1)S(1)}, bf16[2,64,2560]{2,1,0:T(8,128)(2,1)S(1)}, u32[]{:S(2)}, u32[]{:S(2)}) collective-permute-start(bf16[2,64,2560]{2,1,0:T(8,128)(2,1)S(1)} %get-tuple-element.170.rest_0_.state_ref.refs_2_), channel_id=1, source_target_pairs={{0,24},{4,12},{8,0},{12,20},{16,8},{20,28},{24,16},{28,4},{1,25},{... | collective-permute-start | bytes 1966088 | tf_op jit(solution)/shard_map/ppermute | solution.py:432
  314.4 21.6 %collective-permute-start.46 = (bf16[2,64,2560]{2,1,0:T(8,128)(2,1)S(1)}, bf16[2,64,2560]{2,1,0:T(8,128)(2,1)S(1)}, u32[]{:S(2)}, u32[]{:S(2)}) collective-permute-start(bf16[2,64,2560]{2,1,0:T(8,128)(2,1)S(1)} %get-tuple-element.172.rest_0_.state_ref.refs_2_), channel_id=1, source_target_pairs={{0,24},{4,12},{8,0},{12,20},{16,8},{20,28},{24,16},{28,4},{1,25},{... | collective-permute-start | bytes 1966088 | tf_op jit(solution)/shard_map/ppermute | solution.py:432
  318.7 21.2 %collective-permute-start.50 = (bf16[2,64,2560]{2,1,0:T(8,128)(2,1)S(1)}, bf16[2,64,2560]{2,1,0:T(8,128)(2,1)S(1)}, u32[]{:S(2)}, u32[]{:S(2)}) collective-permute-start(bf16[2,64,2560]{2,1,0:T(8,128)(2,1)S(1)} %shard_map.145.refs_17_), channel_id=1, source_target_pairs={{0,4},{4,0},{8,12},{12,8},{16,20},{20,16},{24,28},{28,24},{1,5},{5... | collective-permute-start | bytes 1966088 | tf_op jit(solution)/shard_map/ppermute | solution.py:433
  325.2 25.3 %collective-permute-start.49 = (bf16[2,64,2560]{2,1,0:T(8,128)(2,1)S(1)}, bf16[2,64,2560]{2,1,0:T(8,128)(2,1)S(1)}, u32[]{:S(2)}, u32[]{:S(2)}) collective-permute-start(bf16[2,64,2560]{2,1,0:T(8,128)(2,1)S(1)} %shard_map.147.rest_0_.refs_6_), channel_id=1, source_target_pairs={{0,4},{4,0},{8,12},{12,8},{16,20},{20,16},{24,28},{28,24},{1,5},{5... | collective-permute-start | bytes 1966088 | tf_op jit(solution)/shard_map/ppermute | solution.py:433
  337.1 22.0 %collective-permute-start.48 = (bf16[2,64,2560]{2,1,0:T(8,128)(2,1)S(1)}, bf16[2,64,2560]{2,1,0:T(8,128)(2,1)S(1)}, u32[]{:S(2)}, u32[]{:S(2)}) collective-permute-start(bf16[2,64,2560]{2,1,0:T(8,128)(2,1)S(1)} %shard_map.148.refs_6_), channel_id=1, source_target_pairs={{0,4},{4,0},{8,12},{12,8},{16,20},{20,16},{24,28},{28,24},{1,5},{5... | collective-permute-start | bytes 1966088 | tf_op jit(solution)/shard_map/ppermute | solution.py:433
  (35 other events, 365.5 us)

commit v4 on v3

--- a/solution.py
+++ b/solution.py
@@ -11,13 +11,14 @@
 learn_rate = 0.5
 beta_decay = 0.9
 
-UNIT = 32
+UNIT = 64
 CHUNKS = ((64, 1),)
 Z_AHEAD = 2
 Y_AHEAD = 1
 MIB = 1024 * 1024
 FORWARD_ROWS = 256
-FORWARD_MIB = SECOND_MIB = STEP_MIB = PAIR_MIB = 24
+FORWARD_MIB = SECOND_MIB = 24
+STEP_MIB = PAIR_MIB = 44
 F32 = jnp.float32
 BF16 = jnp.bfloat16
 NT = (((1,), (1,)), ((), ()))

time: 362 us -> 357 us (0.986)
  waiting for transfers between devices: 140 us -> 122 us
  local copies, waits for them, and re-layouts: 13.6 us -> 24.2 us
  Pallas kernels: 104 us -> 113 us
  starting transfers between devices: 100 us -> 92.1 us
    ppermute x20, starting transfers between devices: 44.8 us -> 19 us  [local(): over_z = lambda value: lax.ppermute(value, 'rep', along_z)]
    ppermute x20, waiting for transfers between devices: 118 us -> 99.3 us  [local(): over_z = lambda value: lax.ppermute(value, 'rep', along_z)]
    ppermute x20, starting transfers between devices: 43.3 us -> 61.1 us  [local(): over_y = lambda value: lax.ppermute(value, 'rep', along_y)]
    pallas_call x23, Pallas kernels: 66 us -> 76.7 us  [step_call(): pl.pallas_call(functools.partial(step_kernel, count, features, bool(updat...]
    unnamed x17 -> x247, local copies, waits for them, and re-layouts: 12.1 us -> 22.7 us
  transfers between devices with their start and end apart: 51 -> 51, of which waited for: 28 -> 27; matrix products, arithmetic and copies ran while one was open for 1% -> 1% of each run, Pallas kernels for 24% -> 27%
where the time goes in v4:
time: 357 us; the launch traced here: 356 us
  waiting for transfers between devices  122 us (34%)
  Pallas kernels  113 us (32%)
  starting transfers between devices  92.1 us (26%)
  local copies, waits for them, and re-layouts  24.2 us (7%)
    ppermute x20, waiting for transfers between devices, local(): over_z = lambda value: lax.ppermute(value, 'rep', along_z)  99.3 us
    pallas_call x23, Pallas kernels, step_call(): pl.pallas_call(functools.partial(step_kernel, count, features, bool(updat...  76.7 us
    ppermute x20, starting transfers between devices, local(): over_y = lambda value: lax.ppermute(value, 'rep', along_y)  61.1 us
    unnamed x247, local copies, waits for them, and re-layouts  22.7 us
    pallas_call x20, Pallas kernels, pair_sum(): pl.pallas_call(pair_kernel, grid=(rows // UNIT,), in_specs=[SMEM_SPEC, pl...  21.1 us
    ppermute x20, starting transfers between devices, local(): over_z = lambda value: lax.ppermute(value, 'rep', along_z)  19 us
    ppermute x20, waiting for transfers between devices, local(): over_y = lambda value: lax.ppermute(value, 'rep', along_y)  15.9 us
    pallas_call x1, Pallas kernels, forward(): pl.pallas_call(functools.partial(forward_kernel, count), grid=(rows // bl...  10.8 us
  transfers between devices with their start and end apart: 51, of which 27 were waited for; matrix products, arithmetic and copies ran while one was open for 1% of the time, Pallas kernels for 27%

profile of v4, /device:TPU:0, one launch (start us, length us, event | category | flops | bytes accessed | tf_op | source)
XLA Modules:
  0.0 355.9 jit_solution(14858630575502330704)
XLA Ops:
  21.3 10.8 %shard_map.107 = (f32[1280,512]{1,0:T(8,128)S(1)}, f32[1280,512]{1,0:T(8,128)S(1)}, f32[8,512]{1,0:T(8,128)S(1)}, bf16[512,2560]{1,0:T(8,128)(2,1)S(1)}, f32[8,128]{1,0:T(8,128)S(1)}) custom-call(s32[24]{0:T(128)S(1)} %reshape.10.refs_2_.mix_ref.refs_0_, f32[1]{0:T(128)} %copy.112.push_ref, f32[8,128]{1,0:T(8,128)S(1)} %collective-permute-done.refs_4_.low_ref, ...), custom_call_target="tpu_custom_call" | custom-call | flops 6710886400 | bytes 19660800 | tf_op jit(solution)/shard_map/pallas_call | solution.py:181
  54.6 11.9 %collective-permute-done.12.other_ref = bf16[2,64,2560]{2,1,0:T(8,128)(2,1)S(1)} collective-permute-done((bf16[2,64,2560]{2,1,0:T(8,128)(2,1)S(1)}, bf16[2,64,2560]{2,1,0:T(8,128)(2,1)S(1)}, u32[]{:S(2)}, u32[]{:S(2)}) %collective-permute-start.12) | collective-permute-done | bytes 655392 | tf_op jit(solution)/shard_map/ppermute | solution.py:433
  74.6 5.9 %collective-permute-done.11.other_ref = bf16[2,64,2560]{2,1,0:T(8,128)(2,1)S(1)} collective-permute-done((bf16[2,64,2560]{2,1,0:T(8,128)(2,1)S(1)}, bf16[2,64,2560]{2,1,0:T(8,128)(2,1)S(1)}, u32[]{:S(2)}, u32[]{:S(2)}) %collective-permute-start.11) | collective-permute-done | bytes 655392 | tf_op jit(solution)/shard_map/ppermute | solution.py:433
  89.8 4.9 %collective-permute-done.15.other_ref = bf16[2,64,2560]{2,1,0:T(8,128)(2,1)S(1)} collective-permute-done((bf16[2,64,2560]{2,1,0:T(8,128)(2,1)S(1)}, bf16[2,64,2560]{2,1,0:T(8,128)(2,1)S(1)}, u32[]{:S(2)}, u32[]{:S(2)}) %collective-permute-start.15) | collective-permute-done | bytes 655392 | tf_op jit(solution)/shard_map/ppermute | solution.py:433
  138.5 3.9 %collective-permute-start.23 = (bf16[2,64,2560]{2,1,0:T(8,128)(2,1)S(1)}, bf16[2,64,2560]{2,1,0:T(8,128)(2,1)S(1)}, u32[]{:S(2)}, u32[]{:S(2)}) collective-permute-start(bf16[2,64,2560]{2,1,0:T(8,128)(2,1)S(1)} %shard_map.121.refs_17_), channel_id=1, source_target_pairs={{0,4},{4,0},{8,12},{12,8},{16,20},{20,16},{24,28},{28,24},{1,5},{5... | collective-permute-start | bytes 1966088 | tf_op jit(solution)/shard_map/ppermute | solution.py:434
  146.3 5.2 %collective-permute-done.24.other_ref = bf16[2,64,2560]{2,1,0:T(8,128)(2,1)S(1)} collective-permute-done((bf16[2,64,2560]{2,1,0:T(8,128)(2,1)S(1)}, bf16[2,64,2560]{2,1,0:T(8,128)(2,1)S(1)}, u32[]{:S(2)}, u32[]{:S(2)}) %collective-permute-start.24) | collective-permute-done | bytes 655392 | tf_op jit(solution)/shard_map/ppermute | solution.py:433
  160.4 5.2 %collective-permute-done.22.other_ref = bf16[2,64,2560]{2,1,0:T(8,128)(2,1)S(1)} collective-permute-done((bf16[2,64,2560]{2,1,0:T(8,128)(2,1)S(1)}, bf16[2,64,2560]{2,1,0:T(8,128)(2,1)S(1)}, u32[]{:S(2)}, u32[]{:S(2)}) %collective-permute-start.22) | collective-permute-done | bytes 655392 | tf_op jit(solution)/shard_map/ppermute | solution.py:433
  174.4 5.2 %collective-permute-done.27.other_ref = bf16[2,64,2560]{2,1,0:T(8,128)(2,1)S(1)} collective-permute-done((bf16[2,64,2560]{2,1,0:T(8,128)(2,1)S(1)}, bf16[2,64,2560]{2,1,0:T(8,128)(2,1)S(1)}, u32[]{:S(2)}, u32[]{:S(2)}) %collective-permute-start.27) | collective-permute-done | bytes 655392 | tf_op jit(solution)/shard_map/ppermute | solution.py:433
  188.5 5.2 %collective-permute-done.30.other_ref = bf16[2,64,2560]{2,1,0:T(8,128)(2,1)S(1)} collective-permute-done((bf16[2,64,2560]{2,1,0:T(8,128)(2,1)S(1)}, bf16[2,64,2560]{2,1,0:T(8,128)(2,1)S(1)}, u32[]{:S(2)}, u32[]{:S(2)}) %collective-permute-start.30) | collective-permute-done | bytes 655392 | tf_op jit(solution)/shard_map/ppermute | solution.py:433
  202.5 5.2 %collective-permute-done.28.other_ref = bf16[2,64,2560]{2,1,0:T(8,128)(2,1)S(1)} collective-permute-done((bf16[2,64,2560]{2,1,0:T(8,128)(2,1)S(1)}, bf16[2,64,2560]{2,1,0:T(8,128)(2,1)S(1)}, u32[]{:S(2)}, u32[]{:S(2)}) %collective-permute-start.28) | collective-permute-done | bytes 655392 | tf_op jit(solution)/shard_map/ppermute | solution.py:433
  216.5 5.2 %collective-permute-done.33.other_ref = bf16[2,64,2560]{2,1,0:T(8,128)(2,1)S(1)} collective-permute-done((bf16[2,64,2560]{2,1,0:T(8,128)(2,1)S(1)}, bf16[2,64,2560]{2,1,0:T(8,128)(2,1)S(1)}, u32[]{:S(2)}, u32[]{:S(2)}) %collective-permute-start.33) | collective-permute-done | bytes 655392 | tf_op jit(solution)/shard_map/ppermute | solution.py:433
  222.7 3.9 %collective-permute-start.35 = (bf16[2,64,2560]{2,1,0:T(8,128)(2,1)S(1)}, bf16[2,64,2560]{2,1,0:T(8,128)(2,1)S(1)}, u32[]{:S(2)}, u32[]{:S(2)}) collective-permute-start(bf16[2,64,2560]{2,1,0:T(8,128)(2,1)S(1)} %shard_map.133.refs_17_), channel_id=1, source_target_pairs={{0,4},{4,0},{8,12},{12,8},{16,20},{20,16},{24,28},{28,24},{1,5},{5... | collective-permute-start | bytes 1966088 | tf_op jit(solution)/shard_map/ppermute | solution.py:434
  230.6 5.2 %collective-permute-done.36.other_ref = bf16[2,64,2560]{2,1,0:T(8,128)(2,1)S(1)} collective-permute-done((bf16[2,64,2560]{2,1,0:T(8,128)(2,1)S(1)}, bf16[2,64,2560]{2,1,0:T(8,128)(2,1)S(1)}, u32[]{:S(2)}, u32[]{:S(2)}) %collective-permute-start.36) | collective-permute-done | bytes 655392 | tf_op jit(solution)/shard_map/ppermute | solution.py:433
  236.8 3.9 %collective-permute-start.38 = (bf16[2,64,2560]{2,1,0:T(8,128)(2,1)S(1)}, bf16[2,64,2560]{2,1,0:T(8,128)(2,1)S(1)}, u32[]{:S(2)}, u32[]{:S(2)}) collective-permute-start(bf16[2,64,2560]{2,1,0:T(8,128)(2,1)S(1)} %shard_map.135.refs_17_), channel_id=1, source_target_pairs={{0,4},{4,0},{8,12},{12,8},{16,20},{20,16},{24,28},{28,24},{1,5},{5... | collective-permute-start | bytes 1966088 | tf_op jit(solution)/shard_map/ppermute | solution.py:434
  244.6 5.2 %collective-permute-done.34.other_ref = bf16[2,64,2560]{2,1,0:T(8,128)(2,1)S(1)} collective-permute-done((bf16[2,64,2560]{2,1,0:T(8,128)(2,1)S(1)}, bf16[2,64,2560]{2,1,0:T(8,128)(2,1)S(1)}, u32[]{:S(2)}, u32[]{:S(2)}) %collective-permute-start.34) | collective-permute-done | bytes 655392 | tf_op jit(solution)/shard_map/ppermute | solution.py:433
  259.4 4.5 %collective-permute-done.39.other_ref = bf16[2,64,2560]{2,1,0:T(8,128)(2,1)S(1)} collective-permute-done((bf16[2,64,2560]{2,1,0:T(8,128)(2,1)S(1)}, bf16[2,64,2560]{2,1,0:T(8,128)(2,1)S(1)}, u32[]{:S(2)}, u32[]{:S(2)}) %collective-permute-start.39) | collective-permute-done | bytes 655392 | tf_op jit(solution)/shard_map/ppermute | solution.py:433
  264.9 3.9 %collective-permute-start.41 = (bf16[2,64,2560]{2,1,0:T(8,128)(2,1)S(1)}, bf16[2,64,2560]{2,1,0:T(8,128)(2,1)S(1)}, u32[]{:S(2)}, u32[]{:S(2)}) collective-permute-start(bf16[2,64,2560]{2,1,0:T(8,128)(2,1)S(1)} %shard_map.139.refs_17_), channel_id=1, source_target_pairs={{0,4},{4,0},{8,12},{12,8},{16,20},{20,16},{24,28},{28,24},{1,5},{5... | collective-permute-start | bytes 1966088 | tf_op jit(solution)/shard_map/ppermute | solution.py:434
  278.9 3.9 %collective-permute-start.44 = (bf16[2,64,2560]{2,1,0:T(8,128)(2,1)S(1)}, bf16[2,64,2560]{2,1,0:T(8,128)(2,1)S(1)}, u32[]{:S(2)}, u32[]{:S(2)}) collective-permute-start(bf16[2,64,2560]{2,1,0:T(8,128)(2,1)S(1)} %shard_map.141.refs_17_), channel_id=1, source_target_pairs={{0,4},{4,0},{8,12},{12,8},{16,20},{20,16},{24,28},{28,24},{1,5},{5... | collective-permute-start | bytes 1966088 | tf_op jit(solution)/shard_map/ppermute | solution.py:434
  286.8 5.5 %collective-permute-done.40.other_ref = bf16[2,64,2560]{2,1,0:T(8,128)(2,1)S(1)} collective-permute-done((bf16[2,64,2560]{2,1,0:T(8,128)(2,1)S(1)}, bf16[2,64,2560]{2,1,0:T(8,128)(2,1)S(1)}, u32[]{:S(2)}, u32[]{:S(2)}) %collective-permute-start.40) | collective-permute-done | bytes 655392 | tf_op jit(solution)/shard_map/ppermute | solution.py:433
  300.6 5.7 %collective-permute-done.45.other_ref = bf16[2,64,2560]{2,1,0:T(8,128)(2,1)S(1)} collective-permute-done((bf16[2,64,2560]{2,1,0:T(8,128)(2,1)S(1)}, bf16[2,64,2560]{2,1,0:T(8,128)(2,1)S(1)}, u32[]{:S(2)}, u32[]{:S(2)}) %collective-permute-start.45) | collective-permute-done | bytes 655392 | tf_op jit(solution)/shard_map/ppermute | solution.py:433
  314.5 5.8 %collective-permute-done.47.other_ref = bf16[2,64,2560]{2,1,0:T(8,128)(2,1)S(1)} collective-permute-done((bf16[2,64,2560]{2,1,0:T(8,128)(2,1)S(1)}, bf16[2,64,2560]{2,1,0:T(8,128)(2,1)S(1)}, u32[]{:S(2)}, u32[]{:S(2)}) %collective-permute-start.47) | collective-permute-done | bytes 655392 | tf_op jit(solution)/shard_map/ppermute | solution.py:433
  324.9 6.3 %collective-permute-done.46.other_ref = bf16[2,64,2560]{2,1,0:T(8,128)(2,1)S(1)} collective-permute-done((bf16[2,64,2560]{2,1,0:T(8,128)(2,1)S(1)}, bf16[2,64,2560]{2,1,0:T(8,128)(2,1)S(1)}, u32[]{:S(2)}, u32[]{:S(2)}) %collective-permute-start.46) | collective-permute-done | bytes 655392 | tf_op jit(solution)/shard_map/ppermute | solution.py:433
  336.8 9.4 %collective-permute-done.49.refs_3_ = bf16[2,64,2560]{2,1,0:T(8,128)(2,1)S(1)} collective-permute-done((bf16[2,64,2560]{2,1,0:T(8,128)(2,1)S(1)}, bf16[2,64,2560]{2,1,0:T(8,128)(2,1)S(1)}, u32[]{:S(2)}, u32[]{:S(2)}) %collective-permute-start.49) | collective-permute-done | bytes 655392 | tf_op jit(solution)/shard_map/ppermute | solution.py:434
  347.9 6.5 %collective-permute-done.48.refs_3_ = bf16[2,64,2560]{2,1,0:T(8,128)(2,1)S(1)} collective-permute-done((bf16[2,64,2560]{2,1,0:T(8,128)(2,1)S(1)}, bf16[2,64,2560]{2,1,0:T(8,128)(2,1)S(1)}, u32[]{:S(2)}, u32[]{:S(2)}) %collective-permute-start.48) | collective-permute-done | bytes 655392 | tf_op jit(solution)/shard_map/ppermute | solution.py:434
  (376 shorter events, 215.0 us)
Async XLA Ops:
  1.1 18.1 %collective-permute-start.2 = (bf16[128,2560]{1,0:T(8,128)(2,1)}, bf16[128,2560]{1,0:T(8,128)(2,1)S(1)}, u32[]{:S(2)}, u32[]{:S(2)}) collective-permute-start(bf16[128,2560]{1,0:T(8,128)(2,1)} %bitcast.60), channel_id=1, source_target_pairs={{0,2},{1,3},{2,0},{3,1},{4,6},{5,7},{6,4},{7,5},{8,10},{9,11},{10,... | collective-permute-start | bytes 1966088 | tf_op jit(solution)/shard_map/ppermute | solution.py:397
  47.6 19.0 %collective-permute-start.12 = (bf16[2,64,2560]{2,1,0:T(8,128)(2,1)S(1)}, bf16[2,64,2560]{2,1,0:T(8,128)(2,1)S(1)}, u32[]{:S(2)}, u32[]{:S(2)}) collective-permute-start(bf16[2,64,2560]{2,1,0:T(8,128)(2,1)S(1)} %get-tuple-element.102.refs_12_.state_ref.refs_13_), channel_id=1, source_target_pairs={{0,24},{4,12},{8,0},{12,20},{16,8},{20,28},{24,16},{28,4},{1,25},{... | collective-permute-start | bytes 1966088 | tf_op jit(solution)/shard_map/ppermute | solution.py:433
  54.1 26.5 %collective-permute-start.11 = (bf16[2,64,2560]{2,1,0:T(8,128)(2,1)S(1)}, bf16[2,64,2560]{2,1,0:T(8,128)(2,1)S(1)}, u32[]{:S(2)}, u32[]{:S(2)}) collective-permute-start(bf16[2,64,2560]{2,1,0:T(8,128)(2,1)S(1)} %get-tuple-element.104.rest_0_.state_ref.refs_13_), channel_id=1, source_target_pairs={{0,24},{4,12},{8,0},{12,20},{16,8},{20,28},{24,16},{28,4},{1,25},{... | collective-permute-start | bytes 1966088 | tf_op jit(solution)/shard_map/ppermute | solution.py:433
  72.5 22.1 %collective-permute-start.15 = (bf16[2,64,2560]{2,1,0:T(8,128)(2,1)S(1)}, bf16[2,64,2560]{2,1,0:T(8,128)(2,1)S(1)}, u32[]{:S(2)}, u32[]{:S(2)}) collective-permute-start(bf16[2,64,2560]{2,1,0:T(8,128)(2,1)S(1)} %get-tuple-element.106.rest_0_.state_ref.refs_13_), channel_id=1, source_target_pairs={{0,24},{4,12},{8,0},{12,20},{16,8},{20,28},{24,16},{28,4},{1,25},{... | collective-permute-start | bytes 1966088 | tf_op jit(solution)/shard_map/ppermute | solution.py:433
  87.6 22.3 %collective-permute-start.18 = (bf16[2,64,2560]{2,1,0:T(8,128)(2,1)S(1)}, bf16[2,64,2560]{2,1,0:T(8,128)(2,1)S(1)}, u32[]{:S(2)}, u32[]{:S(2)}) collective-permute-start(bf16[2,64,2560]{2,1,0:T(8,128)(2,1)S(1)} %get-tuple-element.110.rest_0_.state_ref.refs_13_), channel_id=1, source_target_pairs={{0,24},{4,12},{8,0},{12,20},{16,8},{20,28},{24,16},{28,4},{1,25},{... | collective-permute-start | bytes 1966088 | tf_op jit(solution)/shard_map/ppermute | solution.py:433
  124.1 18.3 %collective-permute-start.19 = (bf16[2,64,2560]{2,1,0:T(8,128)(2,1)}, bf16[2,64,2560]{2,1,0:T(8,128)(2,1)S(1)}, u32[]{:S(2)}, u32[]{:S(2)}) collective-permute-start(bf16[2,64,2560]{2,1,0:T(8,128)(2,1)} %shard_map.119.refs_17_), channel_id=1, source_target_pairs={{0,4},{4,0},{8,12},{12,8},{16,20},{20,16},{24,28},{28,24},{1,5},{5... | collective-permute-start | bytes 1966088 | tf_op jit(solution)/shard_map/ppermute | solution.py:434
  131.9 19.7 %collective-permute-start.24 = (bf16[2,64,2560]{2,1,0:T(8,128)(2,1)S(1)}, bf16[2,64,2560]{2,1,0:T(8,128)(2,1)S(1)}, u32[]{:S(2)}, u32[]{:S(2)}) collective-permute-start(bf16[2,64,2560]{2,1,0:T(8,128)(2,1)S(1)} %get-tuple-element.122.rest_0_.state_ref.refs_13_), channel_id=1, source_target_pairs={{0,24},{4,12},{8,0},{12,20},{16,8},{20,28},{24,16},{28,4},{1,25},{... | collective-permute-start | bytes 1966088 | tf_op jit(solution)/shard_map/ppermute | solution.py:433
  146.3 19.3 %collective-permute-start.22 = (bf16[2,64,2560]{2,1,0:T(8,128)(2,1)S(1)}, bf16[2,64,2560]{2,1,0:T(8,128)(2,1)S(1)}, u32[]{:S(2)}, u32[]{:S(2)}) collective-permute-start(bf16[2,64,2560]{2,1,0:T(8,128)(2,1)S(1)} %get-tuple-element.124.rest_0_.state_ref.refs_13_), channel_id=1, source_target_pairs={{0,24},{4,12},{8,0},{12,20},{16,8},{20,28},{24,16},{28,4},{1,25},{... | collective-permute-start | bytes 1966088 | tf_op jit(solution)/shard_map/ppermute | solution.py:433
  160.3 19.3 %collective-permute-start.27 = (bf16[2,64,2560]{2,1,0:T(8,128)(2,1)S(1)}, bf16[2,64,2560]{2,1,0:T(8,128)(2,1)S(1)}, u32[]{:S(2)}, u32[]{:S(2)}) collective-permute-start(bf16[2,64,2560]{2,1,0:T(8,128)(2,1)S(1)} %get-tuple-element.128.rest_0_.state_ref.refs_13_), channel_id=1, source_target_pairs={{0,24},{4,12},{8,0},{12,20},{16,8},{20,28},{24,16},{28,4},{1,25},{... | collective-permute-start | bytes 1966088 | tf_op jit(solution)/shard_map/ppermute | solution.py:433
  174.4 19.3 %collective-permute-start.30 = (bf16[2,64,2560]{2,1,0:T(8,128)(2,1)S(1)}, bf16[2,64,2560]{2,1,0:T(8,128)(2,1)S(1)}, u32[]{:S(2)}, u32[]{:S(2)}) collective-permute-start(bf16[2,64,2560]{2,1,0:T(8,128)(2,1)S(1)} %get-tuple-element.134.rest_0_.state_ref.refs_13_), channel_id=1, source_target_pairs={{0,24},{4,12},{8,0},{12,20},{16,8},{20,28},{24,16},{28,4},{1,25},{... | collective-permute-start | bytes 1966088 | tf_op jit(solution)/shard_map/ppermute | solution.py:433
  188.4 19.3 %collective-permute-start.28 = (bf16[2,64,2560]{2,1,0:T(8,128)(2,1)S(1)}, bf16[2,64,2560]{2,1,0:T(8,128)(2,1)S(1)}, u32[]{:S(2)}, u32[]{:S(2)}) collective-permute-start(bf16[2,64,2560]{2,1,0:T(8,128)(2,1)S(1)} %get-tuple-element.136.rest_0_.state_ref.refs_13_), channel_id=1, source_target_pairs={{0,24},{4,12},{8,0},{12,20},{16,8},{20,28},{24,16},{28,4},{1,25},{... | collective-permute-start | bytes 1966088 | tf_op jit(solution)/shard_map/ppermute | solution.py:433
  202.5 19.3 %collective-permute-start.33 = (bf16[2,64,2560]{2,1,0:T(8,128)(2,1)S(1)}, bf16[2,64,2560]{2,1,0:T(8,128)(2,1)S(1)}, u32[]{:S(2)}, u32[]{:S(2)}) collective-permute-start(bf16[2,64,2560]{2,1,0:T(8,128)(2,1)S(1)} %get-tuple-element.140.rest_0_.state_ref.refs_13_), channel_id=1, source_target_pairs={{0,24},{4,12},{8,0},{12,20},{16,8},{20,28},{24,16},{28,4},{1,25},{... | collective-permute-start | bytes 1966088 | tf_op jit(solution)/shard_map/ppermute | solution.py:433
  208.7 17.9 %collective-permute-start.31 = (bf16[2,64,2560]{2,1,0:T(8,128)(2,1)S(1)}, bf16[2,64,2560]{2,1,0:T(8,128)(2,1)S(1)}, u32[]{:S(2)}, u32[]{:S(2)}) collective-permute-start(bf16[2,64,2560]{2,1,0:T(8,128)(2,1)S(1)} %shard_map.131.refs_17_), channel_id=1, source_target_pairs={{0,4},{4,0},{8,12},{12,8},{16,20},{20,16},{24,28},{28,24},{1,5},{5... | collective-permute-start | bytes 1966088 | tf_op jit(solution)/shard_map/ppermute | solution.py:434
  216.5 19.3 %collective-permute-start.36 = (bf16[2,64,2560]{2,1,0:T(8,128)(2,1)S(1)}, bf16[2,64,2560]{2,1,0:T(8,128)(2,1)S(1)}, u32[]{:S(2)}, u32[]{:S(2)}) collective-permute-start(bf16[2,64,2560]{2,1,0:T(8,128)(2,1)S(1)} %get-tuple-element.146.rest_0_.state_ref.refs_13_), channel_id=1, source_target_pairs={{0,24},{4,12},{8,0},{12,20},{16,8},{20,28},{24,16},{28,4},{1,25},{... | collective-permute-start | bytes 1966088 | tf_op jit(solution)/shard_map/ppermute | solution.py:433
  230.5 19.3 %collective-permute-start.34 = (bf16[2,64,2560]{2,1,0:T(8,128)(2,1)S(1)}, bf16[2,64,2560]{2,1,0:T(8,128)(2,1)S(1)}, u32[]{:S(2)}, u32[]{:S(2)}) collective-permute-start(bf16[2,64,2560]{2,1,0:T(8,128)(2,1)S(1)} %get-tuple-element.148.rest_0_.state_ref.refs_13_), channel_id=1, source_target_pairs={{0,24},{4,12},{8,0},{12,20},{16,8},{20,28},{24,16},{28,4},{1,25},{... | collective-permute-start | bytes 1966088 | tf_op jit(solution)/shard_map/ppermute | solution.py:433
  236.8 18.7 %collective-permute-start.38 = (bf16[2,64,2560]{2,1,0:T(8,128)(2,1)S(1)}, bf16[2,64,2560]{2,1,0:T(8,128)(2,1)S(1)}, u32[]{:S(2)}, u32[]{:S(2)}) collective-permute-start(bf16[2,64,2560]{2,1,0:T(8,128)(2,1)S(1)} %shard_map.135.refs_17_), channel_id=1, source_target_pairs={{0,4},{4,0},{8,12},{12,8},{16,20},{20,16},{24,28},{28,24},{1,5},{5... | collective-permute-start | bytes 1966088 | tf_op jit(solution)/shard_map/ppermute | solution.py:434
  244.6 19.3 %collective-permute-start.39 = (bf16[2,64,2560]{2,1,0:T(8,128)(2,1)S(1)}, bf16[2,64,2560]{2,1,0:T(8,128)(2,1)S(1)}, u32[]{:S(2)}, u32[]{:S(2)}) collective-permute-start(bf16[2,64,2560]{2,1,0:T(8,128)(2,1)S(1)} %get-tuple-element.152.rest_0_.state_ref.refs_13_), channel_id=1, source_target_pairs={{0,24},{4,12},{8,0},{12,20},{16,8},{20,28},{24,16},{28,4},{1,25},{... | collective-permute-start | bytes 1966088 | tf_op jit(solution)/shard_map/ppermute | solution.py:433
  259.4 18.5 %collective-permute-start.42 = (bf16[2,64,2560]{2,1,0:T(8,128)(2,1)S(1)}, bf16[2,64,2560]{2,1,0:T(8,128)(2,1)S(1)}, u32[]{:S(2)}, u32[]{:S(2)}) collective-permute-start(bf16[2,64,2560]{2,1,0:T(8,128)(2,1)S(1)} %get-tuple-element.158.rest_0_.state_ref.refs_13_), channel_id=1, source_target_pairs={{0,24},{4,12},{8,0},{12,20},{16,8},{20,28},{24,16},{28,4},{1,25},{... | collective-permute-start | bytes 1966088 | tf_op jit(solution)/shard_map/ppermute | solution.py:433
  286.7 19.6 %collective-permute-start.45 = (bf16[2,64,2560]{2,1,0:T(8,128)(2,1)S(1)}, bf16[2,64,2560]{2,1,0:T(8,128)(2,1)S(1)}, u32[]{:S(2)}, u32[]{:S(2)}) collective-permute-start(bf16[2,64,2560]{2,1,0:T(8,128)(2,1)S(1)} %get-tuple-element.164.rest_0_.state_ref.refs_2_), channel_id=1, source_target_pairs={{0,24},{4,12},{8,0},{12,20},{16,8},{20,28},{24,16},{28,4},{1,25},{... | collective-permute-start | bytes 1966088 | tf_op jit(solution)/shard_map/ppermute | solution.py:433
  300.6 19.8 %collective-permute-start.47 = (bf16[2,64,2560]{2,1,0:T(8,128)(2,1)S(1)}, bf16[2,64,2560]{2,1,0:T(8,128)(2,1)S(1)}, u32[]{:S(2)}, u32[]{:S(2)}) collective-permute-start(bf16[2,64,2560]{2,1,0:T(8,128)(2,1)S(1)} %get-tuple-element.170.rest_0_.state_ref.refs_2_), channel_id=1, source_target_pairs={{0,24},{4,12},{8,0},{12,20},{16,8},{20,28},{24,16},{28,4},{1,25},{... | collective-permute-start | bytes 1966088 | tf_op jit(solution)/shard_map/ppermute | solution.py:433
  311.0 20.3 %collective-permute-start.46 = (bf16[2,64,2560]{2,1,0:T(8,128)(2,1)S(1)}, bf16[2,64,2560]{2,1,0:T(8,128)(2,1)S(1)}, u32[]{:S(2)}, u32[]{:S(2)}) collective-permute-start(bf16[2,64,2560]{2,1,0:T(8,128)(2,1)S(1)} %get-tuple-element.172.rest_0_.state_ref.refs_2_), channel_id=1, source_target_pairs={{0,24},{4,12},{8,0},{12,20},{16,8},{20,28},{24,16},{28,4},{1,25},{... | collective-permute-start | bytes 1966088 | tf_op jit(solution)/shard_map/ppermute | solution.py:433
  314.5 20.6 %collective-permute-start.50 = (bf16[2,64,2560]{2,1,0:T(8,128)(2,1)S(1)}, bf16[2,64,2560]{2,1,0:T(8,128)(2,1)S(1)}, u32[]{:S(2)}, u32[]{:S(2)}) collective-permute-start(bf16[2,64,2560]{2,1,0:T(8,128)(2,1)S(1)} %shard_map.145.refs_17_), channel_id=1, source_target_pairs={{0,4},{4,0},{8,12},{12,8},{16,20},{20,16},{24,28},{28,24},{1,5},{5... | collective-permute-start | bytes 1966088 | tf_op jit(solution)/shard_map/ppermute | solution.py:434
  321.3 24.9 %collective-permute-start.49 = (bf16[2,64,2560]{2,1,0:T(8,128)(2,1)S(1)}, bf16[2,64,2560]{2,1,0:T(8,128)(2,1)S(1)}, u32[]{:S(2)}, u32[]{:S(2)}) collective-permute-start(bf16[2,64,2560]{2,1,0:T(8,128)(2,1)S(1)} %shard_map.147.rest_0_.refs_6_), channel_id=1, source_target_pairs={{0,4},{4,0},{8,12},{12,8},{16,20},{20,16},{24,28},{28,24},{1,5},{5... | collective-permute-start | bytes 1966088 | tf_op jit(solution)/shard_map/ppermute | solution.py:434
  332.2 22.1 %collective-permute-start.48 = (bf16[2,64,2560]{2,1,0:T(8,128)(2,1)S(1)}, bf16[2,64,2560]{2,1,0:T(8,128)(2,1)S(1)}, u32[]{:S(2)}, u32[]{:S(2)}) collective-permute-start(bf16[2,64,2560]{2,1,0:T(8,128)(2,1)S(1)} %shard_map.148.refs_6_), channel_id=1, source_target_pairs={{0,4},{4,0},{8,12},{12,8},{16,20},{20,16},{24,28},{28,24},{1,5},{5... | collective-permute-start | bytes 1966088 | tf_op jit(solution)/shard_map/ppermute | solution.py:434
  (150 other events, 2000.3 us)

commit v5 on v4

--- a/solution.py
+++ b/solution.py
@@ -18,7 +18,7 @@
 MIB = 1024 * 1024
 FORWARD_ROWS = 256
 FORWARD_MIB = SECOND_MIB = 24
-STEP_MIB = PAIR_MIB = 44
+STEP_MIB = PAIR_MIB = 38
 F32 = jnp.float32
 BF16 = jnp.bfloat16
 NT = (((1,), (1,)), ((), ()))

time: 357 us -> 356 us (level)
  waiting for transfers between devices: 122 us -> 145 us
  Pallas kernels: 113 us -> 96.6 us
  local copies, waits for them, and re-layouts: 24.2 us -> 10.8 us
  starting transfers between devices: 92.1 us -> 99.6 us
    ppermute x20, starting transfers between devices: 19 us -> 44.3 us  [local(): over_z = lambda value: lax.ppermute(value, 'rep', along_z)]
    ppermute x20, waiting for transfers between devices: 99.3 us -> 123 us  [local(): over_z = lambda value: lax.ppermute(value, 'rep', along_z)]
    ppermute x20, starting transfers between devices: 61.1 us -> 43.3 us  [local(): over_y = lambda value: lax.ppermute(value, 'rep', along_y)]
    pallas_call x23, Pallas kernels: 76.7 us -> 61.6 us  [step_call(): pl.pallas_call(functools.partial(step_kernel, count, features, bool(updat...]
    unnamed x247 -> x109, local copies, waits for them, and re-layouts: 22.7 us -> 9.28 us
  transfers between devices with their start and end apart: 51 -> 51, of which waited for: 27 -> 28; matrix products, arithmetic and copies ran while one was open for 1% -> 1% of each run, Pallas kernels for 27% -> 22%
where the time goes in v5:
time: 356 us; the launch traced here: 355 us
  waiting for transfers between devices  145 us (41%)
  starting transfers between devices  99.6 us (28%)
  Pallas kernels  96.6 us (27%)
  local copies, waits for them, and re-layouts  10.8 us (3%)
    ppermute x20, waiting for transfers between devices, local(): over_z = lambda value: lax.ppermute(value, 'rep', along_z)  123 us
    pallas_call x23, Pallas kernels, step_call(): pl.pallas_call(functools.partial(step_kernel, count, features, bool(updat...  61.6 us
    ppermute x20, starting transfers between devices, local(): over_z = lambda value: lax.ppermute(value, 'rep', along_z)  44.3 us
    ppermute x20, starting transfers between devices, local(): over_y = lambda value: lax.ppermute(value, 'rep', along_y)  43.3 us
    pallas_call x20, Pallas kernels, pair_sum(): pl.pallas_call(pair_kernel, grid=(rows // UNIT,), in_specs=[SMEM_SPEC, pl...  19.4 us
    ppermute x20, waiting for transfers between devices, local(): over_y = lambda value: lax.ppermute(value, 'rep', along_y)  15.5 us
    pallas_call x1, Pallas kernels, forward(): pl.pallas_call(functools.partial(forward_kernel, count), grid=(rows // bl...  10.8 us
    unnamed x109, local copies, waits for them, and re-layouts  9.28 us
  transfers between devices with their start and end apart: 51, of which 28 were waited for; matrix products, arithmetic and copies ran while one was open for 1% of the time, Pallas kernels for 22%

profile of v5, /device:TPU:0, one launch (start us, length us, event | category | flops | bytes accessed | tf_op | source)
XLA Modules:
  0.0 355.4 jit_solution(8509366561770809631)
XLA Ops:
  21.3 10.8 %shard_map.107 = (f32[1280,512]{1,0:T(8,128)S(1)}, f32[1280,512]{1,0:T(8,128)S(1)}, f32[8,512]{1,0:T(8,128)S(1)}, bf16[512,2560]{1,0:T(8,128)(2,1)S(1)}, f32[8,128]{1,0:T(8,128)S(1)}) custom-call(s32[24]{0:T(128)S(1)} %reshape.10.refs_2_.mix_ref.refs_0_, f32[1]{0:T(128)} %copy.112.push_ref, f32[8,128]{1,0:T(8,128)S(1)} %collective-permute-done.refs_4_.low_ref, ...), custom_call_target="tpu_custom_call" | custom-call | flops 6710886400 | bytes 19660800 | tf_op jit(solution)/shard_map/pallas_call | solution.py:181
  53.6 12.8 %collective-permute-done.12.other_ref = bf16[2,64,2560]{2,1,0:T(8,128)(2,1)S(1)} collective-permute-done((bf16[2,64,2560]{2,1,0:T(8,128)(2,1)S(1)}, bf16[2,64,2560]{2,1,0:T(8,128)(2,1)S(1)}, u32[]{:S(2)}, u32[]{:S(2)}) %collective-permute-start.12) | collective-permute-done | bytes 655392 | tf_op jit(solution)/shard_map/ppermute | solution.py:433
  73.7 6.8 %collective-permute-done.11.other_ref = bf16[2,64,2560]{2,1,0:T(8,128)(2,1)S(1)} collective-permute-done((bf16[2,64,2560]{2,1,0:T(8,128)(2,1)S(1)}, bf16[2,64,2560]{2,1,0:T(8,128)(2,1)S(1)}, u32[]{:S(2)}, u32[]{:S(2)}) %collective-permute-start.11) | collective-permute-done | bytes 655392 | tf_op jit(solution)/shard_map/ppermute | solution.py:433
  90.5 4.0 %collective-permute-done.15.other_ref = bf16[2,64,2560]{2,1,0:T(8,128)(2,1)S(1)} collective-permute-done((bf16[2,64,2560]{2,1,0:T(8,128)(2,1)S(1)}, bf16[2,64,2560]{2,1,0:T(8,128)(2,1)S(1)}, u32[]{:S(2)}, u32[]{:S(2)}) %collective-permute-start.15) | collective-permute-done | bytes 655392 | tf_op jit(solution)/shard_map/ppermute | solution.py:433
  103.0 5.6 %collective-permute-done.18.other_ref = bf16[2,64,2560]{2,1,0:T(8,128)(2,1)S(1)} collective-permute-done((bf16[2,64,2560]{2,1,0:T(8,128)(2,1)S(1)}, bf16[2,64,2560]{2,1,0:T(8,128)(2,1)S(1)}, u32[]{:S(2)}, u32[]{:S(2)}) %collective-permute-start.18) | collective-permute-done | bytes 655392 | tf_op jit(solution)/shard_map/ppermute | solution.py:433
  117.0 5.6 %collective-permute-done.16.other_ref = bf16[2,64,2560]{2,1,0:T(8,128)(2,1)S(1)} collective-permute-done((bf16[2,64,2560]{2,1,0:T(8,128)(2,1)S(1)}, bf16[2,64,2560]{2,1,0:T(8,128)(2,1)S(1)}, u32[]{:S(2)}, u32[]{:S(2)}) %collective-permute-start.16) | collective-permute-done | bytes 655392 | tf_op jit(solution)/shard_map/ppermute | solution.py:433
  131.1 5.6 %collective-permute-done.21.other_ref = bf16[2,64,2560]{2,1,0:T(8,128)(2,1)S(1)} collective-permute-done((bf16[2,64,2560]{2,1,0:T(8,128)(2,1)S(1)}, bf16[2,64,2560]{2,1,0:T(8,128)(2,1)S(1)}, u32[]{:S(2)}, u32[]{:S(2)}) %collective-permute-start.21) | collective-permute-done | bytes 655392 | tf_op jit(solution)/shard_map/ppermute | solution.py:433
  145.1 5.6 %collective-permute-done.24.other_ref = bf16[2,64,2560]{2,1,0:T(8,128)(2,1)S(1)} collective-permute-done((bf16[2,64,2560]{2,1,0:T(8,128)(2,1)S(1)}, bf16[2,64,2560]{2,1,0:T(8,128)(2,1)S(1)}, u32[]{:S(2)}, u32[]{:S(2)}) %collective-permute-start.24) | collective-permute-done | bytes 655392 | tf_op jit(solution)/shard_map/ppermute | solution.py:433
  159.2 5.6 %collective-permute-done.22.other_ref = bf16[2,64,2560]{2,1,0:T(8,128)(2,1)S(1)} collective-permute-done((bf16[2,64,2560]{2,1,0:T(8,128)(2,1)S(1)}, bf16[2,64,2560]{2,1,0:T(8,128)(2,1)S(1)}, u32[]{:S(2)}, u32[]{:S(2)}) %collective-permute-start.22) | collective-permute-done | bytes 655392 | tf_op jit(solution)/shard_map/ppermute | solution.py:433
  173.2 5.6 %collective-permute-done.27.other_ref = bf16[2,64,2560]{2,1,0:T(8,128)(2,1)S(1)} collective-permute-done((bf16[2,64,2560]{2,1,0:T(8,128)(2,1)S(1)}, bf16[2,64,2560]{2,1,0:T(8,128)(2,1)S(1)}, u32[]{:S(2)}, u32[]{:S(2)}) %collective-permute-start.27) | collective-permute-done | bytes 655392 | tf_op jit(solution)/shard_map/ppermute | solution.py:433
  187.3 5.6 %collective-permute-done.30.other_ref = bf16[2,64,2560]{2,1,0:T(8,128)(2,1)S(1)} collective-permute-done((bf16[2,64,2560]{2,1,0:T(8,128)(2,1)S(1)}, bf16[2,64,2560]{2,1,0:T(8,128)(2,1)S(1)}, u32[]{:S(2)}, u32[]{:S(2)}) %collective-permute-start.30) | collective-permute-done | bytes 655392 | tf_op jit(solution)/shard_map/ppermute | solution.py:433
  201.3 5.6 %collective-permute-done.28.other_ref = bf16[2,64,2560]{2,1,0:T(8,128)(2,1)S(1)} collective-permute-done((bf16[2,64,2560]{2,1,0:T(8,128)(2,1)S(1)}, bf16[2,64,2560]{2,1,0:T(8,128)(2,1)S(1)}, u32[]{:S(2)}, u32[]{:S(2)}) %collective-permute-start.28) | collective-permute-done | bytes 655392 | tf_op jit(solution)/shard_map/ppermute | solution.py:433
  215.3 5.6 %collective-permute-done.33.other_ref = bf16[2,64,2560]{2,1,0:T(8,128)(2,1)S(1)} collective-permute-done((bf16[2,64,2560]{2,1,0:T(8,128)(2,1)S(1)}, bf16[2,64,2560]{2,1,0:T(8,128)(2,1)S(1)}, u32[]{:S(2)}, u32[]{:S(2)}) %collective-permute-start.33) | collective-permute-done | bytes 655392 | tf_op jit(solution)/shard_map/ppermute | solution.py:433
  229.4 5.6 %collective-permute-done.36.other_ref = bf16[2,64,2560]{2,1,0:T(8,128)(2,1)S(1)} collective-permute-done((bf16[2,64,2560]{2,1,0:T(8,128)(2,1)S(1)}, bf16[2,64,2560]{2,1,0:T(8,128)(2,1)S(1)}, u32[]{:S(2)}, u32[]{:S(2)}) %collective-permute-start.36) | collective-permute-done | bytes 655392 | tf_op jit(solution)/shard_map/ppermute | solution.py:433
  243.4 5.6 %collective-permute-done.34.other_ref = bf16[2,64,2560]{2,1,0:T(8,128)(2,1)S(1)} collective-permute-done((bf16[2,64,2560]{2,1,0:T(8,128)(2,1)S(1)}, bf16[2,64,2560]{2,1,0:T(8,128)(2,1)S(1)}, u32[]{:S(2)}, u32[]{:S(2)}) %collective-permute-start.34) | collective-permute-done | bytes 655392 | tf_op jit(solution)/shard_map/ppermute | solution.py:433
  257.5 5.6 %collective-permute-done.39.other_ref = bf16[2,64,2560]{2,1,0:T(8,128)(2,1)S(1)} collective-permute-done((bf16[2,64,2560]{2,1,0:T(8,128)(2,1)S(1)}, bf16[2,64,2560]{2,1,0:T(8,128)(2,1)S(1)}, u32[]{:S(2)}, u32[]{:S(2)}) %collective-permute-start.39) | collective-permute-done | bytes 655392 | tf_op jit(solution)/shard_map/ppermute | solution.py:433
  271.5 5.6 %collective-permute-done.42.other_ref = bf16[2,64,2560]{2,1,0:T(8,128)(2,1)S(1)} collective-permute-done((bf16[2,64,2560]{2,1,0:T(8,128)(2,1)S(1)}, bf16[2,64,2560]{2,1,0:T(8,128)(2,1)S(1)}, u32[]{:S(2)}, u32[]{:S(2)}) %collective-permute-start.42) | collective-permute-done | bytes 655392 | tf_op jit(solution)/shard_map/ppermute | solution.py:433
  285.6 5.6 %collective-permute-done.40.other_ref = bf16[2,64,2560]{2,1,0:T(8,128)(2,1)S(1)} collective-permute-done((bf16[2,64,2560]{2,1,0:T(8,128)(2,1)S(1)}, bf16[2,64,2560]{2,1,0:T(8,128)(2,1)S(1)}, u32[]{:S(2)}, u32[]{:S(2)}) %collective-permute-start.40) | collective-permute-done | bytes 655392 | tf_op jit(solution)/shard_map/ppermute | solution.py:433
  299.4 5.8 %collective-permute-done.45.other_ref = bf16[2,64,2560]{2,1,0:T(8,128)(2,1)S(1)} collective-permute-done((bf16[2,64,2560]{2,1,0:T(8,128)(2,1)S(1)}, bf16[2,64,2560]{2,1,0:T(8,128)(2,1)S(1)}, u32[]{:S(2)}, u32[]{:S(2)}) %collective-permute-start.45) | collective-permute-done | bytes 655392 | tf_op jit(solution)/shard_map/ppermute | solution.py:433
  309.1 4.3 %collective-permute-start.46 = (bf16[2,64,2560]{2,1,0:T(8,128)(2,1)S(1)}, bf16[2,64,2560]{2,1,0:T(8,128)(2,1)S(1)}, u32[]{:S(2)}, u32[]{:S(2)}) collective-permute-start(bf16[2,64,2560]{2,1,0:T(8,128)(2,1)S(1)} %get-tuple-element.172.rest_0_.state_ref.refs_2_), channel_id=1, source_target_pairs={{0,24},{4,12},{8,0},{12,20},{16,8},{20,28},{24,16},{28,4},{1,25},{... | collective-permute-start | bytes 1966088 | tf_op jit(solution)/shard_map/ppermute | solution.py:433
  313.4 5.9 %collective-permute-done.47.other_ref = bf16[2,64,2560]{2,1,0:T(8,128)(2,1)S(1)} collective-permute-done((bf16[2,64,2560]{2,1,0:T(8,128)(2,1)S(1)}, bf16[2,64,2560]{2,1,0:T(8,128)(2,1)S(1)}, u32[]{:S(2)}, u32[]{:S(2)}) %collective-permute-start.47) | collective-permute-done | bytes 655392 | tf_op jit(solution)/shard_map/ppermute | solution.py:433
  322.5 8.7 %collective-permute-done.46.other_ref = bf16[2,64,2560]{2,1,0:T(8,128)(2,1)S(1)} collective-permute-done((bf16[2,64,2560]{2,1,0:T(8,128)(2,1)S(1)}, bf16[2,64,2560]{2,1,0:T(8,128)(2,1)S(1)}, u32[]{:S(2)}, u32[]{:S(2)}) %collective-permute-start.46) | collective-permute-done | bytes 655392 | tf_op jit(solution)/shard_map/ppermute | solution.py:433
  336.6 8.4 %collective-permute-done.49.refs_3_ = bf16[2,64,2560]{2,1,0:T(8,128)(2,1)S(1)} collective-permute-done((bf16[2,64,2560]{2,1,0:T(8,128)(2,1)S(1)}, bf16[2,64,2560]{2,1,0:T(8,128)(2,1)S(1)}, u32[]{:S(2)}, u32[]{:S(2)}) %collective-permute-start.49) | collective-permute-done | bytes 655392 | tf_op jit(solution)/shard_map/ppermute | solution.py:434
  346.7 7.0 %collective-permute-done.48.refs_3_ = bf16[2,64,2560]{2,1,0:T(8,128)(2,1)S(1)} collective-permute-done((bf16[2,64,2560]{2,1,0:T(8,128)(2,1)S(1)}, bf16[2,64,2560]{2,1,0:T(8,128)(2,1)S(1)}, u32[]{:S(2)}, u32[]{:S(2)}) %collective-permute-start.48) | collective-permute-done | bytes 655392 | tf_op jit(solution)/shard_map/ppermute | solution.py:434
  (239 shorter events, 200.3 us)
Async XLA Ops:
  1.1 18.1 %collective-permute-start.2 = (bf16[128,2560]{1,0:T(8,128)(2,1)}, bf16[128,2560]{1,0:T(8,128)(2,1)S(1)}, u32[]{:S(2)}, u32[]{:S(2)}) collective-permute-start(bf16[128,2560]{1,0:T(8,128)(2,1)} %bitcast.62), channel_id=1, source_target_pairs={{0,2},{1,3},{2,0},{3,1},{4,6},{5,7},{6,4},{7,5},{8,10},{9,11},{10,... | collective-permute-start | bytes 1966088 | tf_op jit(solution)/shard_map/ppermute | solution.py:397
  47.5 19.0 %collective-permute-start.12 = (bf16[2,64,2560]{2,1,0:T(8,128)(2,1)S(1)}, bf16[2,64,2560]{2,1,0:T(8,128)(2,1)S(1)}, u32[]{:S(2)}, u32[]{:S(2)}) collective-permute-start(bf16[2,64,2560]{2,1,0:T(8,128)(2,1)S(1)} %get-tuple-element.102.refs_12_.state_ref.refs_13_), channel_id=1, source_target_pairs={{0,24},{4,12},{8,0},{12,20},{16,8},{20,28},{24,16},{28,4},{1,25},{... | collective-permute-start | bytes 1966088 | tf_op jit(solution)/shard_map/ppermute | solution.py:433
  53.1 27.4 %collective-permute-start.11 = (bf16[2,64,2560]{2,1,0:T(8,128)(2,1)S(1)}, bf16[2,64,2560]{2,1,0:T(8,128)(2,1)S(1)}, u32[]{:S(2)}, u32[]{:S(2)}) collective-permute-start(bf16[2,64,2560]{2,1,0:T(8,128)(2,1)S(1)} %get-tuple-element.104.rest_0_.state_ref.refs_13_), channel_id=1, source_target_pairs={{0,24},{4,12},{8,0},{12,20},{16,8},{20,28},{24,16},{28,4},{1,25},{... | collective-permute-start | bytes 1966088 | tf_op jit(solution)/shard_map/ppermute | solution.py:433
  71.6 23.0 %collective-permute-start.15 = (bf16[2,64,2560]{2,1,0:T(8,128)(2,1)S(1)}, bf16[2,64,2560]{2,1,0:T(8,128)(2,1)S(1)}, u32[]{:S(2)}, u32[]{:S(2)}) collective-permute-start(bf16[2,64,2560]{2,1,0:T(8,128)(2,1)S(1)} %get-tuple-element.106.rest_0_.state_ref.refs_13_), channel_id=1, source_target_pairs={{0,24},{4,12},{8,0},{12,20},{16,8},{20,28},{24,16},{28,4},{1,25},{... | collective-permute-start | bytes 1966088 | tf_op jit(solution)/shard_map/ppermute | solution.py:433
  88.4 20.1 %collective-permute-start.18 = (bf16[2,64,2560]{2,1,0:T(8,128)(2,1)S(1)}, bf16[2,64,2560]{2,1,0:T(8,128)(2,1)S(1)}, u32[]{:S(2)}, u32[]{:S(2)}) collective-permute-start(bf16[2,64,2560]{2,1,0:T(8,128)(2,1)S(1)} %get-tuple-element.110.rest_0_.state_ref.refs_13_), channel_id=1, source_target_pairs={{0,24},{4,12},{8,0},{12,20},{16,8},{20,28},{24,16},{28,4},{1,25},{... | collective-permute-start | bytes 1966088 | tf_op jit(solution)/shard_map/ppermute | solution.py:433
  100.9 21.7 %collective-permute-start.16 = (bf16[2,64,2560]{2,1,0:T(8,128)(2,1)S(1)}, bf16[2,64,2560]{2,1,0:T(8,128)(2,1)S(1)}, u32[]{:S(2)}, u32[]{:S(2)}) collective-permute-start(bf16[2,64,2560]{2,1,0:T(8,128)(2,1)S(1)} %get-tuple-element.112.rest_0_.state_ref.refs_13_), channel_id=1, source_target_pairs={{0,24},{4,12},{8,0},{12,20},{16,8},{20,28},{24,16},{28,4},{1,25},{... | collective-permute-start | bytes 1966088 | tf_op jit(solution)/shard_map/ppermute | solution.py:433
  114.9 21.7 %collective-permute-start.21 = (bf16[2,64,2560]{2,1,0:T(8,128)(2,1)S(1)}, bf16[2,64,2560]{2,1,0:T(8,128)(2,1)S(1)}, u32[]{:S(2)}, u32[]{:S(2)}) collective-permute-start(bf16[2,64,2560]{2,1,0:T(8,128)(2,1)S(1)} %get-tuple-element.116.rest_0_.state_ref.refs_13_), channel_id=1, source_target_pairs={{0,24},{4,12},{8,0},{12,20},{16,8},{20,28},{24,16},{28,4},{1,25},{... | collective-permute-start | bytes 1966088 | tf_op jit(solution)/shard_map/ppermute | solution.py:433
  129.0 21.8 %collective-permute-start.24 = (bf16[2,64,2560]{2,1,0:T(8,128)(2,1)S(1)}, bf16[2,64,2560]{2,1,0:T(8,128)(2,1)S(1)}, u32[]{:S(2)}, u32[]{:S(2)}) collective-permute-start(bf16[2,64,2560]{2,1,0:T(8,128)(2,1)S(1)} %get-tuple-element.122.rest_0_.state_ref.refs_13_), channel_id=1, source_target_pairs={{0,24},{4,12},{8,0},{12,20},{16,8},{20,28},{24,16},{28,4},{1,25},{... | collective-permute-start | bytes 1966088 | tf_op jit(solution)/shard_map/ppermute | solution.py:433
  143.0 21.8 %collective-permute-start.22 = (bf16[2,64,2560]{2,1,0:T(8,128)(2,1)S(1)}, bf16[2,64,2560]{2,1,0:T(8,128)(2,1)S(1)}, u32[]{:S(2)}, u32[]{:S(2)}) collective-permute-start(bf16[2,64,2560]{2,1,0:T(8,128)(2,1)S(1)} %get-tuple-element.124.rest_0_.state_ref.refs_13_), channel_id=1, source_target_pairs={{0,24},{4,12},{8,0},{12,20},{16,8},{20,28},{24,16},{28,4},{1,25},{... | collective-permute-start | bytes 1966088 | tf_op jit(solution)/shard_map/ppermute | solution.py:433
  157.1 21.7 %collective-permute-start.27 = (bf16[2,64,2560]{2,1,0:T(8,128)(2,1)S(1)}, bf16[2,64,2560]{2,1,0:T(8,128)(2,1)S(1)}, u32[]{:S(2)}, u32[]{:S(2)}) collective-permute-start(bf16[2,64,2560]{2,1,0:T(8,128)(2,1)S(1)} %get-tuple-element.128.rest_0_.state_ref.refs_13_), channel_id=1, source_target_pairs={{0,24},{4,12},{8,0},{12,20},{16,8},{20,28},{24,16},{28,4},{1,25},{... | collective-permute-start | bytes 1966088 | tf_op jit(solution)/shard_map/ppermute | solution.py:433
  171.1 21.8 %collective-permute-start.30 = (bf16[2,64,2560]{2,1,0:T(8,128)(2,1)S(1)}, bf16[2,64,2560]{2,1,0:T(8,128)(2,1)S(1)}, u32[]{:S(2)}, u32[]{:S(2)}) collective-permute-start(bf16[2,64,2560]{2,1,0:T(8,128)(2,1)S(1)} %get-tuple-element.134.rest_0_.state_ref.refs_13_), channel_id=1, source_target_pairs={{0,24},{4,12},{8,0},{12,20},{16,8},{20,28},{24,16},{28,4},{1,25},{... | collective-permute-start | bytes 1966088 | tf_op jit(solution)/shard_map/ppermute | solution.py:433
  185.1 21.8 %collective-permute-start.28 = (bf16[2,64,2560]{2,1,0:T(8,128)(2,1)S(1)}, bf16[2,64,2560]{2,1,0:T(8,128)(2,1)S(1)}, u32[]{:S(2)}, u32[]{:S(2)}) collective-permute-start(bf16[2,64,2560]{2,1,0:T(8,128)(2,1)S(1)} %get-tuple-element.136.rest_0_.state_ref.refs_13_), channel_id=1, source_target_pairs={{0,24},{4,12},{8,0},{12,20},{16,8},{20,28},{24,16},{28,4},{1,25},{... | collective-permute-start | bytes 1966088 | tf_op jit(solution)/shard_map/ppermute | solution.py:433
  199.2 21.8 %collective-permute-start.33 = (bf16[2,64,2560]{2,1,0:T(8,128)(2,1)S(1)}, bf16[2,64,2560]{2,1,0:T(8,128)(2,1)S(1)}, u32[]{:S(2)}, u32[]{:S(2)}) collective-permute-start(bf16[2,64,2560]{2,1,0:T(8,128)(2,1)S(1)} %get-tuple-element.140.rest_0_.state_ref.refs_13_), channel_id=1, source_target_pairs={{0,24},{4,12},{8,0},{12,20},{16,8},{20,28},{24,16},{28,4},{1,25},{... | collective-permute-start | bytes 1966088 | tf_op jit(solution)/shard_map/ppermute | solution.py:433
  213.2 21.7 %collective-permute-start.36 = (bf16[2,64,2560]{2,1,0:T(8,128)(2,1)S(1)}, bf16[2,64,2560]{2,1,0:T(8,128)(2,1)S(1)}, u32[]{:S(2)}, u32[]{:S(2)}) collective-permute-start(bf16[2,64,2560]{2,1,0:T(8,128)(2,1)S(1)} %get-tuple-element.146.rest_0_.state_ref.refs_13_), channel_id=1, source_target_pairs={{0,24},{4,12},{8,0},{12,20},{16,8},{20,28},{24,16},{28,4},{1,25},{... | collective-permute-start | bytes 1966088 | tf_op jit(solution)/shard_map/ppermute | solution.py:433
  227.3 21.8 %collective-permute-start.34 = (bf16[2,64,2560]{2,1,0:T(8,128)(2,1)S(1)}, bf16[2,64,2560]{2,1,0:T(8,128)(2,1)S(1)}, u32[]{:S(2)}, u32[]{:S(2)}) collective-permute-start(bf16[2,64,2560]{2,1,0:T(8,128)(2,1)S(1)} %get-tuple-element.148.rest_0_.state_ref.refs_13_), channel_id=1, source_target_pairs={{0,24},{4,12},{8,0},{12,20},{16,8},{20,28},{24,16},{28,4},{1,25},{... | collective-permute-start | bytes 1966088 | tf_op jit(solution)/shard_map/ppermute | solution.py:433
  241.3 21.8 %collective-permute-start.39 = (bf16[2,64,2560]{2,1,0:T(8,128)(2,1)S(1)}, bf16[2,64,2560]{2,1,0:T(8,128)(2,1)S(1)}, u32[]{:S(2)}, u32[]{:S(2)}) collective-permute-start(bf16[2,64,2560]{2,1,0:T(8,128)(2,1)S(1)} %get-tuple-element.152.rest_0_.state_ref.refs_13_), channel_id=1, source_target_pairs={{0,24},{4,12},{8,0},{12,20},{16,8},{20,28},{24,16},{28,4},{1,25},{... | collective-permute-start | bytes 1966088 | tf_op jit(solution)/shard_map/ppermute | solution.py:433
  255.4 21.8 %collective-permute-start.42 = (bf16[2,64,2560]{2,1,0:T(8,128)(2,1)S(1)}, bf16[2,64,2560]{2,1,0:T(8,128)(2,1)S(1)}, u32[]{:S(2)}, u32[]{:S(2)}) collective-permute-start(bf16[2,64,2560]{2,1,0:T(8,128)(2,1)S(1)} %get-tuple-element.158.rest_0_.state_ref.refs_13_), channel_id=1, source_target_pairs={{0,24},{4,12},{8,0},{12,20},{16,8},{20,28},{24,16},{28,4},{1,25},{... | collective-permute-start | bytes 1966088 | tf_op jit(solution)/shard_map/ppermute | solution.py:433
  269.4 21.8 %collective-permute-start.40 = (bf16[2,64,2560]{2,1,0:T(8,128)(2,1)S(1)}, bf16[2,64,2560]{2,1,0:T(8,128)(2,1)S(1)}, u32[]{:S(2)}, u32[]{:S(2)}) collective-permute-start(bf16[2,64,2560]{2,1,0:T(8,128)(2,1)S(1)} %get-tuple-element.160.rest_0_.state_ref.refs_13_), channel_id=1, source_target_pairs={{0,24},{4,12},{8,0},{12,20},{16,8},{20,28},{24,16},{28,4},{1,25},{... | collective-permute-start | bytes 1966088 | tf_op jit(solution)/shard_map/ppermute | solution.py:433
  283.4 21.8 %collective-permute-start.45 = (bf16[2,64,2560]{2,1,0:T(8,128)(2,1)S(1)}, bf16[2,64,2560]{2,1,0:T(8,128)(2,1)S(1)}, u32[]{:S(2)}, u32[]{:S(2)}) collective-permute-start(bf16[2,64,2560]{2,1,0:T(8,128)(2,1)S(1)} %get-tuple-element.164.rest_0_.state_ref.refs_2_), channel_id=1, source_target_pairs={{0,24},{4,12},{8,0},{12,20},{16,8},{20,28},{24,16},{28,4},{1,25},{... | collective-permute-start | bytes 1966088 | tf_op jit(solution)/shard_map/ppermute | solution.py:433
  297.3 21.9 %collective-permute-start.47 = (bf16[2,64,2560]{2,1,0:T(8,128)(2,1)S(1)}, bf16[2,64,2560]{2,1,0:T(8,128)(2,1)S(1)}, u32[]{:S(2)}, u32[]{:S(2)}) collective-permute-start(bf16[2,64,2560]{2,1,0:T(8,128)(2,1)S(1)} %get-tuple-element.170.rest_0_.state_ref.refs_2_), channel_id=1, source_target_pairs={{0,24},{4,12},{8,0},{12,20},{16,8},{20,28},{24,16},{28,4},{1,25},{... | collective-permute-start | bytes 1966088 | tf_op jit(solution)/shard_map/ppermute | solution.py:433
  309.1 22.1 %collective-permute-start.46 = (bf16[2,64,2560]{2,1,0:T(8,128)(2,1)S(1)}, bf16[2,64,2560]{2,1,0:T(8,128)(2,1)S(1)}, u32[]{:S(2)}, u32[]{:S(2)}) collective-permute-start(bf16[2,64,2560]{2,1,0:T(8,128)(2,1)S(1)} %get-tuple-element.172.rest_0_.state_ref.refs_2_), channel_id=1, source_target_pairs={{0,24},{4,12},{8,0},{12,20},{16,8},{20,28},{24,16},{28,4},{1,25},{... | collective-permute-start | bytes 1966088 | tf_op jit(solution)/shard_map/ppermute | solution.py:433
  313.4 21.6 %collective-permute-start.50 = (bf16[2,64,2560]{2,1,0:T(8,128)(2,1)S(1)}, bf16[2,64,2560]{2,1,0:T(8,128)(2,1)S(1)}, u32[]{:S(2)}, u32[]{:S(2)}) collective-permute-start(bf16[2,64,2560]{2,1,0:T(8,128)(2,1)S(1)} %shard_map.145.refs_17_), channel_id=1, source_target_pairs={{0,4},{4,0},{8,12},{12,8},{16,20},{20,16},{24,28},{28,24},{1,5},{5... | collective-permute-start | bytes 1966088 | tf_op jit(solution)/shard_map/ppermute | solution.py:434
  320.2 24.8 %collective-permute-start.49 = (bf16[2,64,2560]{2,1,0:T(8,128)(2,1)S(1)}, bf16[2,64,2560]{2,1,0:T(8,128)(2,1)S(1)}, u32[]{:S(2)}, u32[]{:S(2)}) collective-permute-start(bf16[2,64,2560]{2,1,0:T(8,128)(2,1)S(1)} %shard_map.147.rest_0_.refs_6_), channel_id=1, source_target_pairs={{0,4},{4,0},{8,12},{12,8},{16,20},{20,16},{24,28},{28,24},{1,5},{5... | collective-permute-start | bytes 1966088 | tf_op jit(solution)/shard_map/ppermute | solution.py:434
  332.2 21.6 %collective-permute-start.48 = (bf16[2,64,2560]{2,1,0:T(8,128)(2,1)S(1)}, bf16[2,64,2560]{2,1,0:T(8,128)(2,1)S(1)}, u32[]{:S(2)}, u32[]{:S(2)}) collective-permute-start(bf16[2,64,2560]{2,1,0:T(8,128)(2,1)S(1)} %shard_map.148.refs_6_), channel_id=1, source_target_pairs={{0,4},{4,0},{8,12},{12,8},{16,20},{20,16},{24,28},{28,24},{1,5},{5... | collective-permute-start | bytes 1966088 | tf_op jit(solution)/shard_map/ppermute | solution.py:434
  (81 other events, 1145.3 us)
